TPU v7x, 128 devices: a whole 4x4x4 slice. The times are simulated.
128 devices in a mesh: member: 8 (over z_hi, x), space: 16 (over z_lo, y, core).
Axes of the slice: x: 4, y: 4, z: 4 (z_hi: 2, z_lo: 2; z = z_hi * 2 + z_lo), core: 2. Of those that a mesh axis runs over, the one named last changes fastest.
Arguments:
- ens: bfloat16 [16, 36, 256, 1440], P('member', None, 'space'), may hold values from -6 to 6
- truth: bfloat16 [36, 256, 1440], P(None, 'space'), may hold values from -6 to 6
- legendre: bfloat16 [256, 128, 721], P('space'), may hold values from -0.375 to 0.375
- orders: int32 [128], replicated, may hold values from 0 to 720, as said below
Outputs:
- grid_score: float32 [36, 16, 16], P(None, 'space', 'member')
- grid_grad: bfloat16 [16, 36, 16, 16, 1440], P(None, None, 'space', 'member')
- spec_score: float32 [128, 36, 721], P('space')
- spec_grad: bfloat16 [16, 36, 256, 1440], P('member', None, 'space')
Inputs may be any that keep to these rules, and one draw needn't show every extreme that they name: The 128 listed orders are distinct; 0 and 720 are always among them.
All inputs are finite; a program needn't handle non-finite values.
Results may differ from a plain program's by a relative error of at most 0.024.
Values may be sent and summed in bfloat16 or wider, within the bound.
No kernel may reach another device: no remote copies, remote signals or barrier semaphores. Data moves between devices by JAX's collectives and lax.ppermute only.
A program may use at most 192 MiB of HBM per device.

v0:
```python
import math

import jax
import jax.numpy as jnp
from jax import lax
from jax.sharding import PartitionSpec as P

FAIR_GAP = 0.05
SOFTEN = 0.1


def fourier_table(orders, lon_count):
    longitude = jnp.arange(lon_count, dtype=jnp.int32)
    phase_index = longitude[:, None] * orders[None, :] % lon_count
    angles = phase_index.astype(jnp.float32) * (2.0 * math.pi / lon_count)
    norm_scale = 1.0 / math.sqrt(lon_count)
    return jnp.stack([jnp.cos(angles) * norm_scale, -jnp.sin(angles) * norm_scale], axis=1).astype(
        jnp.bfloat16
    )


def latitude_weights(lat_count):
    row_index = jnp.arange(lat_count, dtype=jnp.float32)
    sine_values = jnp.sin((row_index + 0.5) * (math.pi / lat_count))
    return sine_values * (lat_count / jnp.sum(sine_values))


def grid_block(members, target, weights, fairness):
    values = members.astype(jnp.float32)
    ens_count = values.shape[0]
    differences = values[:, None] - values[None]
    spread = jnp.sum(jnp.abs(differences), axis=(0, 1))
    sign_sums = jnp.sum(jnp.sign(differences), axis=1)
    errors = values - target.astype(jnp.float32)[None]
    cell_scores = (
        jnp.mean(jnp.abs(errors), axis=0) - fairness / (2.0 * ens_count * (ens_count - 1)) * spread
    )
    gradient = weights[None, None, :, None] * (
        jnp.sign(errors) - fairness / (ens_count - 1) * sign_sums
    )
    return (jnp.mean(cell_scores, axis=-1), gradient.astype(jnp.bfloat16))


def spectral_block(members, target, order_weight, fairness, first_member, own_count):
    values = members.astype(jnp.float32)
    ens_count = values.shape[2]
    own_values = lax.dynamic_slice_in_dim(values, first_member, own_count, 2)
    differences = own_values[:, :, :, None, :] - values[:, :, None, :, :]
    magnitude = jnp.sqrt(differences[:, 0] ** 2 + differences[:, 1] ** 2 + SOFTEN * SOFTEN)
    spread = jnp.sum(magnitude - SOFTEN, axis=(1, 2))
    pulls = jnp.sum(differences / magnitude[:, None], axis=3)
    errors = own_values - target.astype(jnp.float32)[:, :, None]
    error_size = jnp.sqrt(errors[:, 0] ** 2 + errors[:, 1] ** 2 + SOFTEN * SOFTEN)
    scores = (
        jnp.sum(error_size - SOFTEN, axis=1) / ens_count
        - fairness / (2.0 * ens_count * (ens_count - 1)) * spread
    )
    gradient = order_weight * (errors / error_size[:, None] - fairness / (ens_count - 1) * pulls)
    return (scores.T, gradient)


def local(ens, truth, legendre, orders):
    own_count, var_count, band_rows, lon_count = ens.shape
    order_count = orders.shape[0]
    degree_count = legendre.shape[2]
    space_count = lax.axis_size("space")
    member_count = lax.axis_size("member")
    space_index = lax.axis_index("space")
    member_index = lax.axis_index("member")
    lat_count = band_rows * space_count
    ens_count = own_count * member_count
    owned_orders = order_count // space_count
    sub_rows = band_rows // member_count
    fairness = 1.0 - FAIR_GAP / ens_count
    transform = fourier_table(orders, lon_count)
    gathered = lax.all_gather(ens, "member", axis=0, tiled=True)
    rows_members = lax.dynamic_slice_in_dim(gathered, member_index * sub_rows, sub_rows, 2)
    rows_truth = lax.dynamic_slice_in_dim(truth, member_index * sub_rows, sub_rows, 1)
    row_weights = lax.dynamic_slice_in_dim(
        latitude_weights(lat_count), space_index * band_rows + member_index * sub_rows, sub_rows, 0
    )
    group_size = 4

    def grid_step(group_index, carried):
        scores_so_far, grads_so_far = carried
        block_members = lax.dynamic_slice_in_dim(
            rows_members, group_index * group_size, group_size, 1
        )
        block_truth = lax.dynamic_slice_in_dim(rows_truth, group_index * group_size, group_size, 0)
        block_scores, block_grads = grid_block(block_members, block_truth, row_weights, fairness)
        return (
            lax.dynamic_update_slice_in_dim(
                scores_so_far, block_scores, group_index * group_size, 0
            ),
            lax.dynamic_update_slice_in_dim(grads_so_far, block_grads, group_index * group_size, 1),
        )

    grid_initial = (
        jnp.zeros((var_count, sub_rows), jnp.float32),
        jnp.zeros((ens_count, var_count, sub_rows, lon_count), jnp.bfloat16),
    )
    grid_rows, grid_grads = lax.fori_loop(0, var_count // group_size, grid_step, grid_initial)
    grid_score = grid_rows.reshape(var_count, 1, sub_rows)
    grid_grad = grid_grads.reshape(ens_count, var_count, 1, sub_rows, lon_count)
    fields = jnp.concatenate([ens, truth[None]], axis=0)
    fourier = jnp.einsum(
        "evtn,nck->tkcev", fields, transform, preferred_element_type=jnp.float32
    ).astype(jnp.bfloat16)
    fourier = fourier.reshape(band_rows, order_count, -1)
    columns, fourier_rows = (
        lax.all_to_all(legendre, "space", split_axis=1, concat_axis=0, tiled=True),
        lax.all_to_all(fourier, "space", split_axis=1, concat_axis=0, tiled=True),
    )

    def add_band(band_index, running):
        weights = lax.dynamic_slice_in_dim(columns, band_index * band_rows, band_rows, 0)
        values = lax.dynamic_slice_in_dim(fourier_rows, band_index * band_rows, band_rows, 0)
        band_part = jnp.einsum(
            "tkl,tkx->klx", weights, values, preferred_element_type=jnp.float32
        ).astype(jnp.bfloat16)
        return running + lax.optimization_barrier(band_part).astype(jnp.float32)

    summed = lax.fori_loop(
        0,
        space_count,
        add_band,
        jnp.zeros((owned_orders, degree_count, fourier.shape[2]), jnp.float32),
    )
    spectra = summed.astype(jnp.bfloat16).reshape(
        owned_orders, degree_count, 2, own_count + 1, var_count
    )
    ensemble = lax.all_gather(spectra[:, :, :, :own_count], "member", axis=3, tiled=True)
    target = spectra[:, :, :, own_count]
    order_list = lax.dynamic_slice_in_dim(orders, space_index * owned_orders, owned_orders, 0)
    order_weight = jnp.where(order_list == 0, 1.0, 2.0).astype(jnp.float32)

    def one_order(pieces):
        members, goal, factor = pieces
        order_scores, gradient = spectral_block(
            members, goal, factor, fairness, member_index * own_count, own_count
        )
        return (order_scores, gradient.astype(jnp.bfloat16))

    score_share, pull_own = lax.map(one_order, (ensemble, target, order_weight))
    spec_score = lax.psum(score_share.astype(jnp.bfloat16), "member").astype(jnp.float32)
    pull_own = pull_own.reshape(owned_orders, degree_count, -1)
    at_owners = jnp.einsum(
        "tkl,klx->tkx", columns, pull_own, preferred_element_type=jnp.float32
    ).astype(jnp.bfloat16)
    fourier_grad = lax.all_to_all(at_owners, "space", split_axis=0, concat_axis=1, tiled=True)
    fourier_grad = fourier_grad.reshape(band_rows, order_count, 2, own_count, var_count)
    spec_grad = jnp.einsum(
        "tkcev,nck->evtn", fourier_grad, transform, preferred_element_type=jnp.float32
    ).astype(jnp.bfloat16)
    return (grid_score, grid_grad, spec_score, spec_grad)


def solution(mesh):
    in_specs = (
        P("member", None, "space", None),
        P(None, "space", None),
        P("space", None, None),
        P(),
    )
    out_specs = (
        P(None, "space", "member"),
        P(None, None, "space", "member", None),
        P("space", None, None),
        P("member", None, "space", None),
    )
    return jax.shard_map(local, mesh=mesh, in_specs=in_specs, out_specs=out_specs, check_vma=False)
```

profile of v0, /device:TPU:0, one launch (start us, length us, event | category | flops | bytes accessed | tf_op | source)
XLA Modules:
  0.0 1015.3 jit_solution(6375524555121860961)
XLA Ops:
  7.2 4.0 multiply_convert_fusion.3
  11.2 4.1 copy.139
  20.2 6.0 all-to-all-start.1
  26.2 5.4 copy.135
  31.6 11.1 %all-to-all-done.1 = bf16[16,128,216]{2,0,1:T(8,128)(2,1)S(1)} async-done(((bf16[16,128,216]{2,0,1:T(8,128)(2,1)}), bf16[16,128,216]{2,0,1:T(8,128)(2,1)S(1)}, u32[]{:S(2)}, u32[]{:S(2)}) %all-to-all-start.1) | async-done | bytes 884768 | tf_op jit(solution)/shard_map/all_to_all | solution.py:112
  43.6 3.7 all-to-all-start
  48.0 2.7 copy.143
  50.6 39.0 %all-to-all-done = bf16[16,128,721]{2,0,1:T(8,128)(2,1)S(1)} async-done(((bf16[16,128,721]{2,0,1:T(8,128)(2,1)}), bf16[16,128,721]{2,0,1:T(8,128)(2,1)S(1)}, u32[]{:S(2)}, u32[]{:S(2)}) %all-to-all-start) | async-done | bytes 2953248 | tf_op jit(solution)/shard_map/all_to_all | solution.py:111
  89.7 2.9 copy.137
  92.5 126.6 %while.46 = (s32[]{:T(128)}, f32[8,721,216]{1,2,0:T(8,128)}, bf16[256,8,721]{2,1,0:T(8,128)(2,1)}, bf16[256,8,216]{2,1,0:T(8,128)(2,1)}, s32[]{:T(128)}, /*index=5*/s32[]{:T(128)}, s32[]{:T(128)}, s32[]{:T(128)}) while((s32[]{:T(128)}, f32[8,721,216]{1,2,0:T(8,128)}, bf16[256,8,721]{2,1,0:T(8,128)(2,1)}, ...), condition=%wide.region_8.9_spmd.clone, body=%wide.region_7.8_spmd.clone.sunk | while | flops 44851972 | bytes 15670421 | solution.py:123
  95.2 2.9 select_add_fusion.2
  100.8 5.4 select_add_fusion.2
  108.9 5.4 select_add_fusion.2
  117.0 5.4 select_add_fusion.2
  125.0 5.4 select_add_fusion.2
  133.1 5.4 select_add_fusion.2
  141.2 5.4 select_add_fusion.2
  149.2 5.4 select_add_fusion.2
  157.3 5.4 select_add_fusion.2
  165.4 5.4 select_add_fusion.2
  173.4 5.4 select_add_fusion.2
  181.5 5.4 select_add_fusion.2
  189.6 5.4 select_add_fusion.2
  197.7 5.4 select_add_fusion.2
  205.7 5.4 select_add_fusion.2
  213.8 5.4 select_add_fusion.2
  219.2 4.0 copy.189
  225.1 162.6 %all-gather.5.cloned.1.call-done = bf16[8,721,2,16,36]{1,0,4,3,2:T(8,128)(2,1)} async-done(((bf16[8,721,2,2,36]{1,0,4,3,2:T(8,128)(2,1)}), bf16[8,721,2,16,36]{1,0,4,3,2:T(8,128)(2,1)}) %all-gather.5.cloned.1.call-update) | async-done | bytes 13289488 | tf_op jit(solution)/shard_map/all_gather | solution.py:132
  387.7 12.1 %copy.147 = bf16[8,721,2,16,36]{1,4,3,2,0:T(8,128)(2,1)} copy(bf16[8,721,2,16,36]{1,0,4,3,2:T(8,128)(2,1)} %all-gather.5.cloned.1.call-done) | data formatting | bytes 26578944 | tf_op jit(solution)/shard_map/while | solution.py:144
  399.8 111.4 %while.45 = (s32[]{:T(128)}, bf16[8,36,721]{2,0,1:T(8,128)(2,1)S(1)}, bf16[8,721,2,2,36]{1,4,3,2,0:T(8,128)(2,1)}, bf16[8,721,2,16,36]{1,4,3,2,0:T(8,128)(2,1)},...) while((s32[]{:T(128)}, ...), condition=%wide.region_13.14_spmd, body=%wide.region_9.13_spmd.sunk | while | flops 13393298 | bytes 47123440 | solution.py:144
  406.4 2.6 divide_reduce_fusion.2
  411.3 2.4 dynamic_update_slice.39
  420.4 2.6 divide_reduce_fusion.2
  425.2 2.4 dynamic_update_slice.39
  434.3 2.6 divide_reduce_fusion.2
  439.1 2.4 dynamic_update_slice.39
  448.2 2.6 divide_reduce_fusion.2
  453.1 2.4 dynamic_update_slice.39
  462.1 2.6 divide_reduce_fusion.2
  467.0 2.4 dynamic_update_slice.39
  476.1 2.6 divide_reduce_fusion.2
  480.9 2.4 dynamic_update_slice.39
  490.0 2.6 divide_reduce_fusion.2
  503.9 2.6 divide_reduce_fusion.2
  508.7 2.4 dynamic_update_slice.39
  512.7 2.7 copy.150
  517.4 2.6 copy.153
  520.0 4.7 all-to-all-start.2
  528.3 68.9 %all-reduce.2.cloned.1.call-done = bf16[8,36,721]{2,0,1:T(8,128)(2,1)} async-done(((bf16[8,36,721]{2,0,1:T(8,128)(2,1)}), bf16[8,36,721]{2,0,1:T(8,128)(2,1)}) %all-reduce.2.cloned.1.call-update) | async-done | bytes 415312 | tf_op jit(solution)/shard_map/psum | solution.py:145
  600.3 2.4 fusion.17
  602.7 3.7 copy.156
  606.4 283.2 %all-gather.3.cloned.1.call-done = bf16[16,36,16,1440]{3,2,1,0:T(8,128)(2,1)} async-done(((bf16[2,36,16,1440]{3,2,1,0:T(8,128)(2,1)}), bf16[16,36,16,1440]{3,2,1,0:T(8,128)(2,1)}) %all-gather.3.cloned.1.call-update) | async-done | bytes 26542096 | tf_op jit(solution)/shard_map/all_gather | solution.py:76
  889.7 8.0 constant_dynamic-slice_fusion.3
  897.6 3.6 broadcast_in_dim.62
  901.3 106.7 %while.44 = (s32[]{:T(128)}, f32[36,2]{0,1:T(2,128)S(1)}, bf16[16,36,2,1440]{3,2,1,0:T(2,128)(2,1)}, bf16[16,36,2,1440]{3,2,1,0:T(2,128)(2,1)S(1)}, bf16[36,2,14...) while((s32[]{:T(128)}, f32[36,2]{0,1:T(2,128)S(1)}, ...), condition=%wide.region_6.7_spmd, body=%wide.region_1.6_spmd.sunk | while | flops 16807684 | bytes 7006095 | solution.py:102
  902.4 7.1 fusion.51
  914.1 7.1 fusion.51
  926.0 7.1 fusion.51
  937.8 7.1 fusion.51
  949.6 7.1 fusion.51
  961.5 7.1 fusion.51
  973.3 7.1 fusion.51
  985.1 7.1 fusion.51
  997.0 7.1 fusion.51
  (259 shorter events, 176.4 us)
Async XLA Ops:
  11.2 5.1 copy-start.4
  11.2 4.1 copy-start.2
  20.2 22.5 %all-to-all-start.1 = ((bf16[16,128,216]{2,0,1:T(8,128)(2,1)}), bf16[16,128,216]{2,0,1:T(8,128)(2,1)S(1)}, u32[]{:S(2)}, u32[]{:S(2)}) async-start(bf16[16,128,216]{2,0,1:T(8,128)(2,1)} %copy.141), calls=%async_computation.1 | async-start | bytes 2097152 | tf_op jit(solution)/shard_map/all_to_all | solution.py:112
  42.7 1.0 copy-start.1
  43.6 46.0 %all-to-all-start = ((bf16[16,128,721]{2,0,1:T(8,128)(2,1)}), bf16[16,128,721]{2,0,1:T(8,128)(2,1)S(1)}, u32[]{:S(2)}, u32[]{:S(2)}) async-start(bf16[16,128,721]{2,0,1:T(8,128)(2,1)} %copy.135), calls=%async_computation | async-start | bytes 6291456 | tf_op jit(solution)/shard_map/all_to_all | solution.py:111
  47.4 340.3 %all-gather.5.cloned.1.call-start = ((), (), s32[]{:S(2)}) async-start(), calls=%async_computation.4 | async-start | bytes 15925248 | tf_op jit(solution)/shard_map/all_gather | solution.py:132
  223.1 1.7 copy-start.5
  224.5 372.6 %all-reduce.2.cloned.1.call-start = ((), (), s32[]{:S(2)}) async-start(), calls=%async_computation.5 | async-start | bytes 884736 | tf_op jit(solution)/shard_map/psum | solution.py:145
  511.2 0.8 copy-start.3
  511.9 3.5 copy-start
  512.0 377.7 %all-gather.3.cloned.1.call-start = ((), (), s32[]{:S(2)}) async-start(), calls=%async_computation.3 | async-start | bytes 31850496 | tf_op jit(solution)/shard_map/all_gather | solution.py:76
  520.0 79.1 %all-to-all-start.2 = ((bf16[256,8,144]{2,1,0:T(8,128)(2,1)}), bf16[256,8,144]{2,1,0:T(8,128)(2,1)S(1)}, u32[]{:S(2)}, u32[]{:S(2)}) async-start(bf16[256,8,144]{2,1,0:T(8,128)(2,1)} %copy.153), calls=%async_computation.2 | async-start | bytes 2097152 | tf_op jit(solution)/shard_map/all_to_all | solution.py:150
  1007.9 0.6 copy-start.6
Sparse Core Ops, SparseCore 0:
  224.7 162.9 all-gather.4
  512.1 85.0 all-reduce.1
  599.8 289.8 all-gather.2
where the time goes:
time: 1020 us
  waiting for transfers between devices  565 us (55%)
  other arithmetic  268 us (26%)
  local copies, waits for them, and re-layouts  130 us (13%)
  matrix products  20.5 us (2%)
  starting transfers between devices  15.3 us (2%)
  between operations  14.9 us (1%)
    all_gather x1, waiting for transfers between devices, local(): gathered = lax.all_gather(ens, 'member', axis=0, tiled=True)  283 us
    all_gather x1, waiting for transfers between devices, local(): lax.all_gather(spectra[:, :, :, :own_count], 'member', axis=3, tiled=True)  163 us
    add x16, other arithmetic, add_band(): return running + lax.optimization_barrier(band_part).astype(jnp.float32)  83.5 us
    psum x1, waiting for transfers between devices, local(): lax.psum(score_share.astype(jnp.bfloat16), 'member').astype(jnp.float32)  68.9 us
    reduce_sum x9, other arithmetic, grid_block(): sign_sums = jnp.sum(jnp.sign(differences), axis=1)  64.2 us
    all_to_all x1, waiting for transfers between devices, local(): lax.all_to_all(legendre, 'space', split_axis=1, concat_axis=0, tiled=True)  39 us
    reduce_sum x8, other arithmetic, spectral_block(): pulls = jnp.sum(differences / magnitude[:, None], axis=3)  20.7 us
  transfers between devices with their start and end apart: 6, of which 5 were waited for; matrix products, arithmetic and copies ran while one was open for 3% of the time, Pallas kernels for 0%

commit v1 on v0

v1 whole, which is shorter than its diff:
```python
import functools
import math

import jax
import jax.numpy as jnp
from jax import lax
from jax.experimental import pallas as pl
from jax.experimental.pallas import tpu as pltpu
from jax.sharding import PartitionSpec as P

FAIR_GAP = 0.05
SOFTEN = 0.1
MIB = 1024 * 1024
BAND = 16
LANES = 128
ROW_PAD = 40


def latitude_weights(lat_count):
    row_index = jnp.arange(lat_count, dtype=jnp.float32)
    sine_values = jnp.sin((row_index + 0.5) * (math.pi / lat_count))
    return sine_values * (lat_count / jnp.sum(sine_values))


def write_table(orders_ref, table_ref):
    lon_count = table_ref.shape[0]
    order_count = orders_ref.shape[1]
    chunk = 160
    norm = 1.0 / math.sqrt(lon_count)
    listed = orders_ref[...].astype(jnp.float32)

    def fill(step, _):
        start = pl.multiple_of(step * chunk, chunk)
        rows = lax.broadcasted_iota(jnp.int32, (chunk, order_count), 0) + start
        product = rows.astype(jnp.float32) * listed
        turns = jnp.floor(product * (1.0 / lon_count))
        phase = product - turns * lon_count
        quarter = jnp.floor(phase * (4.0 / lon_count) + 0.5)
        angle = (phase - quarter * (lon_count / 4.0)) * (2.0 * math.pi / lon_count)
        square = angle * angle
        sine = angle * (
            1.0 + square * (-1.0 / 6 + square * (1.0 / 120 + square * (-1.0 / 5040 + square / 362880)))
        )
        cosine = 1.0 + square * (
            -0.5 + square * (1.0 / 24 + square * (-1.0 / 720 + square * (1.0 / 40320)))
        )
        half = jnp.floor(quarter * 0.5)
        odd = quarter - 2.0 * half
        half_odd = half - 2.0 * jnp.floor(half * 0.5)
        flip = 1.0 - 2.0 * half_odd
        swap = odd > 0.5
        cos_value = jnp.where(swap, -sine, cosine) * flip
        sin_value = jnp.where(swap, cosine, sine) * flip
        table_ref[pl.ds(start, chunk), :order_count] = (cos_value * norm).astype(jnp.bfloat16)
        table_ref[pl.ds(start, chunk), order_count:] = (-sin_value * norm).astype(jnp.bfloat16)
        return 0

    lax.fori_loop(0, lon_count // chunk, fill, 0)


def forward_kernel(
    var_count, start_ref, orders_ref, ens_ref, truth_ref, leg_ref, out_ref, table_ref,
    staged, swapped, truth_part, leg_part, sems,
):
    step = pl.program_id(0)
    own_rows = 2 * var_count * BAND
    block = ens_ref.shape[0]
    deg_part = leg_part.shape[0]
    var_part = truth_part.shape[0]
    leg_at = 2 * own_rows
    truth_at = leg_at + deg_part * BAND
    truth_rows = var_part * BAND
    used = truth_at + 2 * truth_rows
    order_count = orders_ref.shape[1]

    @pl.when(step == 0)
    def _():
        truth_copy = pltpu.make_async_copy(
            truth_ref.at[pl.ds(start_ref[0], var_part)], truth_part, sems.at[0]
        )
        leg_copy = pltpu.make_async_copy(
            leg_ref.at[pl.ds(start_ref[1], deg_part)], leg_part, sems.at[1]
        )
        truth_copy.start()
        leg_copy.start()
        write_table(orders_ref, table_ref)
        staged[used:, :] = jnp.zeros((staged.shape[0] - used, order_count), jnp.float32)
        truth_copy.wait()
        rows = jnp.dot(
            truth_part[...].reshape(truth_rows, -1), table_ref[...],
            preferred_element_type=jnp.float32,
        )
        staged[truth_at : truth_at + truth_rows, :] = rows[:, :order_count]
        staged[truth_at + truth_rows : used, :] = rows[:, order_count:]
        leg_copy.wait()
        staged[leg_at:truth_at, :] = (
            leg_part[...].reshape(deg_part * BAND, order_count).astype(jnp.float32)
        )

    rows = jnp.dot(ens_ref[...], table_ref[...], preferred_element_type=jnp.float32)
    at = pl.multiple_of(step * block, block)
    staged[pl.ds(at, block), :] = rows[:, :order_count]
    staged[pl.ds(own_rows + at, block), :] = rows[:, order_count:]

    @pl.when(step == pl.num_programs(0) - 1)
    def _():
        width = staged.shape[0] // BAND
        for row in range(BAND):
            piece = staged[pl.ds(row, width, stride=BAND), :]
            swapped[0, pl.ds(row, order_count, stride=BAND), :] = piece[:LANES].T
            swapped[1, pl.ds(row, order_count, stride=BAND), :] = piece[LANES:].T
        for part in range(2):
            out_ref[:, :, part * LANES : (part + 1) * LANES] = (
                swapped[part].reshape(order_count, BAND, LANES).astype(jnp.bfloat16)
            )


def forward(ens, truth, legendre, orders, member_index, member_count):
    own_count, var_count, band_rows, lon_count = ens.shape
    order_count = orders.shape[0]
    deg_count = legendre.shape[2]
    deg_part = -(-deg_count // member_count)
    var_part = -(-var_count // member_count)
    starts = jnp.stack(
        [
            jnp.minimum(member_index * var_part, var_count - var_part),
            jnp.minimum(member_index * deg_part, deg_count - deg_part),
        ]
    ).astype(jnp.int32)
    rows = own_count * var_count * band_rows
    steps = 4
    width = 2 * LANES
    return pl.pallas_call(
        functools.partial(forward_kernel, var_count),
        grid=(steps,),
        in_specs=[
            pl.BlockSpec(memory_space=pltpu.SMEM),
            pl.BlockSpec((1, order_count), lambda i: (0, 0)),
            pl.BlockSpec((rows // steps, lon_count), lambda i: (i, 0)),
            pl.BlockSpec(memory_space=pl.ANY),
            pl.BlockSpec(memory_space=pl.ANY),
        ],
        out_specs=[
            pl.BlockSpec((order_count, band_rows, width), lambda i: (0, 0, 0)),
            pl.BlockSpec((lon_count, 2 * order_count), lambda i: (0, 0)),
        ],
        out_shape=[
            jax.ShapeDtypeStruct((order_count, band_rows, width), jnp.bfloat16),
            jax.ShapeDtypeStruct((lon_count, 2 * order_count), jnp.bfloat16),
        ],
        scratch_shapes=[
            pltpu.VMEM((width * band_rows, order_count), jnp.float32),
            pltpu.VMEM((2, order_count * band_rows, LANES), jnp.float32),
            pltpu.VMEM((var_part, band_rows, lon_count), jnp.bfloat16),
            pltpu.VMEM((deg_part, band_rows, order_count), jnp.bfloat16),
            pltpu.SemaphoreType.DMA((2,)),
        ],
        compiler_params=pltpu.CompilerParams(vmem_limit_bytes=32 * MIB),
        cost_estimate=pl.CostEstimate(
            flops=2 * rows * lon_count * 2 * order_count, bytes_accessed=6 * MIB, transcendentals=0
        ),
        name="forward",
    )(starts, orders.reshape(1, -1), ens.reshape(rows, lon_count), truth,
      jnp.transpose(legendre, (2, 0, 1)))


def spectral_kernel(
    fairness, member_count, var_count, deg_count, omega_ref, in_ref, grad_ref, score_ref,
    weights, values, spectra, pulls, scores,
):
    ens_count = 2 * member_count
    deg_part = -(-deg_count // member_count)
    var_part = -(-var_count // member_count)
    lat_count = weights.shape[0]
    space_count = lat_count // BAND
    leg_at = 4 * var_count
    truth_at = leg_at + deg_part
    omega = omega_ref[0]
    spread_scale = -fairness / (ens_count * (ens_count - 1))
    pull_scale = -fairness / (ens_count - 1)

    values[...] = jnp.zeros_like(values)
    weights[...] = jnp.zeros_like(weights)
    for member in range(member_count):
        block = in_ref[:, member].reshape(lat_count, 2 * LANES)
        deg_start = min(member * deg_part, deg_count - deg_part)
        weights[:, deg_start : deg_start + deg_part] = block[:, leg_at : leg_at + deg_part].astype(
            jnp.float32
        )
        turned = block.astype(jnp.float32).T
        var_start = min(member * var_part, var_count - var_part)
        for c in range(2):
            for own in range(2):
                at = (c * (ens_count + 1) + 2 * member + own) * ROW_PAD
                source = (2 * c + own) * var_count
                values[at : at + var_count, :] = turned[source : source + var_count]
            at = (c * (ens_count + 1) + ens_count) * ROW_PAD + var_start
            source = truth_at + c * var_part
            values[at : at + var_part, :] = turned[source : source + var_part]
    table = weights[...].astype(jnp.bfloat16)
    spectra[...] = jnp.dot(
        values[...].astype(jnp.bfloat16), table, preferred_element_type=jnp.float32
    )

    def tile(index, _):
        lane_tile = index % (weights.shape[1] // LANES)
        row_tile = index // (weights.shape[1] // LANES)
        lanes = pl.ds(pl.multiple_of(lane_tile * LANES, LANES), LANES)

        def load(c, e):
            at = (c * (ens_count + 1) + e) * ROW_PAD
            return spectra[pl.ds(pl.multiple_of(at + row_tile * 8, 8), 8), lanes]

        def pair(a, b):
            d0 = a[0] - b[0]
            d1 = a[1] - b[1]
            square = d0 * d0 + d1 * d1 + SOFTEN * SOFTEN
            inverse = lax.rsqrt(square)
            return square * inverse, d0 * inverse, d1 * inverse

        z = [(load(0, e), load(1, e)) for e in range(ens_count)]
        y = (load(0, ens_count), load(1, ens_count))
        zero = jnp.zeros((8, LANES), jnp.float32)
        pull = [[zero, zero] for _ in range(ens_count)]
        spread = zero
        for i in range(ens_count):
            for j in range(i + 1, ens_count):
                size, u0, u1 = pair(z[i], z[j])
                spread = spread + size
                pull[i][0] = pull[i][0] + u0
                pull[i][1] = pull[i][1] + u1
                pull[j][0] = pull[j][0] - u0
                pull[j][1] = pull[j][1] - u1
        error = zero
        for e in range(ens_count):
            size, u0, u1 = pair(z[e], y)
            error = error + size
            for c, u in enumerate((u0, u1)):
                at = ((e // 2) * 4 + 2 * c + e % 2) * ROW_PAD
                pulls[pl.ds(pl.multiple_of(at + row_tile * 8, 8), 8), lanes] = omega * (
                    u + pull_scale * pull[e][c]
                )
        pairs = ens_count * (ens_count - 1) // 2
        score = (error - SOFTEN * ens_count) * (1.0 / ens_count) + spread_scale * (
            spread - SOFTEN * pairs
        )
        scores[pl.ds(pl.multiple_of(row_tile * 8, 8), 8), lanes] = score
        return 0

    lax.fori_loop(0, (ROW_PAD // 8) * (weights.shape[1] // LANES), tile, 0)
    score_ref[...] = scores[:var_count, :deg_count].astype(jnp.bfloat16)
    for member in range(member_count):
        part = pulls[member * 4 * ROW_PAD : (member + 1) * 4 * ROW_PAD, :].astype(jnp.bfloat16)
        back = lax.dot_general(
            table, part, (((1,), (1,)), ((), ())), preferred_element_type=jnp.float32
        ).astype(jnp.bfloat16)
        grad_ref[:, member, :, : 4 * ROW_PAD] = back.reshape(space_count, BAND, 4 * ROW_PAD)
        grad_ref[:, member, :, 4 * ROW_PAD :] = jnp.zeros(
            (space_count, BAND, 2 * LANES - 4 * ROW_PAD), jnp.bfloat16
        )


def spectral(received, omega, fairness, member_count, var_count, deg_count):
    senders, band_rows, width = received.shape
    space_count = senders // member_count
    lat_count = space_count * band_rows
    deg_pad = -(-deg_count // LANES) * LANES
    ens_count = 2 * member_count
    grads, score = pl.pallas_call(
        functools.partial(spectral_kernel, fairness, member_count, var_count, deg_count),
        in_specs=[
            pl.BlockSpec(memory_space=pltpu.SMEM),
            pl.BlockSpec(memory_space=pltpu.VMEM),
        ],
        out_specs=[pl.BlockSpec(memory_space=pltpu.VMEM)] * 2,
        out_shape=[
            jax.ShapeDtypeStruct((space_count, member_count, band_rows, width), jnp.bfloat16),
            jax.ShapeDtypeStruct((var_count, deg_count), jnp.bfloat16),
        ],
        scratch_shapes=[
            pltpu.VMEM((lat_count, deg_pad), jnp.float32),
            pltpu.VMEM((2 * (ens_count + 1) * ROW_PAD, lat_count), jnp.float32),
            pltpu.VMEM((2 * (ens_count + 1) * ROW_PAD, deg_pad), jnp.float32),
            pltpu.VMEM((2 * ens_count * ROW_PAD, deg_pad), jnp.float32),
            pltpu.VMEM((ROW_PAD, deg_pad), jnp.float32),
        ],
        compiler_params=pltpu.CompilerParams(vmem_limit_bytes=40 * MIB),
        cost_estimate=pl.CostEstimate(
            flops=60_000_000, bytes_accessed=40 * MIB, transcendentals=0
        ),
        name="spectral",
    )(omega, received.reshape(space_count, member_count, band_rows, width))
    return grads.reshape(received.shape), score


def backward_kernel(var_count, in_ref, table_ref, out_ref, staged, turned):
    step = pl.program_id(0)
    order_count = in_ref.shape[0]
    block = out_ref.shape[0]
    rows = 2 * var_count * BAND

    @pl.when(step == 0)
    def _():
        for part in range(2):
            staged[part] = (
                in_ref[:, :, part * LANES : (part + 1) * LANES]
                .astype(jnp.float32)
                .reshape(order_count * BAND, LANES)
            )
        for row in range(BAND):
            low = staged[0, pl.ds(row, order_count, stride=BAND), :].T
            high = staged[1, pl.ds(row, order_count, stride=BAND), :].T
            whole = jnp.concatenate([low, high], axis=0)
            for c in range(2):
                for own in range(2):
                    source = (2 * c + own) * ROW_PAD
                    at = own * var_count * BAND + row
                    turned[c, pl.ds(at, var_count, stride=BAND), :] = whole[
                        source : source + var_count
                    ]

    at = pl.multiple_of(step * block, block)
    left = jnp.concatenate(
        [turned[0, pl.ds(at, block), :], turned[1, pl.ds(at, block), :]], axis=1
    ).astype(jnp.bfloat16)
    out_ref[...] = lax.dot_general(
        left, table_ref[...], (((1,), (1,)), ((), ())), preferred_element_type=jnp.float32
    ).astype(jnp.bfloat16)


def backward(received, table, own_count, var_count):
    order_count, band_rows, width = received.shape
    lon_count = table.shape[0]
    rows = own_count * var_count * band_rows
    steps = 4
    return pl.pallas_call(
        functools.partial(backward_kernel, var_count),
        grid=(steps,),
        in_specs=[
            pl.BlockSpec((order_count, band_rows, width), lambda i: (0, 0, 0)),
            pl.BlockSpec((lon_count, 2 * order_count), lambda i: (0, 0)),
        ],
        out_specs=pl.BlockSpec((rows // steps, lon_count), lambda i: (i, 0)),
        out_shape=jax.ShapeDtypeStruct((rows, lon_count), jnp.bfloat16),
        scratch_shapes=[
            pltpu.VMEM((2, order_count * band_rows, LANES), jnp.float32),
            pltpu.VMEM((2, rows, order_count), jnp.float32),
        ],
        compiler_params=pltpu.CompilerParams(vmem_limit_bytes=32 * MIB),
        cost_estimate=pl.CostEstimate(
            flops=2 * rows * lon_count * 2 * order_count, bytes_accessed=6 * MIB, transcendentals=0
        ),
        name="backward",
    )(received, table)


def grid_kernel(fairness, lon_count, ens_ref, truth_ref, weight_ref, grad_ref, score_ref, total):
    step = pl.program_id(0)
    ens_count, row_count, width = ens_ref.shape
    one = jnp.ones((1, 1), jnp.bfloat16)
    spread_scale = -fairness / (ens_count * (ens_count - 1))
    pull_scale = -fairness / (ens_count - 1)

    @pl.when(step == 0)
    def _():
        total[...] = jnp.zeros_like(total)

    def sign(a, b):
        zero = jnp.zeros(a.shape, jnp.bfloat16)
        return jnp.where(a > b, zero + one, jnp.where(b > a, zero - one, zero))

    def tile(at, rows, lane_at):
        span = pl.ds(at, rows)
        lanes = slice(lane_at, lane_at + LANES)
        x = [ens_ref[e, span, lanes] for e in range(ens_count)]
        y = truth_ref[span, lanes]
        sums = [jnp.zeros((rows, LANES), jnp.bfloat16) for _ in range(ens_count)]
        for i in range(ens_count):
            for j in range(i + 1, ens_count):
                s = sign(x[i], x[j])
                sums[i] = sums[i] + s
                sums[j] = sums[j] - s
        goal = y.astype(jnp.float32)
        weight = weight_ref[span, :]
        error = jnp.zeros((rows, LANES), jnp.float32)
        spread = jnp.zeros((rows, LANES), jnp.float32)
        for e in range(ens_count):
            value = x[e].astype(jnp.float32)
            toward = sums[e].astype(jnp.float32)
            error = error + jnp.abs(value - goal)
            spread = spread + value * toward
            grad_ref[e, span, lanes] = (
                weight * (sign(x[e], y).astype(jnp.float32) + pull_scale * toward)
            ).astype(jnp.bfloat16)
        score = error * (1.0 / ens_count) + spread_scale * spread
        lane = lax.broadcasted_iota(jnp.int32, (rows, LANES), 1) + (step * width + lane_at)
        total[span, :] += jnp.where(lane < lon_count, score, 0.0)

    whole = row_count // 16
    for lane_at in range(0, width, LANES):
        def body(index, _, lane_at=lane_at):
            tile(pl.multiple_of(index * 16, 16), 16, lane_at)
            return 0

        lax.fori_loop(0, whole, body, 0)
        if row_count % 16:
            tile(whole * 16, row_count % 16, lane_at)

    @pl.when(step == pl.num_programs(0) - 1)
    def _():
        score_ref[...] = jnp.sum(total[...], axis=1, keepdims=True) * (1.0 / lon_count)


def grid_scores(members, target, weights, fairness):
    ens_count, row_count, lon_count = members.shape
    width = 2 * LANES
    return pl.pallas_call(
        functools.partial(grid_kernel, fairness, lon_count),
        grid=(-(-lon_count // width),),
        in_specs=[
            pl.BlockSpec((ens_count, row_count, width), lambda i: (0, 0, i)),
            pl.BlockSpec((row_count, width), lambda i: (0, i)),
            pl.BlockSpec((row_count, 1), lambda i: (0, 0)),
        ],
        out_specs=[
            pl.BlockSpec((ens_count, row_count, width), lambda i: (0, 0, i)),
            pl.BlockSpec((row_count, 1), lambda i: (0, 0)),
        ],
        out_shape=[
            jax.ShapeDtypeStruct((ens_count, row_count, lon_count), jnp.bfloat16),
            jax.ShapeDtypeStruct((row_count, 1), jnp.float32),
        ],
        scratch_shapes=[pltpu.VMEM((row_count, LANES), jnp.float32)],
        compiler_params=pltpu.CompilerParams(vmem_limit_bytes=32 * MIB),
        cost_estimate=pl.CostEstimate(
            flops=60_000_000, bytes_accessed=40 * MIB, transcendentals=0
        ),
        name="grid",
    )(members, target, weights)


def local(ens, truth, legendre, orders):
    own_count, var_count, band_rows, lon_count = ens.shape
    order_count = orders.shape[0]
    deg_count = legendre.shape[2]
    space_count = lax.axis_size("space")
    member_count = lax.axis_size("member")
    space_index = lax.axis_index("space")
    member_index = lax.axis_index("member")
    lat_count = band_rows * space_count
    ens_count = own_count * member_count
    sub_rows = band_rows // member_count
    fairness = 1.0 - FAIR_GAP / ens_count

    owners = ("space", "member")
    sent, table = forward(ens, truth, legendre, orders, member_index, member_count)
    received = lax.all_to_all(sent, owners, split_axis=0, concat_axis=0, tiled=True)
    own_order = lax.dynamic_slice_in_dim(orders, space_index * member_count + member_index, 1, 0)
    omega = jnp.where(own_order == 0, 1.0, 2.0).astype(jnp.float32)
    grads, score = spectral(received, omega, fairness, member_count, var_count, deg_count)
    returned = lax.all_to_all(grads, owners, split_axis=0, concat_axis=0, tiled=True)
    spec_grad = backward(returned, table, own_count, var_count).reshape(ens.shape)
    spec_score = lax.all_gather(score, "member", axis=0, tiled=False).astype(jnp.float32)

    parted = ens.reshape(own_count, var_count, member_count, sub_rows, lon_count)
    parted = parted.transpose(2, 0, 3, 1, 4).reshape(
        member_count, own_count * sub_rows * var_count, lon_count
    )
    gathered = lax.all_to_all(parted, "member", split_axis=0, concat_axis=0, tiled=True)
    members = gathered.reshape(ens_count, sub_rows * var_count, lon_count)
    target = lax.dynamic_slice_in_dim(truth, member_index * sub_rows, sub_rows, 1)
    target = target.transpose(1, 0, 2).reshape(sub_rows * var_count, lon_count)
    row_weights = lax.dynamic_slice_in_dim(
        latitude_weights(lat_count), space_index * band_rows + member_index * sub_rows, sub_rows, 0
    )
    row_weights = jnp.broadcast_to(row_weights[:, None], (sub_rows, var_count)).reshape(-1, 1)
    grid_grad, grid_rows = grid_scores(members, target, row_weights, fairness)
    grid_grad = grid_grad.reshape(ens_count, sub_rows, var_count, lon_count).swapaxes(1, 2)
    grid_grad = grid_grad.reshape(ens_count, var_count, 1, sub_rows, lon_count)
    grid_score = grid_rows.reshape(sub_rows, var_count).T.reshape(var_count, 1, sub_rows)
    return (grid_score, grid_grad, spec_score, spec_grad)


def solution(mesh):
    in_specs = (
        P("member", None, "space", None),
        P(None, "space", None),
        P("space", None, None),
        P(),
    )
    out_specs = (
        P(None, "space", "member"),
        P(None, None, "space", "member", None),
        P("space", None, None),
        P("member", None, "space", None),
    )
    return jax.shard_map(local, mesh=mesh, in_specs=in_specs, out_specs=out_specs, check_vma=False)
```

time: 1020 us -> 200 us (0.20)
  waiting for transfers between devices: 565 us -> 26.7 us
  other arithmetic: 268 us -> 0.88 us
  local copies, waits for them, and re-layouts: 130 us -> 32.9 us
  blocking collectives: 0 us -> 75.2 us
  Pallas kernels: 0 us -> 40 us
  matrix products: 20.5 us -> 0 us
  between operations: 14.9 us -> 2.15 us
    all_gather x2 -> x0, waiting for transfers between devices: 446 us -> none  [the longest x1 283 us: local(): gathered = lax.all_gather(ens, 'member', axis=0, tiled=True)]
    reduce_sum x51 -> x0, other arithmetic: 108 us -> none  [the longest x9 64.2 us: grid_block(): sign_sums = jnp.sum(jnp.sign(differences), axis=1)]
    add x16 -> x0, other arithmetic: 83.5 us -> none  [add_band(): return running + lax.optimization_barrier(band_part).astype(jnp.float32)]
    all_gather x0 -> x1, blocking collectives: none -> 75.2 us  [local(): lax.all_gather(score, 'member', axis=0, tiled=False).astype(jnp.float32)]
    psum x1 -> x0, waiting for transfers between devices: 68.9 us -> none  [local(): lax.psum(score_share.astype(jnp.bfloat16), 'member').astype(jnp.float32)]
    dynamic_slice x42 -> x1, local copies, waits for them, and re-layouts: 43.4 us -> 0.59 us  [local(): lax.dynamic_slice_in_dim(orders, space_index * member_count + member_inde...]
    pallas_call x0 -> x4, Pallas kernels: none -> 40 us  [the longest x1 15.1 us: grid_scores(): pl.pallas_call(functools.partial(grid_kernel, fairness, lon_count), grid=...]
    convert_element_type x35 -> x0, other arithmetic: 30.2 us -> none  [the longest x8 17.6 us: spectral_block(): values = members.astype(jnp.float32)]
  transfers between devices with their start and end apart: 6 -> 3, of which waited for: 5 -> 2; matrix products, arithmetic and copies ran while one was open for 3% -> 7% of each run, Pallas kernels for 0% -> 3%
where the time goes in v1:
time: 200 us; the launch traced here: 199 us
  blocking collectives  75.2 us (38%)
  Pallas kernels  40 us (20%)
  local copies, waits for them, and re-layouts  32.9 us (16%)
  waiting for transfers between devices  26.7 us (13%)
  starting transfers between devices  21.6 us (11%)
  between operations  2.15 us (1%)
    all_gather x1, blocking collectives, local(): lax.all_gather(score, 'member', axis=0, tiled=False).astype(jnp.float32)  75.2 us
    unnamed x33, local copies, waits for them, and re-layouts  22.4 us
    all_to_all x1, waiting for transfers between devices, local(): lax.all_to_all(sent, owners, split_axis=0, concat_axis=0, tiled=True)  16.3 us
    pallas_call x1, Pallas kernels, grid_scores(): pl.pallas_call(functools.partial(grid_kernel, fairness, lon_count), grid=...  15.1 us
    pallas_call x1, Pallas kernels, spectral(): pl.pallas_call(functools.partial(spectral_kernel, fairness, member_count,...  13.7 us
    all_to_all x1, starting transfers between devices, local(): lax.all_to_all(sent, owners, split_axis=0, concat_axis=0, tiled=True)  11.7 us
    all_to_all x1, waiting for transfers between devices, local(): lax.all_to_all(grads, owners, split_axis=0, concat_axis=0, tiled=True)  10.4 us
    all_to_all x1, starting transfers between devices, local(): lax.all_to_all(grads, owners, split_axis=0, concat_axis=0, tiled=True)  6.08 us
  transfers between devices with their start and end apart: 3, of which 2 were waited for; matrix products, arithmetic and copies ran while one was open for 7% of the time, Pallas kernels for 3%

profile of v1, /device:TPU:0, one launch (start us, length us, event | category | flops | bytes accessed | tf_op | source)
XLA Modules:
  0.0 199.4 jit_solution(11875161021769794984)
XLA Ops:
  0.6 0.1 pad_add_fusion.start_ref
  0.7 0.0 copy-start
  0.7 2.0 %copy-done = bf16[2,36,16,1440]{3,2,1,0:T(8,128)(2,1)S(1)} copy-done((bf16[2,36,16,1440]{3,2,1,0:T(8,128)(2,1)S(1)}, bf16[2,36,16,1440]{3,2,1,0:T(8,128)(2,1)}, u32[]{:S(2)}) %copy-start) | copy-done | bytes 3317784
  2.7 0.0 copy-start.2
  2.7 1.8 copy-done.2
  4.6 0.0 copy-start.3
  4.6 1.5 copy-done.3
  6.0 0.0 copy-start.13
  6.0 0.7 copy-done.13
  6.7 0.0 copy-start.14
  6.7 5.7 %forward.1 = (bf16[128,16,256]{2,1,0:T(8,128)(2,1)S(1)}, bf16[1440,256]{1,0:T(8,128)(2,1)S(1)}) custom-call(s32[2]{0:T(128)S(1)} %pad_add_fusion.start_ref, s32[1,128]{1,0:T(1,128)S(1)} %bitcast.29, bf16[1152,1440]{1,0:T(8,128)(2,1)S(1)} %bitcast.25, bf16[36,16,1440]{2,1,0:T(8,128)(2,1)S(1)} %copy-done.3, bf16[721,16,128]{2,1,0:T(8,128)(2,1)S(1)} %bitcast.26), custom_call_target="tpu_custom_call" | custom-call | flops 849346560 | bytes 6291456 | tf_op jit(solution)/shard_map/forward/pallas_call | solution.py:133
  12.4 0.0 copy-start.4
  12.4 1.0 copy-done.4
  13.4 0.0 copy-start.7
  13.4 0.9 copy-done.7
  14.3 0.0 copy-start.1
  14.3 11.7 %all-to-all-start.1 = ((bf16[128,16,256]{2,1,0:T(8,128)(2,1)}), bf16[128,16,256]{2,1,0:T(8,128)(2,1)}, u32[]{:S(2)}, u32[]{:S(2)}) async-start(bf16[128,16,256]{2,1,0:T(8,128)(2,1)} %copy-done.4), calls=%async_computation.1 | async-start | bytes 2097152 | tf_op jit(solution)/shard_map/all_to_all | solution.py:457
  26.0 0.0 copy-done.14
  26.0 0.6 dynamic_slice.11
  27.3 16.3 %all-to-all-done.1 = bf16[128,16,256]{2,1,0:T(8,128)(2,1)} async-done(((bf16[128,16,256]{2,1,0:T(8,128)(2,1)}), bf16[128,16,256]{2,1,0:T(8,128)(2,1)}, u32[]{:S(2)}, u32[]{:S(2)}) %all-to-all-start.1) | async-done | bytes 1048608 | tf_op jit(solution)/shard_map/all_to_all | solution.py:457
  43.6 13.7 %spectral.1 = (bf16[16,8,16,256]{3,2,1,0:T(8,128)(2,1)S(1)}, bf16[36,721]{1,0:T(8,128)(2,1)S(1)}) custom-call(f32[1]{0:T(128)S(6)} %select_n.16.omega_ref, bf16[16,8,16,256]{3,2,1,0:T(8,128)(2,1)} %bitcast.15.in_ref), custom_call_target="tpu_custom_call" | custom-call | flops 60000000 | bytes 41943040 | tf_op jit(solution)/shard_map/spectral/pallas_call | solution.py:269
  57.3 0.0 copy-start.5
  57.3 1.0 copy-done.5
  58.3 0.0 copy-start.10
  58.3 0.6 copy-done.10
  58.9 6.1 %all-to-all-start.2 = ((bf16[128,16,256]{2,1,0:T(8,128)(2,1)}), bf16[128,16,256]{2,1,0:T(8,128)(2,1)}, u32[]{:S(2)}, u32[]{:S(2)}) async-start(bf16[128,16,256]{2,1,0:T(8,128)(2,1)} %bitcast.27), calls=%async_computation.2 | async-start | bytes 2097152 | tf_op jit(solution)/shard_map/all_to_all | solution.py:461
  65.0 0.0 copy-done.1
  65.0 3.6 %copy.27 = bf16[2,36,16,1440]{3,0,2,1:T(2,128)(2,1)S(1)} copy(bf16[2,36,16,1440]{3,2,1,0:T(8,128)(2,1)S(1)} %copy-done.1) | data formatting | bytes 6635520 | tf_op args[0]
  68.7 0.7 copy.28
  69.3 2.9 %copy.29 = bf16[8,144,1440]{2,1,0:T(8,128)(2,1)} copy(bf16[8,144,1440]{2,0,1:T(8,128)(2,1)S(1)} %bitcast.30) | data formatting | bytes 6635520 | tf_op jit(solution)/shard_map/reshape | solution.py:466
  72.2 10.4 %all-to-all-done.2.in_ref = bf16[128,16,256]{2,1,0:T(8,128)(2,1)} async-done(((bf16[128,16,256]{2,1,0:T(8,128)(2,1)}), bf16[128,16,256]{2,1,0:T(8,128)(2,1)}, u32[]{:S(2)}, u32[]{:S(2)}) %all-to-all-start.2) | async-done | bytes 1048608 | tf_op jit(solution)/shard_map/all_to_all | solution.py:461
  82.6 3.8 %all-to-all-start = ((bf16[8,144,1440]{2,1,0:T(8,128)(2,1)}), bf16[8,144,1440]{2,1,0:T(8,128)(2,1)S(1)}, u32[]{:S(2)}, u32[]{:S(2)}) async-start(bf16[8,144,1440]{2,1,0:T(8,128)(2,1)} %copy.29), calls=%async_computation | async-start | bytes 7077888 | tf_op jit(solution)/shard_map/all_to_all | solution.py:469
  86.4 0.7 fusion.1
  87.8 0.1 dynamic_slice.10
  87.9 0.1 broadcast_in_dim.6
  88.0 0.7 reshape.71.weight_ref
  88.7 1.4 dynamic-slice_bitcast_fusion
  90.1 0.7 copy.30
  90.8 1.7 reshape.54.truth_ref
  92.5 75.2 %all-gather.1 = bf16[8,36,721]{2,1,0:T(8,128)(2,1)S(1)} all-gather(bf16[1,36,721]{2,1,0:T(8,128)(2,1)} %bitcast.28), channel_id=2, replica_groups=mesh['member'=8,'space'=16] {'member'}, dimensions={0}, use_global_device_ids=true | all-gather | bytes 467208 | tf_op jit(solution)/shard_map/all_gather | solution.py:463
  167.7 1.0 copy.34
  168.7 0.0 copy-start.8
  168.7 1.1 copy-done.8
  169.8 5.4 %backward.1 = bf16[1152,1440]{1,0:T(8,128)(2,1)} custom-call(bf16[128,16,256]{2,1,0:T(8,128)(2,1)} %all-to-all-done.2.in_ref, bf16[1440,256]{1,0:T(8,128)(2,1)S(1)} %copy-done.8), custom_call_target="tpu_custom_call" | custom-call | flops 849346560 | bytes 6291456 | tf_op jit(solution)/shard_map/backward/pallas_call | solution.py:336
  175.2 0.0 all-to-all-done
  175.2 0.0 copy-start.6
  175.2 0.9 copy-done.6
  176.2 0.0 copy-start.9
  176.2 0.8 copy-done.9
  176.9 15.1 %grid.1 = (bf16[16,72,1440]{2,1,0:T(8,128)(2,1)S(1)}, f32[72,1]{1,0:T(8,128)S(1)}) custom-call(bf16[16,72,1440]{2,1,0:T(8,128)(2,1)S(1)} %bitcast.24, bf16[72,1440]{1,0:T(8,128)(2,1)S(1)} %copy-done.6, f32[72,1]{1,0:T(8,128)S(1)} %copy-done.9), custom_call_target="tpu_custom_call" | custom-call | flops 60000000 | bytes 41943040 | tf_op jit(solution)/shard_map/grid/pallas_call | solution.py:417
  192.1 0.0 copy-start.11
  192.1 1.1 copy.32
  193.1 0.0 copy-done.11
  193.1 0.0 copy-start.12
  193.2 5.4 %copy.33 = bf16[16,36,1,2,1440]{4,3,2,1,0:T(2,128)(2,1)} copy(bf16[16,36,1,2,1440]{4,0,1,3,2:T(8,128)(2,1)S(1)} %bitcast.31) | data formatting | bytes 6635520
  198.6 0.0 copy-done.12
  198.6 0.1 reduce
  198.7 0.7 reshape.56
  (1 shorter events, 0.0 us)
Async XLA Ops:
  0.7 2.0 %copy-start = (bf16[2,36,16,1440]{3,2,1,0:T(8,128)(2,1)S(1)}, bf16[2,36,16,1440]{3,2,1,0:T(8,128)(2,1)}, u32[]{:S(2)}) copy-start(bf16[2,36,16,1440]{3,2,1,0:T(8,128)(2,1)} %param.4) | copy-start | bytes 9953284
  2.7 1.8 copy-start.2
  4.6 1.5 copy-start.3
  6.0 0.7 copy-start.13
  6.7 19.3 %copy-start.14 = (s32[128]{0:T(128)S(1)}, s32[128]{0:T(128)}, u32[]{:S(2)}) copy-start(s32[128]{0:T(128)} %param.7) | copy-start | bytes 1540
  12.4 1.0 copy-start.4
  13.4 0.9 copy-start.7
  14.3 50.7 %copy-start.1 = (bf16[2,36,16,1440]{3,2,1,0:T(8,128)(2,1)S(1)}, bf16[2,36,16,1440]{3,2,1,0:T(8,128)(2,1)}, u32[]{:S(2)}) copy-start(bf16[2,36,16,1440]{3,2,1,0:T(8,128)(2,1)} %param.4) | copy-start | bytes 9953284
  14.3 29.3 %all-to-all-start.1 = ((bf16[128,16,256]{2,1,0:T(8,128)(2,1)}), bf16[128,16,256]{2,1,0:T(8,128)(2,1)}, u32[]{:S(2)}, u32[]{:S(2)}) async-start(bf16[128,16,256]{2,1,0:T(8,128)(2,1)} %copy-done.4), calls=%async_computation.1 | async-start | bytes 2097152 | tf_op jit(solution)/shard_map/all_to_all | solution.py:457
  57.3 1.0 copy-start.5
  58.3 0.6 copy-start.10
  58.9 23.7 %all-to-all-start.2 = ((bf16[128,16,256]{2,1,0:T(8,128)(2,1)}), bf16[128,16,256]{2,1,0:T(8,128)(2,1)}, u32[]{:S(2)}, u32[]{:S(2)}) async-start(bf16[128,16,256]{2,1,0:T(8,128)(2,1)} %bitcast.27), calls=%async_computation.2 | async-start | bytes 2097152 | tf_op jit(solution)/shard_map/all_to_all | solution.py:461
  82.6 92.7 %all-to-all-start = ((bf16[8,144,1440]{2,1,0:T(8,128)(2,1)}), bf16[8,144,1440]{2,1,0:T(8,128)(2,1)S(1)}, u32[]{:S(2)}, u32[]{:S(2)}) async-start(bf16[8,144,1440]{2,1,0:T(8,128)(2,1)} %copy.29), calls=%async_computation | async-start | bytes 7077888 | tf_op jit(solution)/shard_map/all_to_all | solution.py:469
  168.7 1.1 copy-start.8
  175.2 0.9 copy-start.6
  176.2 0.8 copy-start.9
  192.1 1.1 copy-start.11
  193.1 5.4 %copy-start.12 = (f32[72,1]{1,0:T(8,128)S(1)}, f32[72,1]{1,0:T(8,128)}, u32[]{:S(2)}) copy-start(f32[72,1]{1,0:T(8,128)} %copy-done.11) | copy-start | bytes 868

commit v2 on v1

--- a/solution.py
+++ b/solution.py
@@ -3,6 +3,7 @@
 
 import jax
 import jax.numpy as jnp
+import numpy as np
 from jax import lax
 from jax.experimental import pallas as pl
 from jax.experimental.pallas import tpu as pltpu
@@ -11,15 +12,16 @@
 FAIR_GAP = 0.05
 SOFTEN = 0.1
 MIB = 1024 * 1024
+COST = 1024
 BAND = 16
 LANES = 128
+HALF = 6 * LANES
 ROW_PAD = 40
 
 
 def latitude_weights(lat_count):
-    row_index = jnp.arange(lat_count, dtype=jnp.float32)
-    sine_values = jnp.sin((row_index + 0.5) * (math.pi / lat_count))
-    return sine_values * (lat_count / jnp.sum(sine_values))
+    sine_values = np.sin((np.arange(lat_count) + 0.5) * (math.pi / lat_count))
+    return (sine_values * (lat_count / sine_values.sum())).astype(np.float32)
 
 
 def write_table(orders_ref, table_ref):
@@ -155,10 +157,8 @@
             pltpu.VMEM((deg_part, band_rows, order_count), jnp.bfloat16),
             pltpu.SemaphoreType.DMA((2,)),
         ],
-        compiler_params=pltpu.CompilerParams(vmem_limit_bytes=32 * MIB),
-        cost_estimate=pl.CostEstimate(
-            flops=2 * rows * lon_count * 2 * order_count, bytes_accessed=6 * MIB, transcendentals=0
-        ),
+        compiler_params=pltpu.CompilerParams(vmem_limit_bytes=56 * MIB),
+        cost_estimate=pl.CostEstimate(flops=COST, bytes_accessed=COST, transcendentals=0),
         name="forward",
     )(starts, orders.reshape(1, -1), ens.reshape(rows, lon_count), truth,
       jnp.transpose(legendre, (2, 0, 1)))
@@ -253,11 +253,17 @@
         part = pulls[member * 4 * ROW_PAD : (member + 1) * 4 * ROW_PAD, :].astype(jnp.bfloat16)
         back = lax.dot_general(
             table, part, (((1,), (1,)), ((), ())), preferred_element_type=jnp.float32
-        ).astype(jnp.bfloat16)
-        grad_ref[:, member, :, : 4 * ROW_PAD] = back.reshape(space_count, BAND, 4 * ROW_PAD)
-        grad_ref[:, member, :, 4 * ROW_PAD :] = jnp.zeros(
-            (space_count, BAND, 2 * LANES - 4 * ROW_PAD), jnp.bfloat16
-        )
+        )
+        halves = back.reshape(space_count, 2, BAND // 2, 4 * ROW_PAD)
+        packed = jnp.concatenate(
+            [
+                halves[:, 0],
+                halves[:, 1],
+                jnp.zeros((space_count, BAND // 2, 3 * LANES - 8 * ROW_PAD), jnp.float32),
+            ],
+            axis=2,
+        )
+        grad_ref[:, member] = packed.astype(jnp.bfloat16)
 
 
 def spectral(received, omega, fairness, member_count, var_count, deg_count):
@@ -274,7 +280,9 @@
         ],
         out_specs=[pl.BlockSpec(memory_space=pltpu.VMEM)] * 2,
         out_shape=[
-            jax.ShapeDtypeStruct((space_count, member_count, band_rows, width), jnp.bfloat16),
+            jax.ShapeDtypeStruct(
+                (space_count, member_count, band_rows // 2, 3 * LANES), jnp.bfloat16
+            ),
             jax.ShapeDtypeStruct((var_count, deg_count), jnp.bfloat16),
         ],
         scratch_shapes=[
@@ -284,13 +292,11 @@
             pltpu.VMEM((2 * ens_count * ROW_PAD, deg_pad), jnp.float32),
             pltpu.VMEM((ROW_PAD, deg_pad), jnp.float32),
         ],
-        compiler_params=pltpu.CompilerParams(vmem_limit_bytes=40 * MIB),
-        cost_estimate=pl.CostEstimate(
-            flops=60_000_000, bytes_accessed=40 * MIB, transcendentals=0
-        ),
+        compiler_params=pltpu.CompilerParams(vmem_limit_bytes=56 * MIB),
+        cost_estimate=pl.CostEstimate(flops=COST, bytes_accessed=COST, transcendentals=0),
         name="spectral",
     )(omega, received.reshape(space_count, member_count, band_rows, width))
-    return grads.reshape(received.shape), score
+    return grads.reshape(senders, band_rows // 2, 3 * LANES), score
 
 
 def backward_kernel(var_count, in_ref, table_ref, out_ref, staged, turned):
@@ -301,23 +307,26 @@
 
     @pl.when(step == 0)
     def _():
-        for part in range(2):
+        half = BAND // 2
+        for part in range(3):
             staged[part] = (
                 in_ref[:, :, part * LANES : (part + 1) * LANES]
                 .astype(jnp.float32)
-                .reshape(order_count * BAND, LANES)
+                .reshape(order_count * half, LANES)
             )
-        for row in range(BAND):
-            low = staged[0, pl.ds(row, order_count, stride=BAND), :].T
-            high = staged[1, pl.ds(row, order_count, stride=BAND), :].T
-            whole = jnp.concatenate([low, high], axis=0)
-            for c in range(2):
-                for own in range(2):
-                    source = (2 * c + own) * ROW_PAD
-                    at = own * var_count * BAND + row
-                    turned[c, pl.ds(at, var_count, stride=BAND), :] = whole[
-                        source : source + var_count
-                    ]
+        for row in range(half):
+            whole = jnp.concatenate(
+                [staged[part, pl.ds(row, order_count, stride=half), :].T for part in range(3)],
+                axis=0,
+            )
+            for high in range(2):
+                for c in range(2):
+                    for own in range(2):
+                        source = (4 * high + 2 * c + own) * ROW_PAD
+                        at = own * var_count * BAND + high * half + row
+                        turned[c, pl.ds(at, var_count, stride=BAND), :] = whole[
+                            source : source + var_count
+                        ]
 
     at = pl.multiple_of(step * block, block)
     left = jnp.concatenate(
@@ -329,7 +338,8 @@
 
 
 def backward(received, table, own_count, var_count):
-    order_count, band_rows, width = received.shape
+    order_count, half_rows, width = received.shape
+    band_rows = 2 * half_rows
     lon_count = table.shape[0]
     rows = own_count * var_count * band_rows
     steps = 4
@@ -337,27 +347,84 @@
         functools.partial(backward_kernel, var_count),
         grid=(steps,),
         in_specs=[
-            pl.BlockSpec((order_count, band_rows, width), lambda i: (0, 0, 0)),
+            pl.BlockSpec((order_count, half_rows, width), lambda i: (0, 0, 0)),
             pl.BlockSpec((lon_count, 2 * order_count), lambda i: (0, 0)),
         ],
         out_specs=pl.BlockSpec((rows // steps, lon_count), lambda i: (i, 0)),
         out_shape=jax.ShapeDtypeStruct((rows, lon_count), jnp.bfloat16),
         scratch_shapes=[
-            pltpu.VMEM((2, order_count * band_rows, LANES), jnp.float32),
+            pltpu.VMEM((3, order_count * half_rows, LANES), jnp.float32),
             pltpu.VMEM((2, rows, order_count), jnp.float32),
         ],
-        compiler_params=pltpu.CompilerParams(vmem_limit_bytes=32 * MIB),
-        cost_estimate=pl.CostEstimate(
-            flops=2 * rows * lon_count * 2 * order_count, bytes_accessed=6 * MIB, transcendentals=0
-        ),
+        compiler_params=pltpu.CompilerParams(vmem_limit_bytes=56 * MIB),
+        cost_estimate=pl.CostEstimate(flops=COST, bytes_accessed=COST, transcendentals=0),
         name="backward",
     )(received, table)
 
 
-def grid_kernel(fairness, lon_count, ens_ref, truth_ref, weight_ref, grad_ref, score_ref, total):
+def regroup_kernel(var_count, sub_rows, member_ref, ens_ref, truth_ref, out_ref, target_ref,
+                   wide, paired):
+    member_count = out_ref.shape[0]
+
+    def move(rows_ref, lanes, tile, member, keep):
+        for row in range(sub_rows):
+            paired[tile, keep, pl.ds(row, var_count, stride=sub_rows), :] = wide[
+                tile, pl.ds(member * sub_rows + row, var_count, stride=BAND), :
+            ]
+        return paired[tile, keep].astype(jnp.bfloat16)
+
+    for tile in range(wide.shape[0]):
+        lanes = slice(tile * LANES, (tile + 1) * LANES)
+
+        @pl.when(pl.program_id(1) == 0)
+        def _(tile=tile, lanes=lanes):
+            wide[tile] = truth_ref[:, lanes].astype(jnp.float32)
+            target_ref[:, lanes] = move(truth_ref, lanes, tile, member_ref[0], 0)
+
+        wide[tile] = ens_ref[:, lanes].astype(jnp.float32)
+        for member in range(member_count):
+            out_ref[member, 0, :, lanes] = move(ens_ref, lanes, tile, member, member)
+
+
+def regroup(ens, truth, member_index, member_count, span):
+    own_count, var_count, band_rows, lon_count = ens.shape
+    sub_rows = band_rows // member_count
+    width = 3 * LANES
+    rows = var_count * sub_rows
+    first, last = span
+    begin = first // width
+    return pl.pallas_call(
+        functools.partial(regroup_kernel, var_count, sub_rows),
+        grid=(-(-(last - first) // width), own_count),
+        in_specs=[
+            pl.BlockSpec(memory_space=pltpu.SMEM),
+            pl.BlockSpec((var_count * band_rows, width), lambda i, e: (e, i + begin)),
+            pl.BlockSpec((var_count * band_rows, width), lambda i, e: (0, i + begin)),
+        ],
+        out_specs=[
+            pl.BlockSpec((member_count, 1, rows, width), lambda i, e: (0, e, 0, i)),
+            pl.BlockSpec((rows, width), lambda i, e: (0, i)),
+        ],
+        out_shape=[
+            jax.ShapeDtypeStruct((member_count, own_count, rows, last - first), jnp.bfloat16),
+            jax.ShapeDtypeStruct((rows, last - first), jnp.bfloat16),
+        ],
+        scratch_shapes=[
+            pltpu.VMEM((width // LANES, var_count * band_rows, LANES), jnp.float32),
+            pltpu.VMEM((width // LANES, member_count, rows, LANES), jnp.float32),
+        ],
+        compiler_params=pltpu.CompilerParams(vmem_limit_bytes=56 * MIB),
+        cost_estimate=pl.CostEstimate(flops=COST, bytes_accessed=COST, transcendentals=0),
+        name="regroup",
+    )(member_index.reshape(1).astype(jnp.int32), ens.reshape(-1, lon_count),
+      truth.reshape(-1, lon_count))
+
+
+def grid_kernel(fairness, lon_count, first, weight_ref, ens_ref, truth_ref, *rest):
+    grad_ref, score_ref, total = rest[-3:]
     step = pl.program_id(0)
     ens_count, row_count, width = ens_ref.shape
-    one = jnp.ones((1, 1), jnp.bfloat16)
+    sub_rows = grad_ref.shape[2]
     spread_scale = -fairness / (ens_count * (ens_count - 1))
     pull_scale = -fairness / (ens_count - 1)
 
@@ -365,9 +432,15 @@
     def _():
         total[...] = jnp.zeros_like(total)
 
+    which = lax.broadcasted_iota(jnp.int32, (16, LANES), 0) % sub_rows
+    row_weight = jnp.full((16, LANES), weight_ref[0], jnp.float32)
+    for row in range(1, sub_rows):
+        row_weight = jnp.where(which == row, weight_ref[row], row_weight)
+
     def sign(a, b):
         zero = jnp.zeros(a.shape, jnp.bfloat16)
-        return jnp.where(a > b, zero + one, jnp.where(b > a, zero - one, zero))
+        one = jnp.ones(a.shape, jnp.bfloat16)
+        return jnp.where(a > b, one, jnp.where(b > a, -one, zero))
 
     def tile(at, rows, lane_at):
         span = pl.ds(at, rows)
@@ -381,7 +454,7 @@
                 sums[i] = sums[i] + s
                 sums[j] = sums[j] - s
         goal = y.astype(jnp.float32)
-        weight = weight_ref[span, :]
+        weight = row_weight[:rows]
         error = jnp.zeros((rows, LANES), jnp.float32)
         spread = jnp.zeros((rows, LANES), jnp.float32)
         for e in range(ens_count):
@@ -389,11 +462,12 @@
             toward = sums[e].astype(jnp.float32)
             error = error + jnp.abs(value - goal)
             spread = spread + value * toward
-            grad_ref[e, span, lanes] = (
+            grad = (
                 weight * (sign(x[e], y).astype(jnp.float32) + pull_scale * toward)
             ).astype(jnp.bfloat16)
+            grad_ref[e, pl.ds(at // sub_rows, rows // sub_rows), :, lanes] = grad.reshape(rows // sub_rows, sub_rows, LANES)
         score = error * (1.0 / ens_count) + spread_scale * spread
-        lane = lax.broadcasted_iota(jnp.int32, (rows, LANES), 1) + (step * width + lane_at)
+        lane = lax.broadcasted_iota(jnp.int32, (rows, LANES), 1) + ((step + first) * width + lane_at)
         total[span, :] += jnp.where(lane < lon_count, score, 0.0)
 
     whole = row_count // 16
@@ -411,32 +485,35 @@
         score_ref[...] = jnp.sum(total[...], axis=1, keepdims=True) * (1.0 / lon_count)
 
 
-def grid_scores(members, target, weights, fairness):
-    ens_count, row_count, lon_count = members.shape
+def grid_scores(members, target, weights, fairness, lon_count, sub_rows, at, earlier=None):
+    ens_count, row_count, span = members.shape
+    var_count = row_count // sub_rows
     width = 2 * LANES
+    first = at // width
+    carried = () if earlier is None else (earlier,)
     return pl.pallas_call(
-        functools.partial(grid_kernel, fairness, lon_count),
-        grid=(-(-lon_count // width),),
+        functools.partial(grid_kernel, fairness, lon_count, first),
+        grid=(-(-span // width),),
         in_specs=[
+            pl.BlockSpec(memory_space=pltpu.SMEM),
             pl.BlockSpec((ens_count, row_count, width), lambda i: (0, 0, i)),
             pl.BlockSpec((row_count, width), lambda i: (0, i)),
+        ]
+        + [pl.BlockSpec(memory_space=pl.ANY)] * len(carried),
+        out_specs=[
+            pl.BlockSpec((ens_count, var_count, sub_rows, width), lambda i: (0, 0, 0, i + first)),
             pl.BlockSpec((row_count, 1), lambda i: (0, 0)),
         ],
-        out_specs=[
-            pl.BlockSpec((ens_count, row_count, width), lambda i: (0, 0, i)),
-            pl.BlockSpec((row_count, 1), lambda i: (0, 0)),
-        ],
         out_shape=[
-            jax.ShapeDtypeStruct((ens_count, row_count, lon_count), jnp.bfloat16),
+            jax.ShapeDtypeStruct((ens_count, var_count, sub_rows, lon_count), jnp.bfloat16),
             jax.ShapeDtypeStruct((row_count, 1), jnp.float32),
         ],
         scratch_shapes=[pltpu.VMEM((row_count, LANES), jnp.float32)],
-        compiler_params=pltpu.CompilerParams(vmem_limit_bytes=32 * MIB),
-        cost_estimate=pl.CostEstimate(
-            flops=60_000_000, bytes_accessed=40 * MIB, transcendentals=0
-        ),
+        input_output_aliases={3: 0} if carried else {},
+        compiler_params=pltpu.CompilerParams(vmem_limit_bytes=56 * MIB),
+        cost_estimate=pl.CostEstimate(flops=COST, bytes_accessed=COST, transcendentals=0),
         name="grid",
-    )(members, target, weights)
+    )(weights, members, target, *carried)
 
 
 def local(ens, truth, legendre, orders):
@@ -455,29 +532,40 @@
     owners = ("space", "member")
     sent, table = forward(ens, truth, legendre, orders, member_index, member_count)
     received = lax.all_to_all(sent, owners, split_axis=0, concat_axis=0, tiled=True)
+
+    spans = ((0, HALF), (HALF, lon_count))
+    halves = [regroup(ens, truth, member_index, member_count, span) for span in spans]
+    early, late = (half[0] for half in halves)
+    received, early, late = lax.optimization_barrier((received, early, late))
+
+    def exchange(half):
+        return lax.all_to_all(half, "member", split_axis=0, concat_axis=0, tiled=True).reshape(
+            ens_count, var_count * sub_rows, -1
+        )
+
+    early = exchange(early)
     own_order = lax.dynamic_slice_in_dim(orders, space_index * member_count + member_index, 1, 0)
     omega = jnp.where(own_order == 0, 1.0, 2.0).astype(jnp.float32)
     grads, score = spectral(received, omega, fairness, member_count, var_count, deg_count)
+    grads, early, late = lax.optimization_barrier((grads, early, late))
+    late = exchange(late)
+    row_weights = lax.dynamic_slice_in_dim(
+        jnp.asarray(latitude_weights(lat_count)),
+        space_index * band_rows + member_index * sub_rows, sub_rows, 0,
+    )
+    grid_args = (row_weights, fairness, lon_count, sub_rows)
+    grid_grad, early_rows = grid_scores(early, halves[0][1], *grid_args, 0)
+    grads, grid_grad, late = lax.optimization_barrier((grads, grid_grad, late))
     returned = lax.all_to_all(grads, owners, split_axis=0, concat_axis=0, tiled=True)
+    grid_grad, late_rows = grid_scores(late, halves[1][1], *grid_args, HALF, grid_grad)
+    grid_grad = grid_grad.reshape(ens_count, var_count, 1, sub_rows, lon_count)
+    grid_score = (early_rows + late_rows).reshape(var_count, 1, sub_rows)
+
+    returned, score, grid_grad = lax.optimization_barrier((returned, score, grid_grad))
+    copies = jnp.broadcast_to(score[None], (member_count,) + score.shape)
+    spec_score = lax.all_to_all(copies, "member", split_axis=0, concat_axis=0, tiled=True)
+    spec_score = spec_score.astype(jnp.float32)
     spec_grad = backward(returned, table, own_count, var_count).reshape(ens.shape)
-    spec_score = lax.all_gather(score, "member", axis=0, tiled=False).astype(jnp.float32)
-
-    parted = ens.reshape(own_count, var_count, member_count, sub_rows, lon_count)
-    parted = parted.transpose(2, 0, 3, 1, 4).reshape(
-        member_count, own_count * sub_rows * var_count, lon_count
-    )
-    gathered = lax.all_to_all(parted, "member", split_axis=0, concat_axis=0, tiled=True)
-    members = gathered.reshape(ens_count, sub_rows * var_count, lon_count)
-    target = lax.dynamic_slice_in_dim(truth, member_index * sub_rows, sub_rows, 1)
-    target = target.transpose(1, 0, 2).reshape(sub_rows * var_count, lon_count)
-    row_weights = lax.dynamic_slice_in_dim(
-        latitude_weights(lat_count), space_index * band_rows + member_index * sub_rows, sub_rows, 0
-    )
-    row_weights = jnp.broadcast_to(row_weights[:, None], (sub_rows, var_count)).reshape(-1, 1)
-    grid_grad, grid_rows = grid_scores(members, target, row_weights, fairness)
-    grid_grad = grid_grad.reshape(ens_count, sub_rows, var_count, lon_count).swapaxes(1, 2)
-    grid_grad = grid_grad.reshape(ens_count, var_count, 1, sub_rows, lon_count)
-    grid_score = grid_rows.reshape(sub_rows, var_count).T.reshape(var_count, 1, sub_rows)
     return (grid_score, grid_grad, spec_score, spec_grad)
 
 

time: 200 us -> 139 us (0.69)
  blocking collectives: 75.2 us -> 0 us
  local copies, waits for them, and re-layouts: 32.9 us -> 3.84 us
  Pallas kernels: 40 us -> 58.4 us
  waiting for transfers between devices: 26.7 us -> 41.6 us
  starting transfers between devices: 21.6 us -> 30.5 us
    all_gather x1 -> x0, blocking collectives: 75.2 us -> none  [local(): lax.all_gather(score, 'member', axis=0, tiled=False).astype(jnp.float32)]
    all_to_all x1 -> x3, waiting for transfers between devices: 0.01 us -> 28.8 us  [the longest x2 23.8 us: exchange(): lax.all_to_all(half, 'member', split_axis=0, concat_axis=0, tiled=True)]
    unnamed x33 -> x18, local copies, waits for them, and re-layouts: 22.4 us -> 1.68 us
    pallas_call x1 -> x4, Pallas kernels: 15.1 us -> 30.5 us  [the longest x2 20.2 us: grid_scores(): pl.pallas_call(functools.partial(grid_kernel, fairness, lon_count, first)...]
    all_to_all x1 -> x3, starting transfers between devices: 3.85 us -> 14.7 us  [the longest x2 10.8 us: exchange(): lax.all_to_all(half, 'member', split_axis=0, concat_axis=0, tiled=True)]
    all_to_all x1, waiting for transfers between devices: 16.3 us -> 7.67 us  [local(): lax.all_to_all(sent, owners, split_axis=0, concat_axis=0, tiled=True)]
    reshape x4 -> x1, local copies, waits for them, and re-layouts: 5.95 us -> 0.11 us  [local(): grid_score = (early_rows + late_rows).reshape(var_count, 1, sub_rows)]
    all_to_all x1, waiting for transfers between devices: 10.4 us -> 5.2 us  [local(): lax.all_to_all(grads, owners, split_axis=0, concat_axis=0, tiled=True)]
  transfers between devices with their start and end apart: 3 -> 5, of which waited for: 2 -> 5; matrix products, arithmetic and copies ran while one was open for 7% -> 2% of each run, Pallas kernels for 3% -> 37%
where the time goes in v2:
time: 139 us; the launch traced here: 137 us
  Pallas kernels  58.4 us (42%)
  waiting for transfers between devices  41.6 us (30%)
  starting transfers between devices  30.5 us (22%)
  local copies, waits for them, and re-layouts  3.84 us (3%)
  other arithmetic  1.47 us (1%)
  between operations  1.4 us (1%)
    all_to_all x2, waiting for transfers between devices, exchange(): lax.all_to_all(half, 'member', split_axis=0, concat_axis=0, tiled=True)  23.8 us
    pallas_call x2, Pallas kernels, grid_scores(): pl.pallas_call(functools.partial(grid_kernel, fairness, lon_count, first)...  20.2 us
    pallas_call x1, Pallas kernels, spectral(): pl.pallas_call(functools.partial(spectral_kernel, fairness, member_count,...  14.7 us
    all_to_all x1, starting transfers between devices, local(): lax.all_to_all(sent, owners, split_axis=0, concat_axis=0, tiled=True)  11.1 us
    all_to_all x2, starting transfers between devices, exchange(): lax.all_to_all(half, 'member', split_axis=0, concat_axis=0, tiled=True)  10.8 us
    pallas_call x2, Pallas kernels, regroup(): pl.pallas_call(functools.partial(regroup_kernel, var_count, sub_rows), gr...  10.3 us
    pallas_call x1, Pallas kernels, forward(): pl.pallas_call(functools.partial(forward_kernel, var_count), grid=(steps,...  7.89 us
    all_to_all x1, waiting for transfers between devices, local(): lax.all_to_all(sent, owners, split_axis=0, concat_axis=0, tiled=True)  7.67 us
  transfers between devices with their start and end apart: 5, of which 5 were waited for; matrix products, arithmetic and copies ran while one was open for 2% of the time, Pallas kernels for 37%

profile of v2, /device:TPU:0, one launch (start us, length us, event | category | flops | bytes accessed | tf_op | source)
XLA Modules:
  0.0 137.2 jit_solution(7037581595716179012)
XLA Ops:
  0.6 0.6 pad_add_fusion.start_ref
  1.2 7.9 %forward.1 = (bf16[128,16,256]{2,1,0:T(8,128)(2,1)}, bf16[1440,256]{1,0:T(8,128)(2,1)}) custom-call(s32[2]{0:T(128)} %pad_add_fusion.start_ref, s32[1,128]{1,0:T(1,128)} %bitcast.26, bf16[1152,1440]{1,0:T(8,128)(2,1)} %bitcast.14, bf16[36,16,1440]{2,1,0:T(8,128)(2,1)} %truth_ref.1, bf16[721,16,128]{2,1,0:T(8,128)(2,1)} %bitcast.24), custom_call_target="tpu_custom_call" | custom-call | flops 1024 | bytes 1024 | tf_op jit(solution)/shard_map/forward/pallas_call | solution.py:135
  9.1 11.1 %all-to-all-start = ((bf16[128,16,256]{2,1,0:T(8,128)(2,1)}), bf16[128,16,256]{2,1,0:T(8,128)(2,1)S(1)}, u32[]{:S(2)}, u32[]{:S(2)}) async-start(bf16[128,16,256]{2,1,0:T(8,128)(2,1)} %get-tuple-element.28), calls=%async_computation | async-start | bytes 2097152 | tf_op jit(solution)/shard_map/all_to_all | solution.py:534
  20.3 5.2 %regroup.3 = (bf16[8,2,72,672]{3,2,1,0:T(8,128)(2,1)}, bf16[72,672]{1,0:T(8,128)(2,1)}) custom-call(s32[1]{0:T(128)} %bitcast.5.member_ref, bf16[1152,1440]{1,0:T(8,128)(2,1)} %bitcast.15, bf16[576,1440]{1,0:T(8,128)(2,1)} %bitcast.17), custom_call_target="tpu_custom_call" | custom-call | flops 1024 | bytes 1024 | tf_op jit(solution)/shard_map/regroup/pallas_call | solution.py:396
  25.5 5.1 %regroup.2 = (bf16[8,2,72,768]{3,2,1,0:T(8,128)(2,1)}, bf16[72,768]{1,0:T(8,128)(2,1)}) custom-call(s32[1]{0:T(128)} %bitcast.5.member_ref, bf16[1152,1440]{1,0:T(8,128)(2,1)} %bitcast.16, bf16[576,1440]{1,0:T(8,128)(2,1)} %bitcast.18), custom_call_target="tpu_custom_call" | custom-call | flops 1024 | bytes 1024 | tf_op jit(solution)/shard_map/regroup/pallas_call | solution.py:396
  30.6 0.0 copy-start.6
  30.6 7.7 %all-to-all-done = bf16[128,16,256]{2,1,0:T(8,128)(2,1)S(1)} async-done(((bf16[128,16,256]{2,1,0:T(8,128)(2,1)}), bf16[128,16,256]{2,1,0:T(8,128)(2,1)S(1)}, u32[]{:S(2)}, u32[]{:S(2)}) %all-to-all-start) | async-done | bytes 1048608 | tf_op jit(solution)/shard_map/all_to_all | solution.py:534
  38.3 0.0 copy-start.2
  38.3 3.8 %all-to-all-start.1 = ((bf16[8,2,72,768]{3,2,1,0:T(8,128)(2,1)}), bf16[8,2,72,768]{3,2,1,0:T(8,128)(2,1)S(1)}, u32[]{:S(2)}, u32[]{:S(2)}) async-start(bf16[8,2,72,768]{3,2,1,0:T(8,128)(2,1)} %get-tuple-element.33), calls=%async_computation.1 | async-start | bytes 3538944 | tf_op jit(solution)/shard_map/all_to_all | solution.py:542
  42.1 0.0 copy-start.7
  42.1 0.0 copy-done.6
  42.2 0.6 dynamic_slice.7
  43.4 0.0 copy-done.2
  43.4 14.7 %spectral.1 = (bf16[16,8,8,384]{3,2,1,0:T(8,128)(2,1)}, bf16[36,721]{1,0:T(8,128)(2,1)}) custom-call(f32[1]{0:T(128)S(6)} %select_n.12.omega_ref, bf16[16,8,16,256]{3,2,1,0:T(8,128)(2,1)} %bitcast.21), custom_call_target="tpu_custom_call" | custom-call | flops 1024 | bytes 1024 | tf_op jit(solution)/shard_map/spectral/pallas_call | solution.py:275
  58.1 9.8 %all-to-all-done.1 = bf16[8,2,72,768]{3,2,1,0:T(8,128)(2,1)S(1)} async-done(((bf16[8,2,72,768]{3,2,1,0:T(8,128)(2,1)}), bf16[8,2,72,768]{3,2,1,0:T(8,128)(2,1)S(1)}, u32[]{:S(2)}, u32[]{:S(2)}) %all-to-all-start.1) | async-done | bytes 1769504 | tf_op jit(solution)/shard_map/all_to_all | solution.py:542
  67.9 0.0 copy-start.1
  67.9 6.9 %all-to-all-start.2 = ((bf16[8,2,72,672]{3,2,1,0:T(8,128)(2,1)}), bf16[8,2,72,672]{3,2,1,0:T(8,128)(2,1)S(1)}, u32[]{:S(2)}, u32[]{:S(2)}) async-start(bf16[8,2,72,672]{3,2,1,0:T(8,128)(2,1)} %get-tuple-element.40), calls=%async_computation.2 | async-start | bytes 3538944 | tf_op jit(solution)/shard_map/all_to_all | solution.py:542
  74.9 0.0 copy-done.7
  74.9 0.6 dynamic_slice.6.weight_ref
  75.5 0.0 copy-done.1
  75.5 10.1 %grid.2 = (bf16[16,36,2,1440]{3,2,1,0:T(2,128)(2,1)}, f32[72,1]{1,0:T(8,128)}) custom-call(f32[2]{0:T(128)} %dynamic_slice.6.weight_ref, bf16[16,72,768]{2,1,0:T(8,128)(2,1)} %bitcast.20, bf16[72,768]{1,0:T(8,128)(2,1)} %get-tuple-element.36.truth_ref), custom_call_target="tpu_custom_call" | custom-call | flops 1024 | bytes 1024 | tf_op jit(solution)/shard_map/grid/pallas_call | solution.py:494
  85.6 14.0 %all-to-all-done.2 = bf16[8,2,72,672]{3,2,1,0:T(8,128)(2,1)S(1)} async-done(((bf16[8,2,72,672]{3,2,1,0:T(8,128)(2,1)}), bf16[8,2,72,672]{3,2,1,0:T(8,128)(2,1)S(1)}, u32[]{:S(2)}, u32[]{:S(2)}) %all-to-all-start.2) | async-done | bytes 1548320 | tf_op jit(solution)/shard_map/all_to_all | solution.py:542
  99.6 0.0 copy-start
  99.6 4.6 %all-to-all-start.3 = ((bf16[128,8,384]{2,1,0:T(8,128)(2,1)}), bf16[128,8,384]{2,1,0:T(8,128)(2,1)S(1)}, u32[]{:S(2)}, u32[]{:S(2)}) async-start(bf16[128,8,384]{2,1,0:T(8,128)(2,1)} %bitcast.25), calls=%async_computation.3 | async-start | bytes 1572864 | tf_op jit(solution)/shard_map/all_to_all | solution.py:559
  104.2 0.0 copy-start.4
  104.2 0.0 copy-done
  104.2 0.0 copy-start.5
  104.2 10.1 %grid.3 = (bf16[16,36,2,1440]{3,2,1,0:T(2,128)(2,1)}, f32[72,1]{1,0:T(8,128)}) custom-call(f32[2]{0:T(128)} %dynamic_slice.6.weight_ref, bf16[16,72,672]{2,1,0:T(8,128)(2,1)} %bitcast.19, bf16[72,672]{1,0:T(8,128)(2,1)} %get-tuple-element.42.truth_ref, bf16[16,36,2,1440]{3,2,1,0:T(2,128)(2,1)} %get-tuple-element.43.rest_0_), custom_call_target="tpu_custom_call", output_to_operand_aliasing={{0}: (3, {})} | custom-call | flops 1024 | bytes 1024 | tf_op jit(solution)/shard_map/grid/pallas_call | solution.py:494
  114.3 5.2 %all-to-all-done.3.in_ref = bf16[128,8,384]{2,1,0:T(8,128)(2,1)S(1)} async-done(((bf16[128,8,384]{2,1,0:T(8,128)(2,1)}), bf16[128,8,384]{2,1,0:T(8,128)(2,1)S(1)}, u32[]{:S(2)}, u32[]{:S(2)}) %all-to-all-start.3) | async-done | bytes 786464 | tf_op jit(solution)/shard_map/all_to_all | solution.py:559
  119.5 0.0 copy-start.3
  119.6 0.0 copy-done.4
  119.6 0.9 broadcast_in_dim.6
  120.4 3.9 %all-to-all-start.4 = ((bf16[8,36,721]{2,1,0:T(8,128)(2,1)}), bf16[8,36,721]{2,1,0:T(8,128)(2,1)S(1)}, u32[]{:S(2)}, u32[]{:S(2)}) async-start(bf16[8,36,721]{2,1,0:T(8,128)(2,1)} %broadcast_in_dim.6), calls=%async_computation.4 | async-start | bytes 983040 | tf_op jit(solution)/shard_map/all_to_all | solution.py:566
  124.4 0.0 copy-done.5
  124.4 0.9 add_reduce_fusion
  125.2 0.1 reshape.54
  125.4 0.6 copy.14
  126.0 0.0 copy-done.3
  126.0 5.3 %backward.1 = bf16[1152,1440]{1,0:T(8,128)(2,1)} custom-call(bf16[128,8,384]{2,1,0:T(8,128)(2,1)} %copy-done.3, bf16[1440,256]{1,0:T(8,128)(2,1)} %get-tuple-element.51.table_ref), custom_call_target="tpu_custom_call" | custom-call | flops 1024 | bytes 1024 | tf_op jit(solution)/shard_map/backward/pallas_call | solution.py:346
  131.3 4.9 %all-to-all-done.4 = bf16[8,36,721]{2,1,0:T(8,128)(2,1)S(1)} async-done(((bf16[8,36,721]{2,1,0:T(8,128)(2,1)}), bf16[8,36,721]{2,1,0:T(8,128)(2,1)S(1)}, u32[]{:S(2)}, u32[]{:S(2)}) %all-to-all-start.4) | async-done | bytes 415328 | tf_op jit(solution)/shard_map/all_to_all | solution.py:566
  136.2 1.0 copy.16
Async XLA Ops:
  9.1 29.2 %all-to-all-start = ((bf16[128,16,256]{2,1,0:T(8,128)(2,1)}), bf16[128,16,256]{2,1,0:T(8,128)(2,1)S(1)}, u32[]{:S(2)}, u32[]{:S(2)}) async-start(bf16[128,16,256]{2,1,0:T(8,128)(2,1)} %get-tuple-element.28), calls=%async_computation | async-start | bytes 2097152 | tf_op jit(solution)/shard_map/all_to_all | solution.py:534
  30.6 11.5 %copy-start.6 = (s32[128]{0:T(128)S(1)}, s32[128]{0:T(128)}, u32[]{:S(2)}) copy-start(s32[128]{0:T(128)} %param.8) | copy-start | bytes 1540
  38.3 5.1 %copy-start.2 = (bf16[128,16,256]{2,1,0:T(8,128)(2,1)}, bf16[128,16,256]{2,1,0:T(8,128)(2,1)S(1)}, u32[]{:S(2)}) copy-start(bf16[128,16,256]{2,1,0:T(8,128)(2,1)S(1)} %all-to-all-done) | copy-start | bytes 3145732
  38.3 29.6 %all-to-all-start.1 = ((bf16[8,2,72,768]{3,2,1,0:T(8,128)(2,1)}), bf16[8,2,72,768]{3,2,1,0:T(8,128)(2,1)S(1)}, u32[]{:S(2)}, u32[]{:S(2)}) async-start(bf16[8,2,72,768]{3,2,1,0:T(8,128)(2,1)} %get-tuple-element.33), calls=%async_computation.1 | async-start | bytes 3538944 | tf_op jit(solution)/shard_map/all_to_all | solution.py:542
  42.1 32.7 %copy-start.7 = (f32[256]{0:T(256)S(1)}, f32[256]{0:T(256)}, u32[]{:S(2)}) copy-start(f32[256]{0:T(256)} %constant.39.clone) | copy-start | bytes 3076
  67.9 7.5 %copy-start.1 = (bf16[8,2,72,768]{3,2,1,0:T(8,128)(2,1)}, bf16[8,2,72,768]{3,2,1,0:T(8,128)(2,1)S(1)}, u32[]{:S(2)}) copy-start(bf16[8,2,72,768]{3,2,1,0:T(8,128)(2,1)S(1)} %all-to-all-done.1) | copy-start | bytes 5308420
  67.9 31.6 %all-to-all-start.2 = ((bf16[8,2,72,672]{3,2,1,0:T(8,128)(2,1)}), bf16[8,2,72,672]{3,2,1,0:T(8,128)(2,1)S(1)}, u32[]{:S(2)}, u32[]{:S(2)}) async-start(bf16[8,2,72,672]{3,2,1,0:T(8,128)(2,1)} %get-tuple-element.40), calls=%async_computation.2 | async-start | bytes 3538944 | tf_op jit(solution)/shard_map/all_to_all | solution.py:542
  99.6 4.6 %copy-start = (bf16[8,2,72,672]{3,2,1,0:T(8,128)(2,1)}, bf16[8,2,72,672]{3,2,1,0:T(8,128)(2,1)S(1)}, u32[]{:S(2)}) copy-start(bf16[8,2,72,672]{3,2,1,0:T(8,128)(2,1)S(1)} %all-to-all-done.2) | copy-start | bytes 4644868
  99.6 20.0 %all-to-all-start.3 = ((bf16[128,8,384]{2,1,0:T(8,128)(2,1)}), bf16[128,8,384]{2,1,0:T(8,128)(2,1)S(1)}, u32[]{:S(2)}, u32[]{:S(2)}) async-start(bf16[128,8,384]{2,1,0:T(8,128)(2,1)} %bitcast.25), calls=%async_computation.3 | async-start | bytes 1572864 | tf_op jit(solution)/shard_map/all_to_all | solution.py:559
  104.2 15.4 %copy-start.4 = (bf16[36,721]{1,0:T(8,128)(2,1)S(1)}, bf16[36,721]{1,0:T(8,128)(2,1)}, u32[]{:S(2)}) copy-start(bf16[36,721]{1,0:T(8,128)(2,1)} %get-tuple-element.49) | copy-start | bytes 155740
  104.2 20.1 %copy-start.5 = (f32[72,1]{1,0:T(8,128)S(1)}, f32[72,1]{1,0:T(8,128)}, u32[]{:S(2)}) copy-start(f32[72,1]{1,0:T(8,128)} %get-tuple-element.37) | copy-start | bytes 868
  119.5 6.5 %copy-start.3 = (bf16[128,8,384]{2,1,0:T(8,128)(2,1)}, bf16[128,8,384]{2,1,0:T(8,128)(2,1)S(1)}, u32[]{:S(2)}) copy-start(bf16[128,8,384]{2,1,0:T(8,128)(2,1)S(1)} %all-to-all-done.3.in_ref) | copy-start | bytes 2359300
  120.4 15.8 %all-to-all-start.4 = ((bf16[8,36,721]{2,1,0:T(8,128)(2,1)}), bf16[8,36,721]{2,1,0:T(8,128)(2,1)S(1)}, u32[]{:S(2)}, u32[]{:S(2)}) async-start(bf16[8,36,721]{2,1,0:T(8,128)(2,1)} %broadcast_in_dim.6), calls=%async_computation.4 | async-start | bytes 983040 | tf_op jit(solution)/shard_map/all_to_all | solution.py:566

commit v3 on v2

--- a/solution.py
+++ b/solution.py
@@ -15,7 +15,8 @@
 COST = 1024
 BAND = 16
 LANES = 128
-HALF = 6 * LANES
+GRID_WIDTH = 2 * LANES
+EARLY_BLOCKS = 3
 ROW_PAD = 40
 
 
@@ -61,7 +62,7 @@
 
 
 def forward_kernel(
-    var_count, start_ref, orders_ref, ens_ref, truth_ref, leg_ref, out_ref, table_ref,
+    var_count, deg_count, orders_ref, ens_ref, truth_ref, leg_ref, out_ref, table_ref,
     staged, swapped, truth_part, leg_part, sems,
 ):
     step = pl.program_id(0)
@@ -77,11 +78,14 @@
 
     @pl.when(step == 0)
     def _():
+        member = lax.axis_index("member")
+        var_start = jnp.minimum(member * var_part, var_count - var_part)
+        deg_start = jnp.minimum(member * deg_part, deg_count - deg_part)
         truth_copy = pltpu.make_async_copy(
-            truth_ref.at[pl.ds(start_ref[0], var_part)], truth_part, sems.at[0]
+            truth_ref.at[pl.ds(var_start, var_part)], truth_part, sems.at[0]
         )
         leg_copy = pltpu.make_async_copy(
-            leg_ref.at[pl.ds(start_ref[1], deg_part)], leg_part, sems.at[1]
+            leg_ref.at[pl.ds(deg_start, deg_part)], leg_part, sems.at[1]
         )
         truth_copy.start()
         leg_copy.start()
@@ -117,26 +121,19 @@
             )
 
 
-def forward(ens, truth, legendre, orders, member_index, member_count):
+def forward(ens, truth, legendre, orders, member_count):
     own_count, var_count, band_rows, lon_count = ens.shape
     order_count = orders.shape[0]
     deg_count = legendre.shape[2]
     deg_part = -(-deg_count // member_count)
     var_part = -(-var_count // member_count)
-    starts = jnp.stack(
-        [
-            jnp.minimum(member_index * var_part, var_count - var_part),
-            jnp.minimum(member_index * deg_part, deg_count - deg_part),
-        ]
-    ).astype(jnp.int32)
     rows = own_count * var_count * band_rows
     steps = 4
     width = 2 * LANES
     return pl.pallas_call(
-        functools.partial(forward_kernel, var_count),
+        functools.partial(forward_kernel, var_count, deg_count),
         grid=(steps,),
         in_specs=[
-            pl.BlockSpec(memory_space=pltpu.SMEM),
             pl.BlockSpec((1, order_count), lambda i: (0, 0)),
             pl.BlockSpec((rows // steps, lon_count), lambda i: (i, 0)),
             pl.BlockSpec(memory_space=pl.ANY),
@@ -160,12 +157,12 @@
         compiler_params=pltpu.CompilerParams(vmem_limit_bytes=56 * MIB),
         cost_estimate=pl.CostEstimate(flops=COST, bytes_accessed=COST, transcendentals=0),
         name="forward",
-    )(starts, orders.reshape(1, -1), ens.reshape(rows, lon_count), truth,
+    )(orders.reshape(1, -1), ens.reshape(rows, lon_count), truth,
       jnp.transpose(legendre, (2, 0, 1)))
 
 
 def spectral_kernel(
-    fairness, member_count, var_count, deg_count, omega_ref, in_ref, grad_ref, score_ref,
+    fairness, member_count, var_count, deg_count, orders_ref, in_ref, grad_ref, score_ref,
     weights, values, spectra, pulls, scores,
 ):
     ens_count = 2 * member_count
@@ -175,7 +172,8 @@
     space_count = lat_count // BAND
     leg_at = 4 * var_count
     truth_at = leg_at + deg_part
-    omega = omega_ref[0]
+    own_order = orders_ref[lax.axis_index("space") * member_count + lax.axis_index("member")]
+    omega = jnp.where(own_order == 0, 1.0, 2.0).astype(jnp.float32)
     spread_scale = -fairness / (ens_count * (ens_count - 1))
     pull_scale = -fairness / (ens_count - 1)
 
@@ -248,7 +246,9 @@
         return 0
 
     lax.fori_loop(0, (ROW_PAD // 8) * (weights.shape[1] // LANES), tile, 0)
-    score_ref[...] = scores[:var_count, :deg_count].astype(jnp.bfloat16)
+    rounded = scores[:var_count, :deg_count].astype(jnp.bfloat16)
+    for member in range(member_count):
+        score_ref[member] = rounded
     for member in range(member_count):
         part = pulls[member * 4 * ROW_PAD : (member + 1) * 4 * ROW_PAD, :].astype(jnp.bfloat16)
         back = lax.dot_general(
@@ -266,7 +266,7 @@
         grad_ref[:, member] = packed.astype(jnp.bfloat16)
 
 
-def spectral(received, omega, fairness, member_count, var_count, deg_count):
+def spectral(received, orders, fairness, member_count, var_count, deg_count):
     senders, band_rows, width = received.shape
     space_count = senders // member_count
     lat_count = space_count * band_rows
@@ -283,7 +283,7 @@
             jax.ShapeDtypeStruct(
                 (space_count, member_count, band_rows // 2, 3 * LANES), jnp.bfloat16
             ),
-            jax.ShapeDtypeStruct((var_count, deg_count), jnp.bfloat16),
+            jax.ShapeDtypeStruct((member_count, var_count, deg_count), jnp.bfloat16),
         ],
         scratch_shapes=[
             pltpu.VMEM((lat_count, deg_pad), jnp.float32),
@@ -295,7 +295,7 @@
         compiler_params=pltpu.CompilerParams(vmem_limit_bytes=56 * MIB),
         cost_estimate=pl.CostEstimate(flops=COST, bytes_accessed=COST, transcendentals=0),
         name="spectral",
-    )(omega, received.reshape(space_count, member_count, band_rows, width))
+    )(orders, received.reshape(space_count, member_count, band_rows, width))
     return grads.reshape(senders, band_rows // 2, 3 * LANES), score
 
 
@@ -362,14 +362,27 @@
     )(received, table)
 
 
-def regroup_kernel(var_count, sub_rows, member_ref, ens_ref, truth_ref, out_ref, target_ref,
-                   wide, paired):
-    member_count = out_ref.shape[0]
-
-    def move(rows_ref, lanes, tile, member, keep):
+HOPS = ((0, 0), (0, 1), (0, 3), (1, 0), (0, 2), (1, 1), (1, 3), (1, 2))
+RING = 4
+
+
+def partner(member, hop, sign):
+    half, spot = member // RING, member % RING
+    return (half + hop[0]) % 2 * RING + (spot + sign * hop[1] + RING) % RING
+
+
+def hop_pairs(hop, member_count):
+    return [(i, partner(i, hop, 1)) for i in range(member_count)]
+
+
+def regroup_kernel(var_count, sub_rows, ens_ref, truth_ref, *rest):
+    outs, (target_ref, wide, paired) = rest[:-3], rest[-3:]
+    member = lax.axis_index("member")
+
+    def move(tile, goal, keep):
         for row in range(sub_rows):
             paired[tile, keep, pl.ds(row, var_count, stride=sub_rows), :] = wide[
-                tile, pl.ds(member * sub_rows + row, var_count, stride=BAND), :
+                tile, pl.ds(goal * sub_rows + row, var_count, stride=BAND), :
             ]
         return paired[tile, keep].astype(jnp.bfloat16)
 
@@ -379,36 +392,32 @@
         @pl.when(pl.program_id(1) == 0)
         def _(tile=tile, lanes=lanes):
             wide[tile] = truth_ref[:, lanes].astype(jnp.float32)
-            target_ref[:, lanes] = move(truth_ref, lanes, tile, member_ref[0], 0)
+            target_ref[:, lanes] = move(tile, member, 0)
 
         wide[tile] = ens_ref[:, lanes].astype(jnp.float32)
-        for member in range(member_count):
-            out_ref[member, 0, :, lanes] = move(ens_ref, lanes, tile, member, member)
-
-
-def regroup(ens, truth, member_index, member_count, span):
+        for place, hop in enumerate(HOPS):
+            outs[place][0, :, lanes] = move(tile, partner(member, hop, 1), place)
+
+
+def regroup(ens, truth, member_count):
     own_count, var_count, band_rows, lon_count = ens.shape
     sub_rows = band_rows // member_count
     width = 3 * LANES
     rows = var_count * sub_rows
-    first, last = span
-    begin = first // width
     return pl.pallas_call(
         functools.partial(regroup_kernel, var_count, sub_rows),
-        grid=(-(-(last - first) // width), own_count),
+        grid=(-(-lon_count // width), own_count),
         in_specs=[
-            pl.BlockSpec(memory_space=pltpu.SMEM),
-            pl.BlockSpec((var_count * band_rows, width), lambda i, e: (e, i + begin)),
-            pl.BlockSpec((var_count * band_rows, width), lambda i, e: (0, i + begin)),
-        ],
-        out_specs=[
-            pl.BlockSpec((member_count, 1, rows, width), lambda i, e: (0, e, 0, i)),
-            pl.BlockSpec((rows, width), lambda i, e: (0, i)),
-        ],
+            pl.BlockSpec((var_count * band_rows, width), lambda i, e: (e, i)),
+            pl.BlockSpec((var_count * band_rows, width), lambda i, e: (0, i)),
+        ],
+        out_specs=[pl.BlockSpec((1, rows, width), lambda i, e: (e, 0, i))] * member_count
+        + [pl.BlockSpec((rows, width), lambda i, e: (0, i))],
         out_shape=[
-            jax.ShapeDtypeStruct((member_count, own_count, rows, last - first), jnp.bfloat16),
-            jax.ShapeDtypeStruct((rows, last - first), jnp.bfloat16),
-        ],
+            jax.ShapeDtypeStruct((own_count, rows, lon_count), jnp.bfloat16)
+            for _ in range(member_count)
+        ]
+        + [jax.ShapeDtypeStruct((rows, lon_count), jnp.bfloat16)],
         scratch_shapes=[
             pltpu.VMEM((width // LANES, var_count * band_rows, LANES), jnp.float32),
             pltpu.VMEM((width // LANES, member_count, rows, LANES), jnp.float32),
@@ -416,59 +425,74 @@
         compiler_params=pltpu.CompilerParams(vmem_limit_bytes=56 * MIB),
         cost_estimate=pl.CostEstimate(flops=COST, bytes_accessed=COST, transcendentals=0),
         name="regroup",
-    )(member_index.reshape(1).astype(jnp.int32), ens.reshape(-1, lon_count),
-      truth.reshape(-1, lon_count))
-
-
-def grid_kernel(fairness, lon_count, first, weight_ref, ens_ref, truth_ref, *rest):
+    )(ens.reshape(-1, lon_count), truth.reshape(-1, lon_count))
+
+
+def grid_kernel(fairness, lon_count, first, part_count, weight_ref, truth_ref, *rest):
+    parts, carried = rest[:part_count], rest[part_count:-3]
     grad_ref, score_ref, total = rest[-3:]
     step = pl.program_id(0)
-    ens_count, row_count, width = ens_ref.shape
+    per_part, row_count, width = parts[0].shape
+    ens_count = per_part * part_count
     sub_rows = grad_ref.shape[2]
-    spread_scale = -fairness / (ens_count * (ens_count - 1))
     pull_scale = -fairness / (ens_count - 1)
+    member = lax.axis_index("member")
+    senders = [partner(member, hop, -1) for hop in HOPS]
+    lat_start = (lax.axis_index("space") * part_count + member) * sub_rows
+    which = lax.broadcasted_iota(jnp.int32, (8, LANES), 0) % sub_rows
+    weight = jnp.full((8, LANES), weight_ref[lat_start], jnp.float32)
+    for row in range(1, sub_rows):
+        weight = jnp.where(which == row, weight_ref[lat_start + row], weight)
 
     @pl.when(step == 0)
     def _():
         total[...] = jnp.zeros_like(total)
 
-    which = lax.broadcasted_iota(jnp.int32, (16, LANES), 0) % sub_rows
-    row_weight = jnp.full((16, LANES), weight_ref[0], jnp.float32)
-    for row in range(1, sub_rows):
-        row_weight = jnp.where(which == row, weight_ref[row], row_weight)
-
     def sign(a, b):
-        zero = jnp.zeros(a.shape, jnp.bfloat16)
-        one = jnp.ones(a.shape, jnp.bfloat16)
-        return jnp.where(a > b, one, jnp.where(b > a, -one, zero))
+        return jnp.minimum(jnp.maximum((a - b) * 2.0**70, -1.0), 1.0)
 
     def tile(at, rows, lane_at):
+        lanes = slice(lane_at, lane_at + LANES)
         span = pl.ds(at, rows)
-        lanes = slice(lane_at, lane_at + LANES)
-        x = [ens_ref[e, span, lanes] for e in range(ens_count)]
-        y = truth_ref[span, lanes]
-        sums = [jnp.zeros((rows, LANES), jnp.bfloat16) for _ in range(ens_count)]
-        for i in range(ens_count):
-            for j in range(i + 1, ens_count):
-                s = sign(x[i], x[j])
-                sums[i] = sums[i] + s
-                sums[j] = sums[j] - s
-        goal = y.astype(jnp.float32)
-        weight = row_weight[:rows]
-        error = jnp.zeros((rows, LANES), jnp.float32)
-        spread = jnp.zeros((rows, LANES), jnp.float32)
+        wide = [
+            parts[e // per_part][e % per_part, span, lanes].astype(jnp.float32)
+            for e in range(ens_count)
+        ]
+        goals = truth_ref[span, lanes].astype(jnp.float32)
+        pieces = []
+        for half in range(rows // 8):
+            piece = slice(8 * half, 8 * half + 8)
+            x = [value[piece] * 2.0**64 for value in wide]
+            goal = goals[piece]
+            y = goal * 2.0**64
+            zero = jnp.zeros((8, LANES), jnp.float32)
+            sums = [zero] * ens_count
+            for i in range(ens_count):
+                for j in range(i + 1, ens_count):
+                    s = sign(x[i], x[j])
+                    sums[i] = sums[i] + s
+                    sums[j] = sums[j] - s
+            score = zero
+            toward_sum = zero
+            grads = []
+            for e in range(ens_count):
+                toward = sign(x[e], y)
+                toward_sum = toward_sum + toward
+                pull = toward + pull_scale * sums[e]
+                score = score + wide[e][piece] * pull
+                grads.append(weight * pull)
+            pieces.append(grads)
+            score = (score - goal * toward_sum) * (1.0 / ens_count)
+            lane = lax.broadcasted_iota(jnp.int32, (8, LANES), 1) + (
+                (step + first) * width + lane_at
+            )
+            total[pl.ds(at + 8 * half, 8), :] += jnp.where(lane < lon_count, score, 0.0)
         for e in range(ens_count):
-            value = x[e].astype(jnp.float32)
-            toward = sums[e].astype(jnp.float32)
-            error = error + jnp.abs(value - goal)
-            spread = spread + value * toward
-            grad = (
-                weight * (sign(x[e], y).astype(jnp.float32) + pull_scale * toward)
-            ).astype(jnp.bfloat16)
-            grad_ref[e, pl.ds(at // sub_rows, rows // sub_rows), :, lanes] = grad.reshape(rows // sub_rows, sub_rows, LANES)
-        score = error * (1.0 / ens_count) + spread_scale * spread
-        lane = lax.broadcasted_iota(jnp.int32, (rows, LANES), 1) + ((step + first) * width + lane_at)
-        total[span, :] += jnp.where(lane < lon_count, score, 0.0)
+            whole_grad = jnp.concatenate([grads[e] for grads in pieces], axis=0)
+            grad_ref[
+                senders[e // per_part] * per_part + e % per_part,
+                pl.ds(at // sub_rows, rows // sub_rows), :, lanes,
+            ] = whole_grad.astype(jnp.bfloat16).reshape(rows // sub_rows, sub_rows, LANES)
 
     whole = row_count // 16
     for lane_at in range(0, width, LANES):
@@ -482,24 +506,28 @@
 
     @pl.when(step == pl.num_programs(0) - 1)
     def _():
-        score_ref[...] = jnp.sum(total[...], axis=1, keepdims=True) * (1.0 / lon_count)
-
-
-def grid_scores(members, target, weights, fairness, lon_count, sub_rows, at, earlier=None):
-    ens_count, row_count, span = members.shape
+        result = jnp.sum(total[...], axis=1, keepdims=True) * (1.0 / lon_count)
+        score_ref[...] = result + carried[1][...] if carried else result
+
+
+def grid_scores(parts, target, weights, fairness, sub_rows, blocks, earlier=()):
+    per_part, row_count, lon_count = parts[0].shape
+    ens_count = per_part * len(parts)
     var_count = row_count // sub_rows
-    width = 2 * LANES
-    first = at // width
-    carried = () if earlier is None else (earlier,)
+    width = GRID_WIDTH
+    first, last = blocks
     return pl.pallas_call(
-        functools.partial(grid_kernel, fairness, lon_count, first),
-        grid=(-(-span // width),),
+        functools.partial(grid_kernel, fairness, lon_count, first, len(parts)),
+        grid=(last - first,),
         in_specs=[
             pl.BlockSpec(memory_space=pltpu.SMEM),
-            pl.BlockSpec((ens_count, row_count, width), lambda i: (0, 0, i)),
-            pl.BlockSpec((row_count, width), lambda i: (0, i)),
+            pl.BlockSpec((row_count, width), lambda i: (0, i + first)),
         ]
-        + [pl.BlockSpec(memory_space=pl.ANY)] * len(carried),
+        + [pl.BlockSpec((per_part, row_count, width), lambda i: (0, 0, i + first))] * len(parts)
+        + [
+            pl.BlockSpec(memory_space=pl.ANY),
+            pl.BlockSpec((row_count, 1), lambda i: (0, 0)),
+        ][: len(earlier)],
         out_specs=[
             pl.BlockSpec((ens_count, var_count, sub_rows, width), lambda i: (0, 0, 0, i + first)),
             pl.BlockSpec((row_count, 1), lambda i: (0, 0)),
@@ -509,11 +537,11 @@
             jax.ShapeDtypeStruct((row_count, 1), jnp.float32),
         ],
         scratch_shapes=[pltpu.VMEM((row_count, LANES), jnp.float32)],
-        input_output_aliases={3: 0} if carried else {},
+        input_output_aliases={2 + len(parts): 0} if earlier else {},
         compiler_params=pltpu.CompilerParams(vmem_limit_bytes=56 * MIB),
         cost_estimate=pl.CostEstimate(flops=COST, bytes_accessed=COST, transcendentals=0),
         name="grid",
-    )(weights, members, target, *carried)
+    )(weights, target, *parts, *earlier)
 
 
 def local(ens, truth, legendre, orders):
@@ -522,49 +550,36 @@
     deg_count = legendre.shape[2]
     space_count = lax.axis_size("space")
     member_count = lax.axis_size("member")
-    space_index = lax.axis_index("space")
-    member_index = lax.axis_index("member")
     lat_count = band_rows * space_count
     ens_count = own_count * member_count
     sub_rows = band_rows // member_count
     fairness = 1.0 - FAIR_GAP / ens_count
 
     owners = ("space", "member")
-    sent, table = forward(ens, truth, legendre, orders, member_index, member_count)
+    sent, table = forward(ens, truth, legendre, orders, member_count)
     received = lax.all_to_all(sent, owners, split_axis=0, concat_axis=0, tiled=True)
 
-    spans = ((0, HALF), (HALF, lon_count))
-    halves = [regroup(ens, truth, member_index, member_count, span) for span in spans]
-    early, late = (half[0] for half in halves)
-    received, early, late = lax.optimization_barrier((received, early, late))
-
-    def exchange(half):
-        return lax.all_to_all(half, "member", split_axis=0, concat_axis=0, tiled=True).reshape(
-            ens_count, var_count * sub_rows, -1
-        )
-
-    early = exchange(early)
-    own_order = lax.dynamic_slice_in_dim(orders, space_index * member_count + member_index, 1, 0)
-    omega = jnp.where(own_order == 0, 1.0, 2.0).astype(jnp.float32)
-    grads, score = spectral(received, omega, fairness, member_count, var_count, deg_count)
-    grads, early, late = lax.optimization_barrier((grads, early, late))
-    late = exchange(late)
-    row_weights = lax.dynamic_slice_in_dim(
-        jnp.asarray(latitude_weights(lat_count)),
-        space_index * band_rows + member_index * sub_rows, sub_rows, 0,
+    *parts, target = regroup(ens, truth, member_count)
+    for place, hop in enumerate(HOPS):
+        if place:
+            parts[place] = lax.ppermute(parts[place], "member", hop_pairs(hop, member_count))
+
+    received, *parts[1:3] = lax.optimization_barrier((received, *parts[1:3]))
+    grads, score = spectral(received, orders, fairness, member_count, var_count, deg_count)
+    grads, *parts[3:] = lax.optimization_barrier((grads, *parts[3:]))
+    returned = lax.all_to_all(grads, owners, split_axis=0, concat_axis=0, tiled=True)
+    weights = jnp.asarray(latitude_weights(lat_count))
+    grid_args = (parts, target, weights, fairness, sub_rows)
+    early = grid_scores(*grid_args, (0, EARLY_BLOCKS))
+
+    returned, score, *early = lax.optimization_barrier((returned, score, *early))
+    spec_score = lax.all_to_all(score, "member", split_axis=0, concat_axis=0, tiled=True)
+    spec_score = spec_score.astype(jnp.float32)
+    grid_grad, grid_rows = grid_scores(
+        *grid_args, (EARLY_BLOCKS, -(-lon_count // GRID_WIDTH)), early
     )
-    grid_args = (row_weights, fairness, lon_count, sub_rows)
-    grid_grad, early_rows = grid_scores(early, halves[0][1], *grid_args, 0)
-    grads, grid_grad, late = lax.optimization_barrier((grads, grid_grad, late))
-    returned = lax.all_to_all(grads, owners, split_axis=0, concat_axis=0, tiled=True)
-    grid_grad, late_rows = grid_scores(late, halves[1][1], *grid_args, HALF, grid_grad)
     grid_grad = grid_grad.reshape(ens_count, var_count, 1, sub_rows, lon_count)
-    grid_score = (early_rows + late_rows).reshape(var_count, 1, sub_rows)
-
-    returned, score, grid_grad = lax.optimization_barrier((returned, score, grid_grad))
-    copies = jnp.broadcast_to(score[None], (member_count,) + score.shape)
-    spec_score = lax.all_to_all(copies, "member", split_axis=0, concat_axis=0, tiled=True)
-    spec_score = spec_score.astype(jnp.float32)
+    grid_score = grid_rows.reshape(var_count, 1, sub_rows)
     spec_grad = backward(returned, table, own_count, var_count).reshape(ens.shape)
     return (grid_score, grid_grad, spec_score, spec_grad)
 

time: 139 us -> 129 us (0.928)
  waiting for transfers between devices: 41.6 us -> 34.4 us
  Pallas kernels: 58.4 us -> 56.5 us
  starting transfers between devices: 30.5 us -> 32.4 us
    ppermute x0 -> x7, waiting for transfers between devices: none -> 29 us  [local(): lax.ppermute(parts[place], 'member', hop_pairs(hop, member_count))]
    all_to_all x3 -> x1, waiting for transfers between devices: 28.8 us -> 0.01 us  [local(): lax.all_to_all(score, 'member', split_axis=0, concat_axis=0, tiled=True)]
    ppermute x0 -> x7, starting transfers between devices: none -> 12 us  [local(): lax.ppermute(parts[place], 'member', hop_pairs(hop, member_count))]
    all_to_all x3 -> x1, starting transfers between devices: 14.7 us -> 3.91 us  [local(): lax.all_to_all(score, 'member', split_axis=0, concat_axis=0, tiled=True)]
    all_to_all x1, waiting for transfers between devices: 7.67 us -> 0.01 us  [local(): lax.all_to_all(sent, owners, split_axis=0, concat_axis=0, tiled=True)]
    pallas_call x2 -> x1, Pallas kernels: 10.3 us -> 8.65 us  [regroup(): pl.pallas_call(functools.partial(regroup_kernel, var_count, sub_rows), gr...]
  transfers between devices with their start and end apart: 5 -> 10, of which waited for: 5 -> 4; matrix products, arithmetic and copies ran while one was open for 2% -> 1% of each run, Pallas kernels for 37% -> 38%
where the time goes in v3:
time: 129 us; the launch traced here: 127 us
  Pallas kernels  56.5 us (44%)
  waiting for transfers between devices  34.4 us (27%)
  starting transfers between devices  32.4 us (25%)
  local copies, waits for them, and re-layouts  2.76 us (2%)
    ppermute x7, waiting for transfers between devices, local(): lax.ppermute(parts[place], 'member', hop_pairs(hop, member_count))  29 us
    pallas_call x2, Pallas kernels, grid_scores(): pl.pallas_call(functools.partial(grid_kernel, fairness, lon_count, first,...  19.9 us
    pallas_call x1, Pallas kernels, spectral(): pl.pallas_call(functools.partial(spectral_kernel, fairness, member_count,...  14.8 us
    ppermute x7, starting transfers between devices, local(): lax.ppermute(parts[place], 'member', hop_pairs(hop, member_count))  12 us
    all_to_all x1, starting transfers between devices, local(): lax.all_to_all(sent, owners, split_axis=0, concat_axis=0, tiled=True)  11.1 us
    pallas_call x1, Pallas kernels, regroup(): pl.pallas_call(functools.partial(regroup_kernel, var_count, sub_rows), gr...  8.65 us
    pallas_call x1, Pallas kernels, forward(): pl.pallas_call(functools.partial(forward_kernel, var_count, deg_count), g...  7.87 us
    all_to_all x1, starting transfers between devices, local(): lax.all_to_all(grads, owners, split_axis=0, concat_axis=0, tiled=True)  5.37 us
  transfers between devices with their start and end apart: 10, of which 4 were waited for; matrix products, arithmetic and copies ran while one was open for 1% of the time, Pallas kernels for 38%

profile of v3, /device:TPU:0, one launch (start us, length us, event | category | flops | bytes accessed | tf_op | source)
XLA Modules:
  0.0 127.0 jit_solution(1440595585019148895)
XLA Ops:
  0.6 7.9 %forward.1 = (bf16[128,16,256]{2,1,0:T(8,128)(2,1)}, bf16[1440,256]{1,0:T(8,128)(2,1)}) custom-call(s32[1,128]{1,0:T(1,128)} %bitcast.18, bf16[1152,1440]{1,0:T(8,128)(2,1)} %bitcast.10, bf16[36,16,1440]{2,1,0:T(8,128)(2,1)} %truth_ref.1, bf16[721,16,128]{2,1,0:T(8,128)(2,1)} %bitcast.16), custom_call_target="tpu_custom_call" | custom-call | flops 1024 | bytes 1024 | tf_op jit(solution)/shard_map/forward/pallas_call | solution.py:133
  8.5 11.1 %all-to-all-start = ((bf16[128,16,256]{2,1,0:T(8,128)(2,1)}), bf16[128,16,256]{2,1,0:T(8,128)(2,1)S(1)}, u32[]{:S(2)}, u32[]{:S(2)}) async-start(bf16[128,16,256]{2,1,0:T(8,128)(2,1)} %get-tuple-element.36), calls=%async_computation | async-start | bytes 2097152 | tf_op jit(solution)/shard_map/all_to_all | solution.py:560
  19.7 8.7 %regroup.1 = (bf16[2,72,1440]{2,1,0:T(8,128)(2,1)}, bf16[2,72,1440]{2,1,0:T(8,128)(2,1)}, bf16[2,72,1440]{2,1,0:T(8,128)(2,1)}, bf16[2,72,1440]{2,1,0:T(8,128)(2...) custom-call(bf16[1152,1440]{1,0:T(8,128)(2,1)} %bitcast.11, ...), custom_call_target="tpu_custom_call" | custom-call | flops 1024 | bytes 1024 | tf_op jit(solution)/shard_map/regroup/pallas_call | solution.py:407
  28.3 1.0 collective-permute-start
  29.3 2.3 %collective-permute-start.1 = (bf16[2,72,1440]{2,1,0:T(8,128)(2,1)}, bf16[2,72,1440]{2,1,0:T(8,128)(2,1)S(1)}, u32[]{:S(2)}, u32[]{:S(2)}) collective-permute-start(bf16[2,72,1440]{2,1,0:T(8,128)(2,1)} %get-tuple-element.38), channel_id=1, source_target_pairs={{0,48},{16,0},{32,16},{48,32},{64,112},{80,64},{96,80},{112,96},{1... | collective-permute-start | bytes 1244168 | tf_op jit(solution)/shard_map/ppermute | solution.py:565
  31.6 2.9 %collective-permute-start.2 = (bf16[2,72,1440]{2,1,0:T(8,128)(2,1)}, bf16[2,72,1440]{2,1,0:T(8,128)(2,1)S(1)}, u32[]{:S(2)}, u32[]{:S(2)}) collective-permute-start(bf16[2,72,1440]{2,1,0:T(8,128)(2,1)} %get-tuple-element.43), channel_id=1, source_target_pairs={{0,64},{16,80},{32,96},{48,112},{64,0},{80,16},{96,32},{112,48},{1... | collective-permute-start | bytes 1244168 | tf_op jit(solution)/shard_map/ppermute | solution.py:565
  34.5 1.8 %collective-permute-start.3 = (bf16[2,72,1440]{2,1,0:T(8,128)(2,1)}, bf16[2,72,1440]{2,1,0:T(8,128)(2,1)S(1)}, u32[]{:S(2)}, u32[]{:S(2)}) collective-permute-start(bf16[2,72,1440]{2,1,0:T(8,128)(2,1)} %get-tuple-element.44), channel_id=1, source_target_pairs={{0,32},{16,48},{32,0},{48,16},{64,96},{80,112},{96,64},{112,80},{1... | collective-permute-start | bytes 1244168 | tf_op jit(solution)/shard_map/ppermute | solution.py:565
  36.2 0.2 collective-permute-start.4
  36.4 16.0 %collective-permute-done.rest_1_ = bf16[2,72,1440]{2,1,0:T(8,128)(2,1)S(1)} collective-permute-done((bf16[2,72,1440]{2,1,0:T(8,128)(2,1)}, bf16[2,72,1440]{2,1,0:T(8,128)(2,1)S(1)}, u32[]{:S(2)}, u32[]{:S(2)}) %collective-permute-start) | collective-permute-done | bytes 414752 | tf_op jit(solution)/shard_map/ppermute | solution.py:565
  52.5 0.0 copy-start.2
  52.5 0.0 collective-permute-start.5
  52.5 0.0 collective-permute-done.1.rest_2_
  52.5 0.0 copy-start.3
  52.5 3.9 %collective-permute-start.6 = (bf16[2,72,1440]{2,1,0:T(8,128)(2,1)}, bf16[2,72,1440]{2,1,0:T(8,128)(2,1)}, u32[]{:S(2)}, u32[]{:S(2)}) collective-permute-start(bf16[2,72,1440]{2,1,0:T(8,128)(2,1)} %get-tuple-element.47), channel_id=1, source_target_pairs={{0,96},{16,112},{32,64},{48,80},{64,32},{80,48},{96,0},{112,16},{1... | collective-permute-start | bytes 1244168 | tf_op jit(solution)/shard_map/ppermute | solution.py:565
  56.4 0.0 all-to-all-done
  56.4 0.0 copy-start
  56.4 1.0 copy-done
  57.3 14.8 %spectral.1 = (bf16[16,8,8,384]{3,2,1,0:T(8,128)(2,1)}, bf16[8,36,721]{2,1,0:T(8,128)(2,1)}) custom-call(s32[128]{0:T(128)} %orders_ref.1, bf16[16,8,16,256]{3,2,1,0:T(8,128)(2,1)} %bitcast.13), custom_call_target="tpu_custom_call" | custom-call | flops 1024 | bytes 1024 | tf_op jit(solution)/shard_map/spectral/pallas_call | solution.py:275
  72.2 0.0 collective-permute-done.2.rest_3_
  72.2 0.0 copy-start.4
  72.2 0.0 collective-permute-done.3.rest_4_
  72.2 0.0 copy-start.5
  72.2 0.0 collective-permute-done.4.rest_5_
  72.2 0.0 copy-start.6
  72.2 5.4 %collective-permute-done.5.rest_6_ = bf16[2,72,1440]{2,1,0:T(8,128)(2,1)} collective-permute-done((bf16[2,72,1440]{2,1,0:T(8,128)(2,1)}, bf16[2,72,1440]{2,1,0:T(8,128)(2,1)}, u32[]{:S(2)}, u32[]{:S(2)}) %collective-permute-start.5) | collective-permute-done | bytes 414752 | tf_op jit(solution)/shard_map/ppermute | solution.py:565
  77.6 7.5 %collective-permute-done.6.rest_7_ = bf16[2,72,1440]{2,1,0:T(8,128)(2,1)} collective-permute-done((bf16[2,72,1440]{2,1,0:T(8,128)(2,1)}, bf16[2,72,1440]{2,1,0:T(8,128)(2,1)}, u32[]{:S(2)}, u32[]{:S(2)}) %collective-permute-start.6) | collective-permute-done | bytes 414752 | tf_op jit(solution)/shard_map/ppermute | solution.py:565
  85.2 5.4 %all-to-all-start.1 = ((bf16[128,8,384]{2,1,0:T(8,128)(2,1)}), bf16[128,8,384]{2,1,0:T(8,128)(2,1)S(1)}, u32[]{:S(2)}, u32[]{:S(2)}) async-start(bf16[128,8,384]{2,1,0:T(8,128)(2,1)} %bitcast.17), calls=%async_computation.1 | async-start | bytes 1572864 | tf_op jit(solution)/shard_map/all_to_all | solution.py:570
  90.6 0.0 copy-done.2
  90.6 0.0 copy-done.3
  90.6 0.0 copy-done.4
  90.6 0.0 copy-done.5
  90.6 0.0 copy-done.6
  90.6 9.9 %grid.2 = (bf16[16,36,2,1440]{3,2,1,0:T(2,128)(2,1)}, f32[72,1]{1,0:T(8,128)}) custom-call(f32[256]{0:T(256)} %constant.2.clone.weight_ref, bf16[72,1440]{1,0:T(8,128)(2,1)} %get-tuple-element.34.truth_ref, bf16[2,72,1440]{2,1,0:T(8,128)(2,1)} %get-tuple-element.35.rest_0_, bf16[2,72,1440]{2,1,0:T(8,128)(2,1)} %copy-done.2, bf16[2,72,1440]{2,1,0:T(8,128)(2,1)} %copy-done.3, ...), custom_call_target="tpu_custom_call" | custom-call | flops 1024 | bytes 1024 | tf_op jit(solution)/shard_map/grid/pallas_call | solution.py:519
  100.6 5.4 %all-to-all-done.1.in_ref = bf16[128,8,384]{2,1,0:T(8,128)(2,1)S(1)} async-done(((bf16[128,8,384]{2,1,0:T(8,128)(2,1)}), bf16[128,8,384]{2,1,0:T(8,128)(2,1)S(1)}, u32[]{:S(2)}, u32[]{:S(2)}) %all-to-all-start.1) | async-done | bytes 786464 | tf_op jit(solution)/shard_map/all_to_all | solution.py:570
  105.9 0.0 copy-start.1
  105.9 3.9 %all-to-all-start.2 = ((bf16[8,36,721]{2,1,0:T(8,128)(2,1)}), bf16[8,36,721]{2,1,0:T(8,128)(2,1)S(1)}, u32[]{:S(2)}, u32[]{:S(2)}) async-start(bf16[8,36,721]{2,1,0:T(8,128)(2,1)} %get-tuple-element.61), calls=%async_computation.2 | async-start | bytes 983040 | tf_op jit(solution)/shard_map/all_to_all | solution.py:576
  109.8 9.9 %grid.3 = (bf16[16,36,2,1440]{3,2,1,0:T(2,128)(2,1)}, f32[72,1]{1,0:T(8,128)}) custom-call(f32[256]{0:T(256)} %constant.2.clone.weight_ref, bf16[72,1440]{1,0:T(8,128)(2,1)} %get-tuple-element.34.truth_ref, bf16[2,72,1440]{2,1,0:T(8,128)(2,1)} %get-tuple-element.35.rest_0_, bf16[2,72,1440]{2,1,0:T(8,128)(2,1)} %copy-done.2, ...), custom_call_target="tpu_custom_call", output_to_operand_aliasing={{0}: (10, {})} | custom-call | flops 1024 | bytes 1024 | tf_op jit(solution)/shard_map/grid/pallas_call | solution.py:519
  119.8 0.0 copy-done.1
  119.8 0.0 copy-start.7
  119.8 5.3 %backward.1 = bf16[1152,1440]{1,0:T(8,128)(2,1)} custom-call(bf16[128,8,384]{2,1,0:T(8,128)(2,1)} %copy-done.1, bf16[1440,256]{1,0:T(8,128)(2,1)} %get-tuple-element.63.table_ref), custom_call_target="tpu_custom_call" | custom-call | flops 1024 | bytes 1024 | tf_op jit(solution)/shard_map/backward/pallas_call | solution.py:346
  125.1 0.0 copy-done.7
  125.1 0.1 reduce
  125.2 0.1 reshape.38
  125.3 0.6 copy.13
  126.0 0.0 all-to-all-done.2
  126.0 1.0 copy.15
Async XLA Ops:
  8.5 47.9 %all-to-all-start = ((bf16[128,16,256]{2,1,0:T(8,128)(2,1)}), bf16[128,16,256]{2,1,0:T(8,128)(2,1)S(1)}, u32[]{:S(2)}, u32[]{:S(2)}) async-start(bf16[128,16,256]{2,1,0:T(8,128)(2,1)} %get-tuple-element.36), calls=%async_computation | async-start | bytes 2097152 | tf_op jit(solution)/shard_map/all_to_all | solution.py:560
  28.3 24.2 %collective-permute-start = (bf16[2,72,1440]{2,1,0:T(8,128)(2,1)}, bf16[2,72,1440]{2,1,0:T(8,128)(2,1)S(1)}, u32[]{:S(2)}, u32[]{:S(2)}) collective-permute-start(bf16[2,72,1440]{2,1,0:T(8,128)(2,1)} %get-tuple-element.37), channel_id=1, source_target_pairs={{0,16},{16,32},{32,48},{48,0},{64,80},{80,96},{96,112},{112,64},{1... | collective-permute-start | bytes 1244168 | tf_op jit(solution)/shard_map/ppermute | solution.py:565
  29.3 23.1 %collective-permute-start.1 = (bf16[2,72,1440]{2,1,0:T(8,128)(2,1)}, bf16[2,72,1440]{2,1,0:T(8,128)(2,1)S(1)}, u32[]{:S(2)}, u32[]{:S(2)}) collective-permute-start(bf16[2,72,1440]{2,1,0:T(8,128)(2,1)} %get-tuple-element.38), channel_id=1, source_target_pairs={{0,48},{16,0},{32,16},{48,32},{64,112},{80,64},{96,80},{112,96},{1... | collective-permute-start | bytes 1244168 | tf_op jit(solution)/shard_map/ppermute | solution.py:565
  31.6 40.5 %collective-permute-start.2 = (bf16[2,72,1440]{2,1,0:T(8,128)(2,1)}, bf16[2,72,1440]{2,1,0:T(8,128)(2,1)S(1)}, u32[]{:S(2)}, u32[]{:S(2)}) collective-permute-start(bf16[2,72,1440]{2,1,0:T(8,128)(2,1)} %get-tuple-element.43), channel_id=1, source_target_pairs={{0,64},{16,80},{32,96},{48,112},{64,0},{80,16},{96,32},{112,48},{1... | collective-permute-start | bytes 1244168 | tf_op jit(solution)/shard_map/ppermute | solution.py:565
  34.5 37.7 %collective-permute-start.3 = (bf16[2,72,1440]{2,1,0:T(8,128)(2,1)}, bf16[2,72,1440]{2,1,0:T(8,128)(2,1)S(1)}, u32[]{:S(2)}, u32[]{:S(2)}) collective-permute-start(bf16[2,72,1440]{2,1,0:T(8,128)(2,1)} %get-tuple-element.44), channel_id=1, source_target_pairs={{0,32},{16,48},{32,0},{48,16},{64,96},{80,112},{96,64},{112,80},{1... | collective-permute-start | bytes 1244168 | tf_op jit(solution)/shard_map/ppermute | solution.py:565
  36.2 35.9 %collective-permute-start.4 = (bf16[2,72,1440]{2,1,0:T(8,128)(2,1)}, bf16[2,72,1440]{2,1,0:T(8,128)(2,1)S(1)}, u32[]{:S(2)}, u32[]{:S(2)}) collective-permute-start(bf16[2,72,1440]{2,1,0:T(8,128)(2,1)} %get-tuple-element.45), channel_id=1, source_target_pairs={{0,80},{16,96},{32,112},{48,64},{64,16},{80,32},{96,48},{112,0},{1... | collective-permute-start | bytes 1244168 | tf_op jit(solution)/shard_map/ppermute | solution.py:565
  52.5 38.1 %copy-start.2 = (bf16[2,72,1440]{2,1,0:T(8,128)(2,1)}, bf16[2,72,1440]{2,1,0:T(8,128)(2,1)S(1)}, u32[]{:S(2)}) copy-start(bf16[2,72,1440]{2,1,0:T(8,128)(2,1)S(1)} %collective-permute-done.rest_1_) | copy-start | bytes 1244164
  52.5 25.2 %collective-permute-start.5 = (bf16[2,72,1440]{2,1,0:T(8,128)(2,1)}, bf16[2,72,1440]{2,1,0:T(8,128)(2,1)}, u32[]{:S(2)}, u32[]{:S(2)}) collective-permute-start(bf16[2,72,1440]{2,1,0:T(8,128)(2,1)} %get-tuple-element.46), channel_id=1, source_target_pairs={{0,112},{16,64},{32,80},{48,96},{64,48},{80,0},{96,16},{112,32},{1... | collective-permute-start | bytes 1244168 | tf_op jit(solution)/shard_map/ppermute | solution.py:565
  52.5 38.1 %copy-start.3 = (bf16[2,72,1440]{2,1,0:T(8,128)(2,1)}, bf16[2,72,1440]{2,1,0:T(8,128)(2,1)S(1)}, u32[]{:S(2)}) copy-start(bf16[2,72,1440]{2,1,0:T(8,128)(2,1)S(1)} %collective-permute-done.1.rest_2_) | copy-start | bytes 1244164
  52.5 32.7 %collective-permute-start.6 = (bf16[2,72,1440]{2,1,0:T(8,128)(2,1)}, bf16[2,72,1440]{2,1,0:T(8,128)(2,1)}, u32[]{:S(2)}, u32[]{:S(2)}) collective-permute-start(bf16[2,72,1440]{2,1,0:T(8,128)(2,1)} %get-tuple-element.47), channel_id=1, source_target_pairs={{0,96},{16,112},{32,64},{48,80},{64,32},{80,48},{96,0},{112,16},{1... | collective-permute-start | bytes 1244168 | tf_op jit(solution)/shard_map/ppermute | solution.py:565
  56.4 1.0 copy-start
  72.2 18.4 %copy-start.4 = (bf16[2,72,1440]{2,1,0:T(8,128)(2,1)}, bf16[2,72,1440]{2,1,0:T(8,128)(2,1)S(1)}, u32[]{:S(2)}) copy-start(bf16[2,72,1440]{2,1,0:T(8,128)(2,1)S(1)} %collective-permute-done.2.rest_3_) | copy-start | bytes 1244164
  72.2 18.4 %copy-start.5 = (bf16[2,72,1440]{2,1,0:T(8,128)(2,1)}, bf16[2,72,1440]{2,1,0:T(8,128)(2,1)S(1)}, u32[]{:S(2)}) copy-start(bf16[2,72,1440]{2,1,0:T(8,128)(2,1)S(1)} %collective-permute-done.3.rest_4_) | copy-start | bytes 1244164
  72.2 18.4 %copy-start.6 = (bf16[2,72,1440]{2,1,0:T(8,128)(2,1)}, bf16[2,72,1440]{2,1,0:T(8,128)(2,1)S(1)}, u32[]{:S(2)}) copy-start(bf16[2,72,1440]{2,1,0:T(8,128)(2,1)S(1)} %collective-permute-done.4.rest_5_) | copy-start | bytes 1244164
  85.2 20.7 %all-to-all-start.1 = ((bf16[128,8,384]{2,1,0:T(8,128)(2,1)}), bf16[128,8,384]{2,1,0:T(8,128)(2,1)S(1)}, u32[]{:S(2)}, u32[]{:S(2)}) async-start(bf16[128,8,384]{2,1,0:T(8,128)(2,1)} %bitcast.17), calls=%async_computation.1 | async-start | bytes 1572864 | tf_op jit(solution)/shard_map/all_to_all | solution.py:570
  105.9 13.8 %copy-start.1 = (bf16[128,8,384]{2,1,0:T(8,128)(2,1)}, bf16[128,8,384]{2,1,0:T(8,128)(2,1)S(1)}, u32[]{:S(2)}) copy-start(bf16[128,8,384]{2,1,0:T(8,128)(2,1)S(1)} %all-to-all-done.1.in_ref) | copy-start | bytes 2359300
  105.9 20.0 %all-to-all-start.2 = ((bf16[8,36,721]{2,1,0:T(8,128)(2,1)}), bf16[8,36,721]{2,1,0:T(8,128)(2,1)S(1)}, u32[]{:S(2)}, u32[]{:S(2)}) async-start(bf16[8,36,721]{2,1,0:T(8,128)(2,1)} %get-tuple-element.61), calls=%async_computation.2 | async-start | bytes 983040 | tf_op jit(solution)/shard_map/all_to_all | solution.py:576
  119.8 5.3 %copy-start.7 = (f32[72,1]{1,0:T(8,128)S(1)}, f32[72,1]{1,0:T(8,128)}, u32[]{:S(2)}) copy-start(f32[72,1]{1,0:T(8,128)} %get-tuple-element.59) | copy-start | bytes 868

commit v4 on v3

--- a/solution.py
+++ b/solution.py
@@ -16,7 +16,8 @@
 BAND = 16
 LANES = 128
 GRID_WIDTH = 2 * LANES
-EARLY_BLOCKS = 3
+EARLY_PARTS = 5
+FIELD_COPIES = 2
 ROW_PAD = 40
 
 
@@ -63,11 +64,10 @@
 
 def forward_kernel(
     var_count, deg_count, orders_ref, ens_ref, truth_ref, leg_ref, out_ref, table_ref,
-    staged, swapped, truth_part, leg_part, sems,
+    staged, swapped, fields, truth_part, leg_part, sems,
 ):
-    step = pl.program_id(0)
     own_rows = 2 * var_count * BAND
-    block = ens_ref.shape[0]
+    block = own_rows // FIELD_COPIES
     deg_part = leg_part.shape[0]
     var_part = truth_part.shape[0]
     leg_at = 2 * own_rows
@@ -76,49 +76,57 @@
     used = truth_at + 2 * truth_rows
     order_count = orders_ref.shape[1]
 
-    @pl.when(step == 0)
-    def _():
-        member = lax.axis_index("member")
-        var_start = jnp.minimum(member * var_part, var_count - var_part)
-        deg_start = jnp.minimum(member * deg_part, deg_count - deg_part)
-        truth_copy = pltpu.make_async_copy(
-            truth_ref.at[pl.ds(var_start, var_part)], truth_part, sems.at[0]
-        )
-        leg_copy = pltpu.make_async_copy(
-            leg_ref.at[pl.ds(deg_start, deg_part)], leg_part, sems.at[1]
-        )
-        truth_copy.start()
-        leg_copy.start()
-        write_table(orders_ref, table_ref)
-        staged[used:, :] = jnp.zeros((staged.shape[0] - used, order_count), jnp.float32)
-        truth_copy.wait()
+    member = lax.axis_index("member")
+    var_start = jnp.minimum(member * var_part, var_count - var_part)
+    deg_start = jnp.minimum(member * deg_part, deg_count - deg_part)
+    truth_copy = pltpu.make_async_copy(
+        truth_ref.at[pl.ds(var_start, var_part)], truth_part, sems.at[0]
+    )
+    leg_copy = pltpu.make_async_copy(
+        leg_ref.at[pl.ds(deg_start, deg_part)], leg_part, sems.at[1]
+    )
+    copies = [
+        pltpu.make_async_copy(
+            ens_ref.at[pl.ds(part * block, block)], fields.at[pl.ds(part * block, block)],
+            sems.at[2 + part],
+        )
+        for part in range(FIELD_COPIES)
+    ]
+    truth_copy.start()
+    for copy in copies:
+        copy.start()
+    leg_copy.start()
+    write_table(orders_ref, table_ref)
+    staged[used:, :] = jnp.zeros((staged.shape[0] - used, order_count), jnp.float32)
+    truth_copy.wait()
+    rows = jnp.dot(
+        truth_part[...].reshape(truth_rows, -1), table_ref[...],
+        preferred_element_type=jnp.float32,
+    )
+    staged[truth_at : truth_at + truth_rows, :] = rows[:, :order_count]
+    staged[truth_at + truth_rows : used, :] = rows[:, order_count:]
+    for part, copy in enumerate(copies):
+        copy.wait()
+        at = part * block
         rows = jnp.dot(
-            truth_part[...].reshape(truth_rows, -1), table_ref[...],
-            preferred_element_type=jnp.float32,
-        )
-        staged[truth_at : truth_at + truth_rows, :] = rows[:, :order_count]
-        staged[truth_at + truth_rows : used, :] = rows[:, order_count:]
-        leg_copy.wait()
-        staged[leg_at:truth_at, :] = (
-            leg_part[...].reshape(deg_part * BAND, order_count).astype(jnp.float32)
-        )
-
-    rows = jnp.dot(ens_ref[...], table_ref[...], preferred_element_type=jnp.float32)
-    at = pl.multiple_of(step * block, block)
-    staged[pl.ds(at, block), :] = rows[:, :order_count]
-    staged[pl.ds(own_rows + at, block), :] = rows[:, order_count:]
-
-    @pl.when(step == pl.num_programs(0) - 1)
-    def _():
-        width = staged.shape[0] // BAND
-        for row in range(BAND):
-            piece = staged[pl.ds(row, width, stride=BAND), :]
-            swapped[0, pl.ds(row, order_count, stride=BAND), :] = piece[:LANES].T
-            swapped[1, pl.ds(row, order_count, stride=BAND), :] = piece[LANES:].T
-        for part in range(2):
-            out_ref[:, :, part * LANES : (part + 1) * LANES] = (
-                swapped[part].reshape(order_count, BAND, LANES).astype(jnp.bfloat16)
-            )
+            fields[at : at + block, :], table_ref[...], preferred_element_type=jnp.float32
+        )
+        staged[at : at + block, :] = rows[:, :order_count]
+        staged[own_rows + at : own_rows + at + block, :] = rows[:, order_count:]
+    leg_copy.wait()
+    staged[leg_at:truth_at, :] = (
+        leg_part[...].reshape(deg_part * BAND, order_count).astype(jnp.float32)
+    )
+
+    width = staged.shape[0] // BAND
+    for row in range(BAND):
+        piece = staged[pl.ds(row, width, stride=BAND), :]
+        swapped[0, pl.ds(row, order_count, stride=BAND), :] = piece[:LANES].T
+        swapped[1, pl.ds(row, order_count, stride=BAND), :] = piece[LANES:].T
+    for part in range(2):
+        out_ref[:, :, part * LANES : (part + 1) * LANES] = (
+            swapped[part].reshape(order_count, BAND, LANES).astype(jnp.bfloat16)
+        )
 
 
 def forward(ens, truth, legendre, orders, member_count):
@@ -128,21 +136,11 @@
     deg_part = -(-deg_count // member_count)
     var_part = -(-var_count // member_count)
     rows = own_count * var_count * band_rows
-    steps = 4
     width = 2 * LANES
     return pl.pallas_call(
         functools.partial(forward_kernel, var_count, deg_count),
-        grid=(steps,),
-        in_specs=[
-            pl.BlockSpec((1, order_count), lambda i: (0, 0)),
-            pl.BlockSpec((rows // steps, lon_count), lambda i: (i, 0)),
-            pl.BlockSpec(memory_space=pl.ANY),
-            pl.BlockSpec(memory_space=pl.ANY),
-        ],
-        out_specs=[
-            pl.BlockSpec((order_count, band_rows, width), lambda i: (0, 0, 0)),
-            pl.BlockSpec((lon_count, 2 * order_count), lambda i: (0, 0)),
-        ],
+        in_specs=[pl.BlockSpec(memory_space=pltpu.VMEM)] + [pl.BlockSpec(memory_space=pl.ANY)] * 3,
+        out_specs=[pl.BlockSpec(memory_space=pltpu.VMEM)] * 2,
         out_shape=[
             jax.ShapeDtypeStruct((order_count, band_rows, width), jnp.bfloat16),
             jax.ShapeDtypeStruct((lon_count, 2 * order_count), jnp.bfloat16),
@@ -150,9 +148,10 @@
         scratch_shapes=[
             pltpu.VMEM((width * band_rows, order_count), jnp.float32),
             pltpu.VMEM((2, order_count * band_rows, LANES), jnp.float32),
+            pltpu.VMEM((rows, lon_count), jnp.bfloat16),
             pltpu.VMEM((var_part, band_rows, lon_count), jnp.bfloat16),
             pltpu.VMEM((deg_part, band_rows, order_count), jnp.bfloat16),
-            pltpu.SemaphoreType.DMA((2,)),
+            pltpu.SemaphoreType.DMA((2 + FIELD_COPIES,)),
         ],
         compiler_params=pltpu.CompilerParams(vmem_limit_bytes=56 * MIB),
         cost_estimate=pl.CostEstimate(flops=COST, bytes_accessed=COST, transcendentals=0),
@@ -292,7 +291,7 @@
             pltpu.VMEM((2 * ens_count * ROW_PAD, deg_pad), jnp.float32),
             pltpu.VMEM((ROW_PAD, deg_pad), jnp.float32),
         ],
-        compiler_params=pltpu.CompilerParams(vmem_limit_bytes=56 * MIB),
+        compiler_params=pltpu.CompilerParams(vmem_limit_bytes=28 * MIB),
         cost_estimate=pl.CostEstimate(flops=COST, bytes_accessed=COST, transcendentals=0),
         name="spectral",
     )(orders, received.reshape(space_count, member_count, band_rows, width))
@@ -342,7 +341,7 @@
     band_rows = 2 * half_rows
     lon_count = table.shape[0]
     rows = own_count * var_count * band_rows
-    steps = 4
+    steps = 2
     return pl.pallas_call(
         functools.partial(backward_kernel, var_count),
         grid=(steps,),
@@ -356,13 +355,13 @@
             pltpu.VMEM((3, order_count * half_rows, LANES), jnp.float32),
             pltpu.VMEM((2, rows, order_count), jnp.float32),
         ],
-        compiler_params=pltpu.CompilerParams(vmem_limit_bytes=56 * MIB),
+        compiler_params=pltpu.CompilerParams(vmem_limit_bytes=16 * MIB),
         cost_estimate=pl.CostEstimate(flops=COST, bytes_accessed=COST, transcendentals=0),
         name="backward",
     )(received, table)
 
 
-HOPS = ((0, 0), (0, 1), (0, 3), (1, 0), (0, 2), (1, 1), (1, 3), (1, 2))
+HOPS = ((0, 0), (0, 1), (0, 3), (1, 1), (1, 3), (1, 0), (0, 2), (1, 2))
 RING = 4
 
 
@@ -428,8 +427,69 @@
     )(ens.reshape(-1, lon_count), truth.reshape(-1, lon_count))
 
 
-def grid_kernel(fairness, lon_count, first, part_count, weight_ref, truth_ref, *rest):
-    parts, carried = rest[:part_count], rest[part_count:-3]
+def sign(a, b):
+    return jnp.minimum(jnp.maximum((a - b) * 2.0**70, -1.0), 1.0)
+
+
+def count_kernel(*refs):
+    parts, sum_ref = refs[:-1], refs[-1]
+    per_part, row_count, width = parts[0].shape
+    count = per_part * len(parts)
+
+    def tile(at, rows, lane_at):
+        lanes = slice(lane_at, lane_at + LANES)
+        span = pl.ds(at, rows)
+        wide = [
+            parts[e // per_part][e % per_part, span, lanes].astype(jnp.float32) * 2.0**64
+            for e in range(count)
+        ]
+        pieces = []
+        for half in range(rows // 8):
+            x = [value[8 * half : 8 * half + 8] for value in wide]
+            sums = [jnp.zeros((8, LANES), jnp.float32)] * count
+            for i in range(count):
+                for j in range(i + 1, count):
+                    s = sign(x[i], x[j])
+                    sums[i] = sums[i] + s
+                    sums[j] = sums[j] - s
+            pieces.append(sums)
+        for e in range(count):
+            whole_sum = jnp.concatenate([sums[e] for sums in pieces], axis=0)
+            sum_ref[e, span, lanes] = whole_sum.astype(jnp.bfloat16)
+
+    over_tiles(tile, row_count, width)
+
+
+def over_tiles(tile, row_count, width):
+    whole = row_count // 16
+    for lane_at in range(0, width, LANES):
+        def body(index, _, lane_at=lane_at):
+            tile(pl.multiple_of(index * 16, 16), 16, lane_at)
+            return 0
+
+        lax.fori_loop(0, whole, body, 0)
+        if row_count % 16:
+            tile(whole * 16, row_count % 16, lane_at)
+
+
+def count_signs(parts):
+    per_part, row_count, lon_count = parts[0].shape
+    count = per_part * len(parts)
+    width = GRID_WIDTH
+    return pl.pallas_call(
+        count_kernel,
+        grid=(-(-lon_count // width),),
+        in_specs=[pl.BlockSpec((per_part, row_count, width), lambda i: (0, 0, i))] * len(parts),
+        out_specs=pl.BlockSpec((count, row_count, width), lambda i: (0, 0, i)),
+        out_shape=jax.ShapeDtypeStruct((count, row_count, lon_count), jnp.bfloat16),
+        compiler_params=pltpu.CompilerParams(vmem_limit_bytes=56 * MIB),
+        cost_estimate=pl.CostEstimate(flops=COST, bytes_accessed=COST, transcendentals=0),
+        name="count",
+    )(*parts)
+
+
+def grid_kernel(fairness, lon_count, first, part_count, known, weight_ref, truth_ref, *rest):
+    parts, known_ref, carried = rest[:part_count], rest[part_count], rest[part_count + 1 : -3]
     grad_ref, score_ref, total = rest[-3:]
     step = pl.program_id(0)
     per_part, row_count, width = parts[0].shape
@@ -448,9 +508,6 @@
     def _():
         total[...] = jnp.zeros_like(total)
 
-    def sign(a, b):
-        return jnp.minimum(jnp.maximum((a - b) * 2.0**70, -1.0), 1.0)
-
     def tile(at, rows, lane_at):
         lanes = slice(lane_at, lane_at + LANES)
         span = pl.ds(at, rows)
@@ -459,6 +516,7 @@
             for e in range(ens_count)
         ]
         goals = truth_ref[span, lanes].astype(jnp.float32)
+        before = [known_ref[e, span, lanes].astype(jnp.float32) for e in range(known)]
         pieces = []
         for half in range(rows // 8):
             piece = slice(8 * half, 8 * half + 8)
@@ -466,9 +524,9 @@
             goal = goals[piece]
             y = goal * 2.0**64
             zero = jnp.zeros((8, LANES), jnp.float32)
-            sums = [zero] * ens_count
+            sums = [value[piece] for value in before] + [zero] * (ens_count - known)
             for i in range(ens_count):
-                for j in range(i + 1, ens_count):
+                for j in range(max(i + 1, known), ens_count):
                     s = sign(x[i], x[j])
                     sums[i] = sums[i] + s
                     sums[j] = sums[j] - s
@@ -494,54 +552,49 @@
                 pl.ds(at // sub_rows, rows // sub_rows), :, lanes,
             ] = whole_grad.astype(jnp.bfloat16).reshape(rows // sub_rows, sub_rows, LANES)
 
-    whole = row_count // 16
-    for lane_at in range(0, width, LANES):
-        def body(index, _, lane_at=lane_at):
-            tile(pl.multiple_of(index * 16, 16), 16, lane_at)
-            return 0
-
-        lax.fori_loop(0, whole, body, 0)
-        if row_count % 16:
-            tile(whole * 16, row_count % 16, lane_at)
+    over_tiles(tile, row_count, width)
 
     @pl.when(step == pl.num_programs(0) - 1)
     def _():
-        result = jnp.sum(total[...], axis=1, keepdims=True) * (1.0 / lon_count)
-        score_ref[...] = result + carried[1][...] if carried else result
-
-
-def grid_scores(parts, target, weights, fairness, sub_rows, blocks, earlier=()):
+        for row in range(sub_rows):
+            rows = total[pl.ds(row, row_count // sub_rows, stride=sub_rows), :]
+            result = jnp.sum(rows.T, axis=0, keepdims=True) * (1.0 / lon_count)
+            score_ref[row : row + 1, :] = result + carried[1][row : row + 1, :] if carried else result
+
+
+def grid_scores(parts, signs, target, weights, fairness, sub_rows, blocks, earlier=()):
     per_part, row_count, lon_count = parts[0].shape
     ens_count = per_part * len(parts)
     var_count = row_count // sub_rows
     width = GRID_WIDTH
     first, last = blocks
     return pl.pallas_call(
-        functools.partial(grid_kernel, fairness, lon_count, first, len(parts)),
+        functools.partial(grid_kernel, fairness, lon_count, first, len(parts), signs.shape[0]),
         grid=(last - first,),
         in_specs=[
             pl.BlockSpec(memory_space=pltpu.SMEM),
             pl.BlockSpec((row_count, width), lambda i: (0, i + first)),
         ]
         + [pl.BlockSpec((per_part, row_count, width), lambda i: (0, 0, i + first))] * len(parts)
+        + [pl.BlockSpec((signs.shape[0], row_count, width), lambda i: (0, 0, i + first))]
         + [
             pl.BlockSpec(memory_space=pl.ANY),
-            pl.BlockSpec((row_count, 1), lambda i: (0, 0)),
+            pl.BlockSpec((sub_rows, var_count), lambda i: (0, 0)),
         ][: len(earlier)],
         out_specs=[
             pl.BlockSpec((ens_count, var_count, sub_rows, width), lambda i: (0, 0, 0, i + first)),
-            pl.BlockSpec((row_count, 1), lambda i: (0, 0)),
+            pl.BlockSpec((sub_rows, var_count), lambda i: (0, 0)),
         ],
         out_shape=[
             jax.ShapeDtypeStruct((ens_count, var_count, sub_rows, lon_count), jnp.bfloat16),
-            jax.ShapeDtypeStruct((row_count, 1), jnp.float32),
+            jax.ShapeDtypeStruct((sub_rows, var_count), jnp.float32),
         ],
         scratch_shapes=[pltpu.VMEM((row_count, LANES), jnp.float32)],
-        input_output_aliases={2 + len(parts): 0} if earlier else {},
+        input_output_aliases={3 + len(parts): 0} if earlier else {},
         compiler_params=pltpu.CompilerParams(vmem_limit_bytes=56 * MIB),
         cost_estimate=pl.CostEstimate(flops=COST, bytes_accessed=COST, transcendentals=0),
         name="grid",
-    )(weights, target, *parts, *earlier)
+    )(weights, target, *parts, signs, *earlier)
 
 
 def local(ens, truth, legendre, orders):
@@ -566,20 +619,18 @@
 
     received, *parts[1:3] = lax.optimization_barrier((received, *parts[1:3]))
     grads, score = spectral(received, orders, fairness, member_count, var_count, deg_count)
-    grads, *parts[3:] = lax.optimization_barrier((grads, *parts[3:]))
+    signs = count_signs(parts[:EARLY_PARTS])
+    spec_score = lax.all_to_all(score, "member", split_axis=0, concat_axis=0, tiled=True)
+    grads, spec_score, signs, *parts = lax.optimization_barrier(
+        (grads, spec_score, signs, *parts)
+    )
     returned = lax.all_to_all(grads, owners, split_axis=0, concat_axis=0, tiled=True)
+    spec_score = spec_score.astype(jnp.float32)
     weights = jnp.asarray(latitude_weights(lat_count))
-    grid_args = (parts, target, weights, fairness, sub_rows)
-    early = grid_scores(*grid_args, (0, EARLY_BLOCKS))
-
-    returned, score, *early = lax.optimization_barrier((returned, score, *early))
-    spec_score = lax.all_to_all(score, "member", split_axis=0, concat_axis=0, tiled=True)
-    spec_score = spec_score.astype(jnp.float32)
-    grid_grad, grid_rows = grid_scores(
-        *grid_args, (EARLY_BLOCKS, -(-lon_count // GRID_WIDTH)), early
-    )
+    grid_args = (parts, signs, target, weights, fairness, sub_rows)
+    grid_grad, grid_rows = grid_scores(*grid_args, (0, -(-lon_count // GRID_WIDTH)))
     grid_grad = grid_grad.reshape(ens_count, var_count, 1, sub_rows, lon_count)
-    grid_score = grid_rows.reshape(var_count, 1, sub_rows)
+    grid_score = grid_rows.T.reshape(var_count, 1, sub_rows)
     spec_grad = backward(returned, table, own_count, var_count).reshape(ens.shape)
     return (grid_score, grid_grad, spec_score, spec_grad)
 

time: 129 us -> 114 us (0.88)
  waiting for transfers between devices: 34.4 us -> 16.9 us
  starting transfers between devices: 32.4 us -> 38.7 us
  Pallas kernels: 56.5 us -> 54.6 us
    ppermute x7, waiting for transfers between devices: 29 us -> 12.5 us  [local(): lax.ppermute(parts[place], 'member', hop_pairs(hop, member_count))]
    ppermute x7, starting transfers between devices: 12 us -> 18.2 us  [local(): lax.ppermute(parts[place], 'member', hop_pairs(hop, member_count))]
    pallas_call x1 -> x2, Pallas kernels: 7.87 us -> 13.6 us  [the longest x1 6.84 us: count_signs(): pl.pallas_call(count_kernel, grid=(-(-lon_count // width),), in_specs=[pl...]
    all_to_all x1, waiting for transfers between devices: 5.37 us -> 0.01 us  [local(): lax.all_to_all(grads, owners, split_axis=0, concat_axis=0, tiled=True)]
    pallas_call x2 -> x1, Pallas kernels: 19.9 us -> 15 us  [grid_scores(): pl.pallas_call(functools.partial(grid_kernel, fairness, lon_count, first,...]
    all_to_all x1, waiting for transfers between devices: 0.01 us -> 4.4 us  [local(): lax.all_to_all(score, 'member', split_axis=0, concat_axis=0, tiled=True)]
    pallas_call x1, Pallas kernels: 5.28 us -> 3.32 us  [backward(): pl.pallas_call(functools.partial(backward_kernel, var_count), grid=(steps...]
    unnamed x18 -> x15, local copies, waits for them, and re-layouts: 2.65 us -> 1.91 us
  transfers between devices with their start and end apart: 10 -> 10, of which waited for: 4 -> 3; matrix products, arithmetic and copies ran while one was open for 1% -> 1% of each run, Pallas kernels for 38% -> 39%
where the time goes in v4:
time: 114 us; the launch traced here: 113 us
  Pallas kernels  54.6 us (48%)
  starting transfers between devices  38.7 us (34%)
  waiting for transfers between devices  16.9 us (15%)
  local copies, waits for them, and re-layouts  1.91 us (2%)
    ppermute x7, starting transfers between devices, local(): lax.ppermute(parts[place], 'member', hop_pairs(hop, member_count))  18.2 us
    pallas_call x1, Pallas kernels, grid_scores(): pl.pallas_call(functools.partial(grid_kernel, fairness, lon_count, first,...  15 us
    pallas_call x1, Pallas kernels, spectral(): pl.pallas_call(functools.partial(spectral_kernel, fairness, member_count,...  14.1 us
    ppermute x7, waiting for transfers between devices, local(): lax.ppermute(parts[place], 'member', hop_pairs(hop, member_count))  12.5 us
    all_to_all x1, starting transfers between devices, local(): lax.all_to_all(sent, owners, split_axis=0, concat_axis=0, tiled=True)  11.1 us
    pallas_call x1, Pallas kernels, regroup(): pl.pallas_call(functools.partial(regroup_kernel, var_count, sub_rows), gr...  8.65 us
    pallas_call x1, Pallas kernels, count_signs(): pl.pallas_call(count_kernel, grid=(-(-lon_count // width),), in_specs=[pl...  6.84 us
    pallas_call x1, Pallas kernels, forward(): pl.pallas_call(functools.partial(forward_kernel, var_count, deg_count), i...  6.76 us
  transfers between devices with their start and end apart: 10, of which 3 were waited for; matrix products, arithmetic and copies ran while one was open for 1% of the time, Pallas kernels for 39%

profile of v4, /device:TPU:0, one launch (start us, length us, event | category | flops | bytes accessed | tf_op | source)
XLA Modules:
  0.0 112.9 jit_solution(18261466752349166066)
XLA Ops:
  0.6 6.8 %forward.1 = (bf16[128,16,256]{2,1,0:T(8,128)(2,1)}, bf16[1440,256]{1,0:T(8,128)(2,1)}) custom-call(s32[1,128]{1,0:T(1,128)} %bitcast.14, bf16[1152,1440]{1,0:T(8,128)(2,1)} %bitcast.15, bf16[36,16,1440]{2,1,0:T(8,128)(2,1)} %truth_ref.1, bf16[721,16,128]{2,1,0:T(8,128)(2,1)} %bitcast.19), custom_call_target="tpu_custom_call" | custom-call | flops 1024 | bytes 1024 | tf_op jit(solution)/shard_map/forward/pallas_call | solution.py:140
  7.4 0.0 copy-start.1
  7.4 11.1 %all-to-all-start = ((bf16[128,16,256]{2,1,0:T(8,128)(2,1)}), bf16[128,16,256]{2,1,0:T(8,128)(2,1)S(1)}, u32[]{:S(2)}, u32[]{:S(2)}) async-start(bf16[128,16,256]{2,1,0:T(8,128)(2,1)} %get-tuple-element.34), calls=%async_computation | async-start | bytes 2097152 | tf_op jit(solution)/shard_map/all_to_all | solution.py:613
  18.6 8.7 %regroup.1 = (bf16[2,72,1440]{2,1,0:T(8,128)(2,1)}, bf16[2,72,1440]{2,1,0:T(8,128)(2,1)}, bf16[2,72,1440]{2,1,0:T(8,128)(2,1)}, bf16[2,72,1440]{2,1,0:T(8,128)(2...) custom-call(bf16[1152,1440]{1,0:T(8,128)(2,1)} %bitcast.16, ...), custom_call_target="tpu_custom_call" | custom-call | flops 1024 | bytes 1024 | tf_op jit(solution)/shard_map/regroup/pallas_call | solution.py:406
  27.2 1.0 collective-permute-start
  28.2 2.3 %collective-permute-start.1 = (bf16[2,72,1440]{2,1,0:T(8,128)(2,1)}, bf16[2,72,1440]{2,1,0:T(8,128)(2,1)S(1)}, u32[]{:S(2)}, u32[]{:S(2)}) collective-permute-start(bf16[2,72,1440]{2,1,0:T(8,128)(2,1)} %get-tuple-element.36), channel_id=1, source_target_pairs={{0,48},{16,0},{32,16},{48,32},{64,112},{80,64},{96,80},{112,96},{1... | collective-permute-start | bytes 1244168 | tf_op jit(solution)/shard_map/ppermute | solution.py:618
  30.5 2.6 %collective-permute-start.2 = (bf16[2,72,1440]{2,1,0:T(8,128)(2,1)}, bf16[2,72,1440]{2,1,0:T(8,128)(2,1)S(1)}, u32[]{:S(2)}, u32[]{:S(2)}) collective-permute-start(bf16[2,72,1440]{2,1,0:T(8,128)(2,1)} %get-tuple-element.43), channel_id=1, source_target_pairs={{0,80},{16,96},{32,112},{48,64},{64,16},{80,32},{96,48},{112,0},{1... | collective-permute-start | bytes 1244168 | tf_op jit(solution)/shard_map/ppermute | solution.py:618
  33.1 3.1 %collective-permute-start.3 = (bf16[2,72,1440]{2,1,0:T(8,128)(2,1)}, bf16[2,72,1440]{2,1,0:T(8,128)(2,1)S(1)}, u32[]{:S(2)}, u32[]{:S(2)}) collective-permute-start(bf16[2,72,1440]{2,1,0:T(8,128)(2,1)} %get-tuple-element.44), channel_id=1, source_target_pairs={{0,112},{16,64},{32,80},{48,96},{64,48},{80,0},{96,16},{112,32},{1... | collective-permute-start | bytes 1244168 | tf_op jit(solution)/shard_map/ppermute | solution.py:618
  36.2 2.9 %collective-permute-start.4 = (bf16[2,72,1440]{2,1,0:T(8,128)(2,1)}, bf16[2,72,1440]{2,1,0:T(8,128)(2,1)S(1)}, u32[]{:S(2)}, u32[]{:S(2)}) collective-permute-start(bf16[2,72,1440]{2,1,0:T(8,128)(2,1)} %get-tuple-element.45), channel_id=1, source_target_pairs={{0,64},{16,80},{32,96},{48,112},{64,0},{80,16},{96,32},{112,48},{1... | collective-permute-start | bytes 1244168 | tf_op jit(solution)/shard_map/ppermute | solution.py:618
  39.0 3.2 %collective-permute-done.refs_1_.rest_1_ = bf16[2,72,1440]{2,1,0:T(8,128)(2,1)S(1)} collective-permute-done((bf16[2,72,1440]{2,1,0:T(8,128)(2,1)}, bf16[2,72,1440]{2,1,0:T(8,128)(2,1)S(1)}, u32[]{:S(2)}, u32[]{:S(2)}) %collective-permute-start) | collective-permute-done | bytes 414752 | tf_op jit(solution)/shard_map/ppermute | solution.py:618
  42.3 0.0 copy-start.2
  42.3 0.8 collective-permute-start.5
  43.1 0.0 collective-permute-done.1.refs_2_.rest_2_
  43.1 0.0 copy-start.3
  43.1 5.5 %collective-permute-start.6 = (bf16[2,72,1440]{2,1,0:T(8,128)(2,1)}, bf16[2,72,1440]{2,1,0:T(8,128)(2,1)}, u32[]{:S(2)}, u32[]{:S(2)}) collective-permute-start(bf16[2,72,1440]{2,1,0:T(8,128)(2,1)} %get-tuple-element.47), channel_id=1, source_target_pairs={{0,96},{16,112},{32,64},{48,80},{64,32},{80,48},{96,0},{112,16},{1... | collective-permute-start | bytes 1244168 | tf_op jit(solution)/shard_map/ppermute | solution.py:618
  48.6 0.0 all-to-all-done
  48.6 0.0 copy-done.1
  48.6 14.1 %spectral.1 = (bf16[16,8,8,384]{3,2,1,0:T(8,128)(2,1)}, bf16[8,36,721]{2,1,0:T(8,128)(2,1)}) custom-call(s32[128]{0:T(128)S(1)} %copy-done.1, bf16[16,8,16,256]{3,2,1,0:T(8,128)(2,1)S(1)} %bitcast.13), custom_call_target="tpu_custom_call" | custom-call | flops 1024 | bytes 1024 | tf_op jit(solution)/shard_map/spectral/pallas_call | solution.py:274
  62.8 3.5 %all-to-all-start.1 = ((bf16[8,36,721]{2,1,0:T(8,128)(2,1)}), bf16[8,36,721]{2,1,0:T(8,128)(2,1)S(1)}, u32[]{:S(2)}, u32[]{:S(2)}) async-start(bf16[8,36,721]{2,1,0:T(8,128)(2,1)} %get-tuple-element.39), calls=%async_computation.1 | async-start | bytes 983040 | tf_op jit(solution)/shard_map/all_to_all | solution.py:623
  66.3 0.0 collective-permute-done.2.refs_3_.rest_3_
  66.3 0.0 copy-start.4
  66.3 0.0 collective-permute-done.3.refs_4_.rest_4_
  66.3 0.0 copy-start.5
  66.3 0.0 copy-done.2
  66.3 0.0 copy-done.3
  66.3 0.7 copy-done.4
  67.0 0.2 copy-done.5
  67.2 6.8 %count.1.rest_8_ = bf16[10,72,1440]{2,1,0:T(8,128)(2,1)} custom-call(bf16[2,72,1440]{2,1,0:T(8,128)(2,1)} %get-tuple-element.48.refs_0_.rest_0_, bf16[2,72,1440]{2,1,0:T(8,128)(2,1)} %copy-done.2, bf16[2,72,1440]{2,1,0:T(8,128)(2,1)} %copy-done.3, bf16[2,72,1440]{2,1,0:T(8,128)(2,1)} %copy-done.4, bf16[2,72,1440]{2,1,0:T(8,128)(2,1)} %copy-done.5), custom_call_target="tpu_custom_call" | custom-call | flops 1024 | bytes 1024 | tf_op jit(solution)/shard_map/count/pallas_call | solution.py:479
  74.0 0.0 collective-permute-done.4.rest_5_
  74.0 0.0 copy-start.6
  74.0 0.0 collective-permute-done.5.rest_6_
  74.1 9.2 %collective-permute-done.6.rest_7_ = bf16[2,72,1440]{2,1,0:T(8,128)(2,1)} collective-permute-done((bf16[2,72,1440]{2,1,0:T(8,128)(2,1)}, bf16[2,72,1440]{2,1,0:T(8,128)(2,1)}, u32[]{:S(2)}, u32[]{:S(2)}) %collective-permute-start.6) | collective-permute-done | bytes 414752 | tf_op jit(solution)/shard_map/ppermute | solution.py:618
  83.3 4.4 %all-to-all-done.1 = bf16[8,36,721]{2,1,0:T(8,128)(2,1)S(1)} async-done(((bf16[8,36,721]{2,1,0:T(8,128)(2,1)}), bf16[8,36,721]{2,1,0:T(8,128)(2,1)S(1)}, u32[]{:S(2)}, u32[]{:S(2)}) %all-to-all-start.1) | async-done | bytes 415328 | tf_op jit(solution)/shard_map/all_to_all | solution.py:623
  87.7 5.9 %all-to-all-start.2 = ((bf16[128,8,384]{2,1,0:T(8,128)(2,1)}), bf16[128,8,384]{2,1,0:T(8,128)(2,1)S(1)}, u32[]{:S(2)}, u32[]{:S(2)}) async-start(bf16[128,8,384]{2,1,0:T(8,128)(2,1)} %bitcast.5), calls=%async_computation.2 | async-start | bytes 1572864 | tf_op jit(solution)/shard_map/all_to_all | solution.py:627
  93.6 0.0 copy-done.6
  93.7 0.0 copy-start
  93.7 15.0 %grid.1 = (bf16[16,36,2,1440]{3,2,1,0:T(2,128)(2,1)}, f32[2,36]{1,0:T(2,128)}) custom-call(f32[256]{0:T(256)} %constant.2.clone.weight_ref, bf16[72,1440]{1,0:T(8,128)(2,1)} %get-tuple-element.33.truth_ref, bf16[2,72,1440]{2,1,0:T(8,128)(2,1)} %get-tuple-element.48.refs_0_.rest_0_, bf16[2,72,1440]{2,1,0:T(8,128)(2,1)} %copy-done.2, ...), custom_call_target="tpu_custom_call" | custom-call | flops 1024 | bytes 1024 | tf_op jit(solution)/shard_map/grid/pallas_call | solution.py:571
  108.6 1.0 copy.10
  109.6 0.0 all-to-all-done.2.in_ref
  109.6 0.0 copy-done
  109.6 3.3 %backward.1 = bf16[1152,1440]{1,0:T(8,128)(2,1)} custom-call(bf16[128,8,384]{2,1,0:T(8,128)(2,1)S(1)} %all-to-all-done.2.in_ref, bf16[1440,256]{1,0:T(8,128)(2,1)S(1)} %copy-done), custom_call_target="tpu_custom_call" | custom-call | flops 1024 | bytes 1024 | tf_op jit(solution)/shard_map/backward/pallas_call | solution.py:345
Async XLA Ops:
  7.4 41.2 %copy-start.1 = (s32[128]{0:T(128)S(1)}, s32[128]{0:T(128)}, u32[]{:S(2)}) copy-start(s32[128]{0:T(128)} %orders_ref.1) | copy-start | bytes 1540
  7.4 41.2 %all-to-all-start = ((bf16[128,16,256]{2,1,0:T(8,128)(2,1)}), bf16[128,16,256]{2,1,0:T(8,128)(2,1)S(1)}, u32[]{:S(2)}, u32[]{:S(2)}) async-start(bf16[128,16,256]{2,1,0:T(8,128)(2,1)} %get-tuple-element.34), calls=%async_computation | async-start | bytes 2097152 | tf_op jit(solution)/shard_map/all_to_all | solution.py:613
  27.2 15.0 %collective-permute-start = (bf16[2,72,1440]{2,1,0:T(8,128)(2,1)}, bf16[2,72,1440]{2,1,0:T(8,128)(2,1)S(1)}, u32[]{:S(2)}, u32[]{:S(2)}) collective-permute-start(bf16[2,72,1440]{2,1,0:T(8,128)(2,1)} %get-tuple-element.35), channel_id=1, source_target_pairs={{0,16},{16,32},{32,48},{48,0},{64,80},{80,96},{96,112},{112,64},{1... | collective-permute-start | bytes 1244168 | tf_op jit(solution)/shard_map/ppermute | solution.py:618
  28.2 14.8 %collective-permute-start.1 = (bf16[2,72,1440]{2,1,0:T(8,128)(2,1)}, bf16[2,72,1440]{2,1,0:T(8,128)(2,1)S(1)}, u32[]{:S(2)}, u32[]{:S(2)}) collective-permute-start(bf16[2,72,1440]{2,1,0:T(8,128)(2,1)} %get-tuple-element.36), channel_id=1, source_target_pairs={{0,48},{16,0},{32,16},{48,32},{64,112},{80,64},{96,80},{112,96},{1... | collective-permute-start | bytes 1244168 | tf_op jit(solution)/shard_map/ppermute | solution.py:618
  30.5 35.7 %collective-permute-start.2 = (bf16[2,72,1440]{2,1,0:T(8,128)(2,1)}, bf16[2,72,1440]{2,1,0:T(8,128)(2,1)S(1)}, u32[]{:S(2)}, u32[]{:S(2)}) collective-permute-start(bf16[2,72,1440]{2,1,0:T(8,128)(2,1)} %get-tuple-element.43), channel_id=1, source_target_pairs={{0,80},{16,96},{32,112},{48,64},{64,16},{80,32},{96,48},{112,0},{1... | collective-permute-start | bytes 1244168 | tf_op jit(solution)/shard_map/ppermute | solution.py:618
  33.1 33.2 %collective-permute-start.3 = (bf16[2,72,1440]{2,1,0:T(8,128)(2,1)}, bf16[2,72,1440]{2,1,0:T(8,128)(2,1)S(1)}, u32[]{:S(2)}, u32[]{:S(2)}) collective-permute-start(bf16[2,72,1440]{2,1,0:T(8,128)(2,1)} %get-tuple-element.44), channel_id=1, source_target_pairs={{0,112},{16,64},{32,80},{48,96},{64,48},{80,0},{96,16},{112,32},{1... | collective-permute-start | bytes 1244168 | tf_op jit(solution)/shard_map/ppermute | solution.py:618
  36.2 37.9 %collective-permute-start.4 = (bf16[2,72,1440]{2,1,0:T(8,128)(2,1)}, bf16[2,72,1440]{2,1,0:T(8,128)(2,1)S(1)}, u32[]{:S(2)}, u32[]{:S(2)}) collective-permute-start(bf16[2,72,1440]{2,1,0:T(8,128)(2,1)} %get-tuple-element.45), channel_id=1, source_target_pairs={{0,64},{16,80},{32,96},{48,112},{64,0},{80,16},{96,32},{112,48},{1... | collective-permute-start | bytes 1244168 | tf_op jit(solution)/shard_map/ppermute | solution.py:618
  42.3 24.0 %copy-start.2 = (bf16[2,72,1440]{2,1,0:T(8,128)(2,1)}, bf16[2,72,1440]{2,1,0:T(8,128)(2,1)S(1)}, u32[]{:S(2)}) copy-start(bf16[2,72,1440]{2,1,0:T(8,128)(2,1)S(1)} %collective-permute-done.refs_1_.rest_1_) | copy-start | bytes 1244164
  42.3 31.8 %collective-permute-start.5 = (bf16[2,72,1440]{2,1,0:T(8,128)(2,1)}, bf16[2,72,1440]{2,1,0:T(8,128)(2,1)}, u32[]{:S(2)}, u32[]{:S(2)}) collective-permute-start(bf16[2,72,1440]{2,1,0:T(8,128)(2,1)} %get-tuple-element.46), channel_id=1, source_target_pairs={{0,32},{16,48},{32,0},{48,16},{64,96},{80,112},{96,64},{112,80},{1... | collective-permute-start | bytes 1244168 | tf_op jit(solution)/shard_map/ppermute | solution.py:618
  43.1 23.2 %copy-start.3 = (bf16[2,72,1440]{2,1,0:T(8,128)(2,1)}, bf16[2,72,1440]{2,1,0:T(8,128)(2,1)S(1)}, u32[]{:S(2)}) copy-start(bf16[2,72,1440]{2,1,0:T(8,128)(2,1)S(1)} %collective-permute-done.1.refs_2_.rest_2_) | copy-start | bytes 1244164
  43.1 40.2 %collective-permute-start.6 = (bf16[2,72,1440]{2,1,0:T(8,128)(2,1)}, bf16[2,72,1440]{2,1,0:T(8,128)(2,1)}, u32[]{:S(2)}, u32[]{:S(2)}) collective-permute-start(bf16[2,72,1440]{2,1,0:T(8,128)(2,1)} %get-tuple-element.47), channel_id=1, source_target_pairs={{0,96},{16,112},{32,64},{48,80},{64,32},{80,48},{96,0},{112,16},{1... | collective-permute-start | bytes 1244168 | tf_op jit(solution)/shard_map/ppermute | solution.py:618
  62.8 24.9 %all-to-all-start.1 = ((bf16[8,36,721]{2,1,0:T(8,128)(2,1)}), bf16[8,36,721]{2,1,0:T(8,128)(2,1)S(1)}, u32[]{:S(2)}, u32[]{:S(2)}) async-start(bf16[8,36,721]{2,1,0:T(8,128)(2,1)} %get-tuple-element.39), calls=%async_computation.1 | async-start | bytes 983040 | tf_op jit(solution)/shard_map/all_to_all | solution.py:623
  66.3 0.8 copy-start.4
  66.3 0.9 copy-start.5
  74.0 19.6 %copy-start.6 = (bf16[2,72,1440]{2,1,0:T(8,128)(2,1)}, bf16[2,72,1440]{2,1,0:T(8,128)(2,1)S(1)}, u32[]{:S(2)}) copy-start(bf16[2,72,1440]{2,1,0:T(8,128)(2,1)S(1)} %collective-permute-done.4.rest_5_) | copy-start | bytes 1244164
  87.7 21.9 %all-to-all-start.2 = ((bf16[128,8,384]{2,1,0:T(8,128)(2,1)}), bf16[128,8,384]{2,1,0:T(8,128)(2,1)S(1)}, u32[]{:S(2)}, u32[]{:S(2)}) async-start(bf16[128,8,384]{2,1,0:T(8,128)(2,1)} %bitcast.5), calls=%async_computation.2 | async-start | bytes 1572864 | tf_op jit(solution)/shard_map/all_to_all | solution.py:627
  93.7 16.0 %copy-start = (bf16[1440,256]{1,0:T(8,128)(2,1)S(1)}, bf16[1440,256]{1,0:T(8,128)(2,1)}, u32[]{:S(2)}) copy-start(bf16[1440,256]{1,0:T(8,128)(2,1)} %get-tuple-element.61.table_ref) | copy-start | bytes 2211844

commit v5 on v4

--- a/solution.py
+++ b/solution.py
@@ -16,7 +16,7 @@
 BAND = 16
 LANES = 128
 GRID_WIDTH = 2 * LANES
-EARLY_PARTS = 5
+EARLY_PARTS = 6
 FIELD_COPIES = 2
 ROW_PAD = 40
 
@@ -162,7 +162,7 @@
 
 def spectral_kernel(
     fairness, member_count, var_count, deg_count, orders_ref, in_ref, grad_ref, score_ref,
-    weights, values, spectra, pulls, scores,
+    weights, values, spectra, pulls, scores, split,
 ):
     ens_count = 2 * member_count
     deg_part = -(-deg_count // member_count)
@@ -248,21 +248,26 @@
     rounded = scores[:var_count, :deg_count].astype(jnp.bfloat16)
     for member in range(member_count):
         score_ref[member] = rounded
+    half = BAND // 2
     for member in range(member_count):
-        part = pulls[member * 4 * ROW_PAD : (member + 1) * 4 * ROW_PAD, :].astype(jnp.bfloat16)
+        part = jnp.concatenate(
+            [
+                pulls[at : at + var_count, :]
+                for at in range(4 * member * ROW_PAD, 4 * (member + 1) * ROW_PAD, ROW_PAD)
+            ],
+            axis=0,
+        ).astype(jnp.bfloat16)
         back = lax.dot_general(
             table, part, (((1,), (1,)), ((), ())), preferred_element_type=jnp.float32
         )
-        halves = back.reshape(space_count, 2, BAND // 2, 4 * ROW_PAD)
-        packed = jnp.concatenate(
-            [
-                halves[:, 0],
-                halves[:, 1],
-                jnp.zeros((space_count, BAND // 2, 3 * LANES - 8 * ROW_PAD), jnp.float32),
-            ],
-            axis=2,
-        )
-        grad_ref[:, member] = packed.astype(jnp.bfloat16)
+        split[0] = back[:, :LANES]
+        split[1, :, : 4 * var_count - LANES] = back[:, LANES:]
+        pieces = []
+        for row in range(half):
+            rows = pl.ds(row, lat_count // half, stride=half)
+            pieces += [split[0, rows, :], split[1, rows, :][:, : 4 * var_count - LANES]]
+        packed = jnp.concatenate(pieces, axis=1).astype(jnp.bfloat16)
+        grad_ref[:, member] = packed.reshape(space_count, 2, half * 4 * var_count)
 
 
 def spectral(received, orders, fairness, member_count, var_count, deg_count):
@@ -280,7 +285,7 @@
         out_specs=[pl.BlockSpec(memory_space=pltpu.VMEM)] * 2,
         out_shape=[
             jax.ShapeDtypeStruct(
-                (space_count, member_count, band_rows // 2, 3 * LANES), jnp.bfloat16
+                (space_count, member_count, 2, band_rows // 2 * 4 * var_count), jnp.bfloat16
             ),
             jax.ShapeDtypeStruct((member_count, var_count, deg_count), jnp.bfloat16),
         ],
@@ -290,12 +295,13 @@
             pltpu.VMEM((2 * (ens_count + 1) * ROW_PAD, deg_pad), jnp.float32),
             pltpu.VMEM((2 * ens_count * ROW_PAD, deg_pad), jnp.float32),
             pltpu.VMEM((ROW_PAD, deg_pad), jnp.float32),
+            pltpu.VMEM((2, lat_count, LANES), jnp.float32),
         ],
         compiler_params=pltpu.CompilerParams(vmem_limit_bytes=28 * MIB),
         cost_estimate=pl.CostEstimate(flops=COST, bytes_accessed=COST, transcendentals=0),
         name="spectral",
     )(orders, received.reshape(space_count, member_count, band_rows, width))
-    return grads.reshape(senders, band_rows // 2, 3 * LANES), score
+    return grads.reshape(senders, 2, band_rows // 2 * 4 * var_count), score
 
 
 def backward_kernel(var_count, in_ref, table_ref, out_ref, staged, turned):
@@ -307,22 +313,23 @@
     @pl.when(step == 0)
     def _():
         half = BAND // 2
-        for part in range(3):
+        tiles = staged.shape[0]
+        for part in range(tiles):
             staged[part] = (
                 in_ref[:, :, part * LANES : (part + 1) * LANES]
+                .reshape(2 * order_count, LANES)
                 .astype(jnp.float32)
-                .reshape(order_count * half, LANES)
             )
-        for row in range(half):
+        for high in range(2):
             whole = jnp.concatenate(
-                [staged[part, pl.ds(row, order_count, stride=half), :].T for part in range(3)],
+                [staged[part, pl.ds(high, order_count, stride=2), :].T for part in range(tiles)],
                 axis=0,
             )
-            for high in range(2):
+            for low in range(half):
                 for c in range(2):
                     for own in range(2):
-                        source = (4 * high + 2 * c + own) * ROW_PAD
-                        at = own * var_count * BAND + high * half + row
+                        source = (4 * low + 2 * c + own) * var_count
+                        at = own * var_count * BAND + high * half + low
                         turned[c, pl.ds(at, var_count, stride=BAND), :] = whole[
                             source : source + var_count
                         ]
@@ -337,8 +344,8 @@
 
 
 def backward(received, table, own_count, var_count):
-    order_count, half_rows, width = received.shape
-    band_rows = 2 * half_rows
+    order_count, _, width = received.shape
+    band_rows = 2 * width // (2 * own_count * var_count)
     lon_count = table.shape[0]
     rows = own_count * var_count * band_rows
     steps = 2
@@ -346,13 +353,13 @@
         functools.partial(backward_kernel, var_count),
         grid=(steps,),
         in_specs=[
-            pl.BlockSpec((order_count, half_rows, width), lambda i: (0, 0, 0)),
+            pl.BlockSpec((order_count, 2, width), lambda i: (0, 0, 0)),
             pl.BlockSpec((lon_count, 2 * order_count), lambda i: (0, 0)),
         ],
         out_specs=pl.BlockSpec((rows // steps, lon_count), lambda i: (i, 0)),
         out_shape=jax.ShapeDtypeStruct((rows, lon_count), jnp.bfloat16),
         scratch_shapes=[
-            pltpu.VMEM((3, order_count * half_rows, LANES), jnp.float32),
+            pltpu.VMEM((width // LANES, 2 * order_count, LANES), jnp.float32),
             pltpu.VMEM((2, rows, order_count), jnp.float32),
         ],
         compiler_params=pltpu.CompilerParams(vmem_limit_bytes=16 * MIB),
@@ -427,8 +434,13 @@
     )(ens.reshape(-1, lon_count), truth.reshape(-1, lon_count))
 
 
+def stretch(x):
+    scaled = x * 2.0**124
+    return scaled + jnp.minimum(jnp.maximum(scaled * 2.0**10, -(2.0**24)), 2.0**24)
+
+
 def sign(a, b):
-    return jnp.minimum(jnp.maximum((a - b) * 2.0**70, -1.0), 1.0)
+    return jnp.minimum(jnp.maximum(a - b, -1.0), 1.0)
 
 
 def count_kernel(*refs):
@@ -440,7 +452,7 @@
         lanes = slice(lane_at, lane_at + LANES)
         span = pl.ds(at, rows)
         wide = [
-            parts[e // per_part][e % per_part, span, lanes].astype(jnp.float32) * 2.0**64
+            stretch(parts[e // per_part][e % per_part, span, lanes].astype(jnp.float32))
             for e in range(count)
         ]
         pieces = []
@@ -488,9 +500,10 @@
     )(*parts)
 
 
-def grid_kernel(fairness, lon_count, first, part_count, known, weight_ref, truth_ref, *rest):
-    parts, known_ref, carried = rest[:part_count], rest[part_count], rest[part_count + 1 : -3]
-    grad_ref, score_ref, total = rest[-3:]
+def grid_kernel(fairness, lon_count, known, weight_ref, truth_ref, spec_ref, *rest):
+    part_count = spec_ref.shape[0]
+    parts, known_ref = rest[:part_count], rest[part_count]
+    grad_ref, score_ref, wide_ref, total, mixed = rest[part_count + 1 :]
     step = pl.program_id(0)
     per_part, row_count, width = parts[0].shape
     ens_count = per_part * part_count
@@ -507,6 +520,15 @@
     @pl.when(step == 0)
     def _():
         total[...] = jnp.zeros_like(total)
+        spec_count, spec_vars, degrees = spec_ref.shape
+        for lane_at in range(0, degrees, LANES):
+            size = min(LANES, degrees - lane_at)
+            lanes = slice(lane_at, lane_at + size)
+            for order in range(spec_count):
+                mixed[pl.ds(order, spec_vars, stride=spec_count), :size] = spec_ref[
+                    order, :, lanes
+                ].astype(jnp.float32)
+            wide_ref[:, :, lanes] = mixed[:, :size].reshape(spec_vars, spec_count, size)
 
     def tile(at, rows, lane_at):
         lanes = slice(lane_at, lane_at + LANES)
@@ -520,9 +542,9 @@
         pieces = []
         for half in range(rows // 8):
             piece = slice(8 * half, 8 * half + 8)
-            x = [value[piece] * 2.0**64 for value in wide]
+            x = [stretch(value[piece]) for value in wide]
             goal = goals[piece]
-            y = goal * 2.0**64
+            y = stretch(goal)
             zero = jnp.zeros((8, LANES), jnp.float32)
             sums = [value[piece] for value in before] + [zero] * (ens_count - known)
             for i in range(ens_count):
@@ -542,7 +564,7 @@
             pieces.append(grads)
             score = (score - goal * toward_sum) * (1.0 / ens_count)
             lane = lax.broadcasted_iota(jnp.int32, (8, LANES), 1) + (
-                (step + first) * width + lane_at
+                step * width + lane_at
             )
             total[pl.ds(at + 8 * half, 8), :] += jnp.where(lane < lon_count, score, 0.0)
         for e in range(ens_count):
@@ -559,42 +581,43 @@
         for row in range(sub_rows):
             rows = total[pl.ds(row, row_count // sub_rows, stride=sub_rows), :]
             result = jnp.sum(rows.T, axis=0, keepdims=True) * (1.0 / lon_count)
-            score_ref[row : row + 1, :] = result + carried[1][row : row + 1, :] if carried else result
-
-
-def grid_scores(parts, signs, target, weights, fairness, sub_rows, blocks, earlier=()):
+            score_ref[row : row + 1, :] = result
+
+
+def grid_scores(parts, signs, target, weights, spec_score, fairness, sub_rows):
     per_part, row_count, lon_count = parts[0].shape
     ens_count = per_part * len(parts)
     var_count = row_count // sub_rows
+    order_count, _, deg_count = spec_score.shape
     width = GRID_WIDTH
-    first, last = blocks
     return pl.pallas_call(
-        functools.partial(grid_kernel, fairness, lon_count, first, len(parts), signs.shape[0]),
-        grid=(last - first,),
+        functools.partial(grid_kernel, fairness, lon_count, signs.shape[0]),
+        grid=(-(-lon_count // width),),
         in_specs=[
             pl.BlockSpec(memory_space=pltpu.SMEM),
-            pl.BlockSpec((row_count, width), lambda i: (0, i + first)),
+            pl.BlockSpec((row_count, width), lambda i: (0, i)),
+            pl.BlockSpec((order_count, var_count, deg_count), lambda i: (0, 0, 0)),
         ]
-        + [pl.BlockSpec((per_part, row_count, width), lambda i: (0, 0, i + first))] * len(parts)
-        + [pl.BlockSpec((signs.shape[0], row_count, width), lambda i: (0, 0, i + first))]
-        + [
-            pl.BlockSpec(memory_space=pl.ANY),
+        + [pl.BlockSpec((per_part, row_count, width), lambda i: (0, 0, i))] * len(parts)
+        + [pl.BlockSpec((signs.shape[0], row_count, width), lambda i: (0, 0, i))],
+        out_specs=[
+            pl.BlockSpec((ens_count, var_count, sub_rows, width), lambda i: (0, 0, 0, i)),
             pl.BlockSpec((sub_rows, var_count), lambda i: (0, 0)),
-        ][: len(earlier)],
-        out_specs=[
-            pl.BlockSpec((ens_count, var_count, sub_rows, width), lambda i: (0, 0, 0, i + first)),
-            pl.BlockSpec((sub_rows, var_count), lambda i: (0, 0)),
+            pl.BlockSpec((var_count, order_count, deg_count), lambda i: (0, 0, 0)),
         ],
         out_shape=[
             jax.ShapeDtypeStruct((ens_count, var_count, sub_rows, lon_count), jnp.bfloat16),
             jax.ShapeDtypeStruct((sub_rows, var_count), jnp.float32),
-        ],
-        scratch_shapes=[pltpu.VMEM((row_count, LANES), jnp.float32)],
-        input_output_aliases={3 + len(parts): 0} if earlier else {},
+            jax.ShapeDtypeStruct((var_count, order_count, deg_count), jnp.float32),
+        ],
+        scratch_shapes=[
+            pltpu.VMEM((row_count, LANES), jnp.float32),
+            pltpu.VMEM((var_count * order_count, LANES), jnp.float32),
+        ],
         compiler_params=pltpu.CompilerParams(vmem_limit_bytes=56 * MIB),
         cost_estimate=pl.CostEstimate(flops=COST, bytes_accessed=COST, transcendentals=0),
         name="grid",
-    )(weights, target, *parts, signs, *earlier)
+    )(weights, target, spec_score, *parts, signs)
 
 
 def local(ens, truth, legendre, orders):
@@ -625,10 +648,11 @@
         (grads, spec_score, signs, *parts)
     )
     returned = lax.all_to_all(grads, owners, split_axis=0, concat_axis=0, tiled=True)
-    spec_score = spec_score.astype(jnp.float32)
     weights = jnp.asarray(latitude_weights(lat_count))
-    grid_args = (parts, signs, target, weights, fairness, sub_rows)
-    grid_grad, grid_rows = grid_scores(*grid_args, (0, -(-lon_count // GRID_WIDTH)))
+    grid_grad, grid_rows, spec_score = grid_scores(
+        parts, signs, target, weights, spec_score, fairness, sub_rows
+    )
+    spec_score = spec_score.swapaxes(0, 1)
     grid_grad = grid_grad.reshape(ens_count, var_count, 1, sub_rows, lon_count)
     grid_score = grid_rows.T.reshape(var_count, 1, sub_rows)
     spec_grad = backward(returned, table, own_count, var_count).reshape(ens.shape)

time: 114 us -> 112 us (0.982)
  local copies, waits for them, and re-layouts: 1.91 us -> 0.03 us
    unnamed x15 -> x16, local copies, waits for them, and re-layouts: 1.91 us -> 0.03 us
  transfers between devices with their start and end apart: 10 -> 10, of which waited for: 3 -> 4; matrix products, arithmetic and copies ran while one was open for 1% -> 0% of each run, Pallas kernels for 39% -> 40%
where the time goes in v5:
time: 112 us; the launch traced here: 111 us
  Pallas kernels  54.6 us (49%)
  starting transfers between devices  38.8 us (35%)
  waiting for transfers between devices  16.8 us (15%)
    ppermute x7, starting transfers between devices, local(): lax.ppermute(parts[place], 'member', hop_pairs(hop, member_count))  18.2 us
    pallas_call x1, Pallas kernels, spectral(): pl.pallas_call(functools.partial(spectral_kernel, fairness, member_count,...  14.2 us
    pallas_call x1, Pallas kernels, grid_scores(): pl.pallas_call(functools.partial(grid_kernel, fairness, lon_count, signs....  13.9 us
    ppermute x7, waiting for transfers between devices, local(): lax.ppermute(parts[place], 'member', hop_pairs(hop, member_count))  12.3 us
    all_to_all x1, starting transfers between devices, local(): lax.all_to_all(sent, owners, split_axis=0, concat_axis=0, tiled=True)  11.1 us
    pallas_call x1, Pallas kernels, regroup(): pl.pallas_call(functools.partial(regroup_kernel, var_count, sub_rows), gr...  8.63 us
    pallas_call x1, Pallas kernels, count_signs(): pl.pallas_call(count_kernel, grid=(-(-lon_count // width),), in_specs=[pl...  7.75 us
    pallas_call x1, Pallas kernels, forward(): pl.pallas_call(functools.partial(forward_kernel, var_count, deg_count), i...  6.76 us
  transfers between devices with their start and end apart: 10, of which 4 were waited for; matrix products, arithmetic and copies ran while one was open for 0% of the time, Pallas kernels for 40%

profile of v5, /device:TPU:0, one launch (start us, length us, event | category | flops | bytes accessed | tf_op | source)
XLA Modules:
  0.0 111.0 jit_solution(12536516808228304226)
XLA Ops:
  0.6 6.8 %forward.1 = (bf16[128,16,256]{2,1,0:T(8,128)(2,1)}, bf16[1440,256]{1,0:T(8,128)(2,1)}) custom-call(s32[1,128]{1,0:T(1,128)} %bitcast.15, bf16[1152,1440]{1,0:T(8,128)(2,1)} %bitcast.16, bf16[36,16,1440]{2,1,0:T(8,128)(2,1)} %truth_ref.1, bf16[721,16,128]{2,1,0:T(8,128)(2,1)} %bitcast.20), custom_call_target="tpu_custom_call" | custom-call | flops 1024 | bytes 1024 | tf_op jit(solution)/shard_map/forward/pallas_call | solution.py:140
  7.4 0.0 copy-start.1
  7.4 11.1 %all-to-all-start = ((bf16[128,16,256]{2,1,0:T(8,128)(2,1)}), bf16[128,16,256]{2,1,0:T(8,128)(2,1)S(1)}, u32[]{:S(2)}, u32[]{:S(2)}) async-start(bf16[128,16,256]{2,1,0:T(8,128)(2,1)} %get-tuple-element.35), calls=%async_computation | async-start | bytes 2097152 | tf_op jit(solution)/shard_map/all_to_all | solution.py:636
  18.6 8.6 %regroup.1 = (bf16[2,72,1440]{2,1,0:T(8,128)(2,1)}, bf16[2,72,1440]{2,1,0:T(8,128)(2,1)}, bf16[2,72,1440]{2,1,0:T(8,128)(2,1)}, bf16[2,72,1440]{2,1,0:T(8,128)(2...) custom-call(bf16[1152,1440]{1,0:T(8,128)(2,1)} %bitcast.17, ...), custom_call_target="tpu_custom_call" | custom-call | flops 1024 | bytes 1024 | tf_op jit(solution)/shard_map/regroup/pallas_call | solution.py:413
  27.2 1.0 collective-permute-start
  28.2 2.3 %collective-permute-start.1 = (bf16[2,72,1440]{2,1,0:T(8,128)(2,1)}, bf16[2,72,1440]{2,1,0:T(8,128)(2,1)S(1)}, u32[]{:S(2)}, u32[]{:S(2)}) collective-permute-start(bf16[2,72,1440]{2,1,0:T(8,128)(2,1)} %get-tuple-element.37), channel_id=1, source_target_pairs={{0,48},{16,0},{32,16},{48,32},{64,112},{80,64},{96,80},{112,96},{1... | collective-permute-start | bytes 1244168 | tf_op jit(solution)/shard_map/ppermute | solution.py:641
  30.5 2.6 %collective-permute-start.2 = (bf16[2,72,1440]{2,1,0:T(8,128)(2,1)}, bf16[2,72,1440]{2,1,0:T(8,128)(2,1)S(1)}, u32[]{:S(2)}, u32[]{:S(2)}) collective-permute-start(bf16[2,72,1440]{2,1,0:T(8,128)(2,1)} %get-tuple-element.44), channel_id=1, source_target_pairs={{0,80},{16,96},{32,112},{48,64},{64,16},{80,32},{96,48},{112,0},{1... | collective-permute-start | bytes 1244168 | tf_op jit(solution)/shard_map/ppermute | solution.py:641
  33.1 3.1 %collective-permute-start.3 = (bf16[2,72,1440]{2,1,0:T(8,128)(2,1)}, bf16[2,72,1440]{2,1,0:T(8,128)(2,1)}, u32[]{:S(2)}, u32[]{:S(2)}) collective-permute-start(bf16[2,72,1440]{2,1,0:T(8,128)(2,1)} %get-tuple-element.45), channel_id=1, source_target_pairs={{0,112},{16,64},{32,80},{48,96},{64,48},{80,0},{96,16},{112,32},{1... | collective-permute-start | bytes 1244168 | tf_op jit(solution)/shard_map/ppermute | solution.py:641
  36.2 2.9 %collective-permute-start.4 = (bf16[2,72,1440]{2,1,0:T(8,128)(2,1)}, bf16[2,72,1440]{2,1,0:T(8,128)(2,1)}, u32[]{:S(2)}, u32[]{:S(2)}) collective-permute-start(bf16[2,72,1440]{2,1,0:T(8,128)(2,1)} %get-tuple-element.46), channel_id=1, source_target_pairs={{0,64},{16,80},{32,96},{48,112},{64,0},{80,16},{96,32},{112,48},{1... | collective-permute-start | bytes 1244168 | tf_op jit(solution)/shard_map/ppermute | solution.py:641
  39.0 3.2 %collective-permute-done.refs_1_.rest_1_ = bf16[2,72,1440]{2,1,0:T(8,128)(2,1)S(1)} collective-permute-done((bf16[2,72,1440]{2,1,0:T(8,128)(2,1)}, bf16[2,72,1440]{2,1,0:T(8,128)(2,1)S(1)}, u32[]{:S(2)}, u32[]{:S(2)}) %collective-permute-start) | collective-permute-done | bytes 414752 | tf_op jit(solution)/shard_map/ppermute | solution.py:641
  42.2 0.0 copy-start.3
  42.3 0.8 collective-permute-start.5
  43.1 0.0 collective-permute-done.1.refs_2_.rest_2_
  43.1 0.0 copy-start.4
  43.1 5.6 %collective-permute-start.6 = (bf16[2,72,1440]{2,1,0:T(8,128)(2,1)}, bf16[2,72,1440]{2,1,0:T(8,128)(2,1)S(1)}, u32[]{:S(2)}, u32[]{:S(2)}) collective-permute-start(bf16[2,72,1440]{2,1,0:T(8,128)(2,1)} %get-tuple-element.48), channel_id=1, source_target_pairs={{0,96},{16,112},{32,64},{48,80},{64,32},{80,48},{96,0},{112,16},{1... | collective-permute-start | bytes 1244168 | tf_op jit(solution)/shard_map/ppermute | solution.py:641
  48.6 0.0 all-to-all-done
  48.6 0.0 copy-done.1
  48.6 14.2 %spectral.1 = (bf16[16,8,2,1152]{3,2,1,0:T(2,128)(2,1)}, bf16[8,36,721]{2,1,0:T(8,128)(2,1)}) custom-call(s32[128]{0:T(128)S(1)} %copy-done.1, bf16[16,8,16,256]{3,2,1,0:T(8,128)(2,1)S(1)} %bitcast.14), custom_call_target="tpu_custom_call" | custom-call | flops 1024 | bytes 1024 | tf_op jit(solution)/shard_map/spectral/pallas_call | solution.py:279
  62.9 3.5 %all-to-all-start.1 = ((bf16[8,36,721]{2,1,0:T(8,128)(2,1)}), bf16[8,36,721]{2,1,0:T(8,128)(2,1)S(1)}, u32[]{:S(2)}, u32[]{:S(2)}) async-start(bf16[8,36,721]{2,1,0:T(8,128)(2,1)} %get-tuple-element.40), calls=%async_computation.1 | async-start | bytes 983040 | tf_op jit(solution)/shard_map/all_to_all | solution.py:646
  66.3 0.0 collective-permute-done.2.refs_3_.rest_3_
  66.4 0.0 copy-start.5
  66.4 0.0 collective-permute-done.3.refs_4_.rest_4_
  66.4 1.3 %collective-permute-done.4.refs_5_.rest_5_ = bf16[2,72,1440]{2,1,0:T(8,128)(2,1)} collective-permute-done((bf16[2,72,1440]{2,1,0:T(8,128)(2,1)}, bf16[2,72,1440]{2,1,0:T(8,128)(2,1)}, u32[]{:S(2)}, u32[]{:S(2)}) %collective-permute-start.4) | collective-permute-done | bytes 414752 | tf_op jit(solution)/shard_map/ppermute | solution.py:641
  67.6 0.0 copy-done.3
  67.6 0.0 copy-done.4
  67.6 0.0 copy-done.5
  67.7 7.8 %count.1.rest_8_ = bf16[12,72,1440]{2,1,0:T(8,128)(2,1)} custom-call(bf16[2,72,1440]{2,1,0:T(8,128)(2,1)} %get-tuple-element.50.refs_0_.rest_0_, bf16[2,72,1440]{2,1,0:T(8,128)(2,1)} %copy-done.3, bf16[2,72,1440]{2,1,0:T(8,128)(2,1)} %copy-done.4, bf16[2,72,1440]{2,1,0:T(8,128)(2,1)} %copy-done.5, ...), custom_call_target="tpu_custom_call" | custom-call | flops 1024 | bytes 1024 | tf_op jit(solution)/shard_map/count/pallas_call | solution.py:491
  75.4 0.0 collective-permute-done.5.rest_6_
  75.4 0.0 copy-start.6
  75.4 7.8 %collective-permute-done.6.rest_7_ = bf16[2,72,1440]{2,1,0:T(8,128)(2,1)S(1)} collective-permute-done((bf16[2,72,1440]{2,1,0:T(8,128)(2,1)}, bf16[2,72,1440]{2,1,0:T(8,128)(2,1)S(1)}, u32[]{:S(2)}, u32[]{:S(2)}) %collective-permute-start.6) | collective-permute-done | bytes 414752 | tf_op jit(solution)/shard_map/ppermute | solution.py:641
  83.2 0.0 copy-start.7
  83.2 4.5 %all-to-all-done.1.spec_ref = bf16[8,36,721]{2,1,0:T(8,128)(2,1)S(1)} async-done(((bf16[8,36,721]{2,1,0:T(8,128)(2,1)}), bf16[8,36,721]{2,1,0:T(8,128)(2,1)S(1)}, u32[]{:S(2)}, u32[]{:S(2)}) %all-to-all-start.1) | async-done | bytes 415328 | tf_op jit(solution)/shard_map/all_to_all | solution.py:646
  87.7 0.0 copy-start.2
  87.7 6.0 %all-to-all-start.2 = ((bf16[128,2,1152]{2,1,0:T(2,128)(2,1)}), bf16[128,2,1152]{2,1,0:T(2,128)(2,1)S(1)}, u32[]{:S(2)}, u32[]{:S(2)}) async-start(bf16[128,2,1152]{2,1,0:T(2,128)(2,1)} %bitcast.5), calls=%async_computation.2 | async-start | bytes 1179648 | tf_op jit(solution)/shard_map/all_to_all | solution.py:650
  93.7 0.0 copy-start
  93.7 0.0 copy-done.6
  93.7 0.0 copy-done.7
  93.7 0.0 copy-done.2
  93.7 13.9 %grid.1 = (bf16[16,36,2,1440]{3,2,1,0:T(2,128)(2,1)}, f32[2,36]{1,0:T(2,128)}, f32[36,8,721]{2,1,0:T(8,128)}) custom-call(f32[256]{0:T(256)} %constant.2.clone.weight_ref, bf16[72,1440]{1,0:T(8,128)(2,1)} %get-tuple-element.34.truth_ref, bf16[8,36,721]{2,1,0:T(8,128)(2,1)} %copy-done.2, bf16[2,72,1440]{2,1,0:T(8,128)(2,1)} %get-tuple-element.50.refs_0_.rest_0_, ...), custom_call_target="tpu_custom_call" | custom-call | flops 1024 | bytes 1024 | tf_op jit(solution)/shard_map/grid/pallas_call | solution.py:593
  107.6 0.0 all-to-all-done.2.in_ref
  107.7 0.0 copy-done
  107.7 3.3 %backward.1 = bf16[1152,1440]{1,0:T(8,128)(2,1)} custom-call(bf16[128,2,1152]{2,1,0:T(2,128)(2,1)S(1)} %all-to-all-done.2.in_ref, bf16[1440,256]{1,0:T(8,128)(2,1)S(1)} %copy-done), custom_call_target="tpu_custom_call" | custom-call | flops 1024 | bytes 1024 | tf_op jit(solution)/shard_map/backward/pallas_call | solution.py:352
Async XLA Ops:
  7.4 41.2 %copy-start.1 = (s32[128]{0:T(128)S(1)}, s32[128]{0:T(128)}, u32[]{:S(2)}) copy-start(s32[128]{0:T(128)} %orders_ref.1) | copy-start | bytes 1540
  7.4 41.2 %all-to-all-start = ((bf16[128,16,256]{2,1,0:T(8,128)(2,1)}), bf16[128,16,256]{2,1,0:T(8,128)(2,1)S(1)}, u32[]{:S(2)}, u32[]{:S(2)}) async-start(bf16[128,16,256]{2,1,0:T(8,128)(2,1)} %get-tuple-element.35), calls=%async_computation | async-start | bytes 2097152 | tf_op jit(solution)/shard_map/all_to_all | solution.py:636
  27.2 15.0 %collective-permute-start = (bf16[2,72,1440]{2,1,0:T(8,128)(2,1)}, bf16[2,72,1440]{2,1,0:T(8,128)(2,1)S(1)}, u32[]{:S(2)}, u32[]{:S(2)}) collective-permute-start(bf16[2,72,1440]{2,1,0:T(8,128)(2,1)} %get-tuple-element.36), channel_id=1, source_target_pairs={{0,16},{16,32},{32,48},{48,0},{64,80},{80,96},{96,112},{112,64},{1... | collective-permute-start | bytes 1244168 | tf_op jit(solution)/shard_map/ppermute | solution.py:641
  28.2 14.8 %collective-permute-start.1 = (bf16[2,72,1440]{2,1,0:T(8,128)(2,1)}, bf16[2,72,1440]{2,1,0:T(8,128)(2,1)S(1)}, u32[]{:S(2)}, u32[]{:S(2)}) collective-permute-start(bf16[2,72,1440]{2,1,0:T(8,128)(2,1)} %get-tuple-element.37), channel_id=1, source_target_pairs={{0,48},{16,0},{32,16},{48,32},{64,112},{80,64},{96,80},{112,96},{1... | collective-permute-start | bytes 1244168 | tf_op jit(solution)/shard_map/ppermute | solution.py:641
  30.5 35.8 %collective-permute-start.2 = (bf16[2,72,1440]{2,1,0:T(8,128)(2,1)}, bf16[2,72,1440]{2,1,0:T(8,128)(2,1)S(1)}, u32[]{:S(2)}, u32[]{:S(2)}) collective-permute-start(bf16[2,72,1440]{2,1,0:T(8,128)(2,1)} %get-tuple-element.44), channel_id=1, source_target_pairs={{0,80},{16,96},{32,112},{48,64},{64,16},{80,32},{96,48},{112,0},{1... | collective-permute-start | bytes 1244168 | tf_op jit(solution)/shard_map/ppermute | solution.py:641
  33.1 33.3 %collective-permute-start.3 = (bf16[2,72,1440]{2,1,0:T(8,128)(2,1)}, bf16[2,72,1440]{2,1,0:T(8,128)(2,1)}, u32[]{:S(2)}, u32[]{:S(2)}) collective-permute-start(bf16[2,72,1440]{2,1,0:T(8,128)(2,1)} %get-tuple-element.45), channel_id=1, source_target_pairs={{0,112},{16,64},{32,80},{48,96},{64,48},{80,0},{96,16},{112,32},{1... | collective-permute-start | bytes 1244168 | tf_op jit(solution)/shard_map/ppermute | solution.py:641
  36.2 31.5 %collective-permute-start.4 = (bf16[2,72,1440]{2,1,0:T(8,128)(2,1)}, bf16[2,72,1440]{2,1,0:T(8,128)(2,1)}, u32[]{:S(2)}, u32[]{:S(2)}) collective-permute-start(bf16[2,72,1440]{2,1,0:T(8,128)(2,1)} %get-tuple-element.46), channel_id=1, source_target_pairs={{0,64},{16,80},{32,96},{48,112},{64,0},{80,16},{96,32},{112,48},{1... | collective-permute-start | bytes 1244168 | tf_op jit(solution)/shard_map/ppermute | solution.py:641
  42.2 25.4 %copy-start.3 = (bf16[2,72,1440]{2,1,0:T(8,128)(2,1)}, bf16[2,72,1440]{2,1,0:T(8,128)(2,1)S(1)}, u32[]{:S(2)}) copy-start(bf16[2,72,1440]{2,1,0:T(8,128)(2,1)S(1)} %collective-permute-done.refs_1_.rest_1_) | copy-start | bytes 1244164
  42.3 33.2 %collective-permute-start.5 = (bf16[2,72,1440]{2,1,0:T(8,128)(2,1)}, bf16[2,72,1440]{2,1,0:T(8,128)(2,1)S(1)}, u32[]{:S(2)}, u32[]{:S(2)}) collective-permute-start(bf16[2,72,1440]{2,1,0:T(8,128)(2,1)} %get-tuple-element.47), channel_id=1, source_target_pairs={{0,32},{16,48},{32,0},{48,16},{64,96},{80,112},{96,64},{112,80},{1... | collective-permute-start | bytes 1244168 | tf_op jit(solution)/shard_map/ppermute | solution.py:641
  43.1 24.6 %copy-start.4 = (bf16[2,72,1440]{2,1,0:T(8,128)(2,1)}, bf16[2,72,1440]{2,1,0:T(8,128)(2,1)S(1)}, u32[]{:S(2)}) copy-start(bf16[2,72,1440]{2,1,0:T(8,128)(2,1)S(1)} %collective-permute-done.1.refs_2_.rest_2_) | copy-start | bytes 1244164
  43.1 40.1 %collective-permute-start.6 = (bf16[2,72,1440]{2,1,0:T(8,128)(2,1)}, bf16[2,72,1440]{2,1,0:T(8,128)(2,1)S(1)}, u32[]{:S(2)}, u32[]{:S(2)}) collective-permute-start(bf16[2,72,1440]{2,1,0:T(8,128)(2,1)} %get-tuple-element.48), channel_id=1, source_target_pairs={{0,96},{16,112},{32,64},{48,80},{64,32},{80,48},{96,0},{112,16},{1... | collective-permute-start | bytes 1244168 | tf_op jit(solution)/shard_map/ppermute | solution.py:641
  62.9 24.8 %all-to-all-start.1 = ((bf16[8,36,721]{2,1,0:T(8,128)(2,1)}), bf16[8,36,721]{2,1,0:T(8,128)(2,1)S(1)}, u32[]{:S(2)}, u32[]{:S(2)}) async-start(bf16[8,36,721]{2,1,0:T(8,128)(2,1)} %get-tuple-element.40), calls=%async_computation.1 | async-start | bytes 983040 | tf_op jit(solution)/shard_map/all_to_all | solution.py:646
  66.4 1.3 %copy-start.5 = (bf16[2,72,1440]{2,1,0:T(8,128)(2,1)}, bf16[2,72,1440]{2,1,0:T(8,128)(2,1)S(1)}, u32[]{:S(2)}) copy-start(bf16[2,72,1440]{2,1,0:T(8,128)(2,1)S(1)} %collective-permute-done.2.refs_3_.rest_3_) | copy-start | bytes 1244164
  75.4 18.3 %copy-start.6 = (bf16[2,72,1440]{2,1,0:T(8,128)(2,1)}, bf16[2,72,1440]{2,1,0:T(8,128)(2,1)S(1)}, u32[]{:S(2)}) copy-start(bf16[2,72,1440]{2,1,0:T(8,128)(2,1)S(1)} %collective-permute-done.5.rest_6_) | copy-start | bytes 1244164
  83.2 10.5 %copy-start.7 = (bf16[2,72,1440]{2,1,0:T(8,128)(2,1)}, bf16[2,72,1440]{2,1,0:T(8,128)(2,1)S(1)}, u32[]{:S(2)}) copy-start(bf16[2,72,1440]{2,1,0:T(8,128)(2,1)S(1)} %collective-permute-done.6.rest_7_) | copy-start | bytes 1244164
  87.7 6.0 %copy-start.2 = (bf16[8,36,721]{2,1,0:T(8,128)(2,1)}, bf16[8,36,721]{2,1,0:T(8,128)(2,1)S(1)}, u32[]{:S(2)}) copy-start(bf16[8,36,721]{2,1,0:T(8,128)(2,1)S(1)} %all-to-all-done.1.spec_ref) | copy-start | bytes 1245892
  87.7 19.9 %all-to-all-start.2 = ((bf16[128,2,1152]{2,1,0:T(2,128)(2,1)}), bf16[128,2,1152]{2,1,0:T(2,128)(2,1)S(1)}, u32[]{:S(2)}, u32[]{:S(2)}) async-start(bf16[128,2,1152]{2,1,0:T(2,128)(2,1)} %bitcast.5), calls=%async_computation.2 | async-start | bytes 1179648 | tf_op jit(solution)/shard_map/all_to_all | solution.py:650
  93.7 14.0 %copy-start = (bf16[1440,256]{1,0:T(8,128)(2,1)S(1)}, bf16[1440,256]{1,0:T(8,128)(2,1)}, u32[]{:S(2)}) copy-start(bf16[1440,256]{1,0:T(8,128)(2,1)} %get-tuple-element.63.table_ref) | copy-start | bytes 2211844

commit v6 on v5

--- a/solution.py
+++ b/solution.py
@@ -368,7 +368,7 @@
     )(received, table)
 
 
-HOPS = ((0, 0), (0, 1), (0, 3), (1, 1), (1, 3), (1, 0), (0, 2), (1, 2))
+HOPS = ((0, 0), (0, 1), (0, 3), (1, 3), (1, 1), (1, 2), (1, 0), (0, 2))
 RING = 4
 
 

time: 112 us -> 112 us (level)
  starting transfers between devices: 38.8 us -> 37.1 us
  waiting for transfers between devices: 16.8 us -> 18.4 us
    ppermute x7, starting transfers between devices: 18.2 us -> 15.9 us  [local(): lax.ppermute(parts[place], 'member', hop_pairs(hop, member_count))]
    all_to_all x1, waiting for transfers between devices: 4.51 us -> 6.27 us  [local(): lax.all_to_all(score, 'member', split_axis=0, concat_axis=0, tiled=True)]
  transfers between devices with their start and end apart: 10 -> 10, of which waited for: 4 -> 3; matrix products, arithmetic and copies ran while one was open for 0% -> 0% of each run, Pallas kernels for 40% -> 40%
where the time goes in v6:
time: 112 us; the launch traced here: 111 us
  Pallas kernels  54.7 us (49%)
  starting transfers between devices  37.1 us (33%)
  waiting for transfers between devices  18.4 us (16%)
    ppermute x7, starting transfers between devices, local(): lax.ppermute(parts[place], 'member', hop_pairs(hop, member_count))  15.9 us
    pallas_call x1, Pallas kernels, spectral(): pl.pallas_call(functools.partial(spectral_kernel, fairness, member_count,...  14.2 us
    pallas_call x1, Pallas kernels, grid_scores(): pl.pallas_call(functools.partial(grid_kernel, fairness, lon_count, signs....  13.9 us
    ppermute x7, waiting for transfers between devices, local(): lax.ppermute(parts[place], 'member', hop_pairs(hop, member_count))  12.2 us
    all_to_all x1, starting transfers between devices, local(): lax.all_to_all(sent, owners, split_axis=0, concat_axis=0, tiled=True)  11.1 us
    pallas_call x1, Pallas kernels, regroup(): pl.pallas_call(functools.partial(regroup_kernel, var_count, sub_rows), gr...  8.64 us
    pallas_call x1, Pallas kernels, count_signs(): pl.pallas_call(count_kernel, grid=(-(-lon_count // width),), in_specs=[pl...  7.75 us
    pallas_call x1, Pallas kernels, forward(): pl.pallas_call(functools.partial(forward_kernel, var_count, deg_count), i...  6.76 us
  transfers between devices with their start and end apart: 10, of which 3 were waited for; matrix products, arithmetic and copies ran while one was open for 0% of the time, Pallas kernels for 40%

profile of v6, /device:TPU:0, one launch (start us, length us, event | category | flops | bytes accessed | tf_op | source)
XLA Modules:
  0.0 111.0 jit_solution(16516727284539085476)
XLA Ops:
  0.6 6.8 %forward.1 = (bf16[128,16,256]{2,1,0:T(8,128)(2,1)}, bf16[1440,256]{1,0:T(8,128)(2,1)}) custom-call(s32[1,128]{1,0:T(1,128)} %bitcast.15, bf16[1152,1440]{1,0:T(8,128)(2,1)} %bitcast.16, bf16[36,16,1440]{2,1,0:T(8,128)(2,1)} %truth_ref.1, bf16[721,16,128]{2,1,0:T(8,128)(2,1)} %bitcast.20), custom_call_target="tpu_custom_call" | custom-call | flops 1024 | bytes 1024 | tf_op jit(solution)/shard_map/forward/pallas_call | solution.py:140
  7.4 0.0 copy-start.1
  7.4 11.1 %all-to-all-start = ((bf16[128,16,256]{2,1,0:T(8,128)(2,1)}), bf16[128,16,256]{2,1,0:T(8,128)(2,1)S(1)}, u32[]{:S(2)}, u32[]{:S(2)}) async-start(bf16[128,16,256]{2,1,0:T(8,128)(2,1)} %get-tuple-element.35), calls=%async_computation | async-start | bytes 2097152 | tf_op jit(solution)/shard_map/all_to_all | solution.py:636
  18.6 8.6 %regroup.1 = (bf16[2,72,1440]{2,1,0:T(8,128)(2,1)}, bf16[2,72,1440]{2,1,0:T(8,128)(2,1)}, bf16[2,72,1440]{2,1,0:T(8,128)(2,1)}, bf16[2,72,1440]{2,1,0:T(8,128)(2...) custom-call(bf16[1152,1440]{1,0:T(8,128)(2,1)} %bitcast.17, ...), custom_call_target="tpu_custom_call" | custom-call | flops 1024 | bytes 1024 | tf_op jit(solution)/shard_map/regroup/pallas_call | solution.py:413
  27.2 1.0 collective-permute-start
  28.2 2.3 %collective-permute-start.1 = (bf16[2,72,1440]{2,1,0:T(8,128)(2,1)}, bf16[2,72,1440]{2,1,0:T(8,128)(2,1)S(1)}, u32[]{:S(2)}, u32[]{:S(2)}) collective-permute-start(bf16[2,72,1440]{2,1,0:T(8,128)(2,1)} %get-tuple-element.37), channel_id=1, source_target_pairs={{0,48},{16,0},{32,16},{48,32},{64,112},{80,64},{96,80},{112,96},{1... | collective-permute-start | bytes 1244168 | tf_op jit(solution)/shard_map/ppermute | solution.py:641
  30.5 3.8 %collective-permute-start.2 = (bf16[2,72,1440]{2,1,0:T(8,128)(2,1)}, bf16[2,72,1440]{2,1,0:T(8,128)(2,1)S(1)}, u32[]{:S(2)}, u32[]{:S(2)}) collective-permute-start(bf16[2,72,1440]{2,1,0:T(8,128)(2,1)} %get-tuple-element.44), channel_id=1, source_target_pairs={{0,112},{16,64},{32,80},{48,96},{64,48},{80,0},{96,16},{112,32},{1... | collective-permute-start | bytes 1244168 | tf_op jit(solution)/shard_map/ppermute | solution.py:641
  34.3 0.6 collective-permute-start.3
  35.0 4.1 %collective-permute-start.4 = (bf16[2,72,1440]{2,1,0:T(8,128)(2,1)}, bf16[2,72,1440]{2,1,0:T(8,128)(2,1)}, u32[]{:S(2)}, u32[]{:S(2)}) collective-permute-start(bf16[2,72,1440]{2,1,0:T(8,128)(2,1)} %get-tuple-element.46), channel_id=1, source_target_pairs={{0,96},{16,112},{32,64},{48,80},{64,32},{80,48},{96,0},{112,16},{1... | collective-permute-start | bytes 1244168 | tf_op jit(solution)/shard_map/ppermute | solution.py:641
  39.0 3.2 %collective-permute-done.refs_1_.rest_1_ = bf16[2,72,1440]{2,1,0:T(8,128)(2,1)S(1)} collective-permute-done((bf16[2,72,1440]{2,1,0:T(8,128)(2,1)}, bf16[2,72,1440]{2,1,0:T(8,128)(2,1)S(1)}, u32[]{:S(2)}, u32[]{:S(2)}) %collective-permute-start) | collective-permute-done | bytes 414752 | tf_op jit(solution)/shard_map/ppermute | solution.py:641
  42.2 0.0 copy-start.3
  42.3 3.4 %collective-permute-start.5 = (bf16[2,72,1440]{2,1,0:T(8,128)(2,1)}, bf16[2,72,1440]{2,1,0:T(8,128)(2,1)S(1)}, u32[]{:S(2)}, u32[]{:S(2)}) collective-permute-start(bf16[2,72,1440]{2,1,0:T(8,128)(2,1)} %get-tuple-element.47), channel_id=1, source_target_pairs={{0,64},{16,80},{32,96},{48,112},{64,0},{80,16},{96,32},{112,48},{1... | collective-permute-start | bytes 1244168 | tf_op jit(solution)/shard_map/ppermute | solution.py:641
  45.7 0.0 collective-permute-done.1.refs_2_.rest_2_
  45.7 0.0 copy-start.4
  45.7 0.7 collective-permute-start.6
  46.4 0.0 all-to-all-done
  46.4 0.0 copy-done.1
  46.4 14.2 %spectral.1 = (bf16[16,8,2,1152]{3,2,1,0:T(2,128)(2,1)}, bf16[8,36,721]{2,1,0:T(8,128)(2,1)}) custom-call(s32[128]{0:T(128)S(1)} %copy-done.1, bf16[16,8,16,256]{3,2,1,0:T(8,128)(2,1)S(1)} %bitcast.14), custom_call_target="tpu_custom_call" | custom-call | flops 1024 | bytes 1024 | tf_op jit(solution)/shard_map/spectral/pallas_call | solution.py:279
  60.6 4.1 %all-to-all-start.1 = ((bf16[8,36,721]{2,1,0:T(8,128)(2,1)}), bf16[8,36,721]{2,1,0:T(8,128)(2,1)S(1)}, u32[]{:S(2)}, u32[]{:S(2)}) async-start(bf16[8,36,721]{2,1,0:T(8,128)(2,1)} %get-tuple-element.40), calls=%async_computation.1 | async-start | bytes 983040 | tf_op jit(solution)/shard_map/all_to_all | solution.py:646
  64.7 0.0 collective-permute-done.2.refs_3_.rest_3_
  64.7 0.0 copy-start.5
  64.7 0.0 collective-permute-done.3.refs_4_.rest_4_
  64.7 8.9 %collective-permute-done.4.refs_5_.rest_5_ = bf16[2,72,1440]{2,1,0:T(8,128)(2,1)} collective-permute-done((bf16[2,72,1440]{2,1,0:T(8,128)(2,1)}, bf16[2,72,1440]{2,1,0:T(8,128)(2,1)}, u32[]{:S(2)}, u32[]{:S(2)}) %collective-permute-start.4) | collective-permute-done | bytes 414752 | tf_op jit(solution)/shard_map/ppermute | solution.py:641
  73.6 0.0 copy-done.3
  73.6 0.0 copy-done.4
  73.7 0.0 copy-done.5
  73.7 7.8 %count.1.rest_8_ = bf16[12,72,1440]{2,1,0:T(8,128)(2,1)} custom-call(bf16[2,72,1440]{2,1,0:T(8,128)(2,1)} %get-tuple-element.50.refs_0_.rest_0_, bf16[2,72,1440]{2,1,0:T(8,128)(2,1)} %copy-done.3, bf16[2,72,1440]{2,1,0:T(8,128)(2,1)} %copy-done.4, bf16[2,72,1440]{2,1,0:T(8,128)(2,1)} %copy-done.5, ...), custom_call_target="tpu_custom_call" | custom-call | flops 1024 | bytes 1024 | tf_op jit(solution)/shard_map/count/pallas_call | solution.py:491
  81.4 0.0 collective-permute-done.5.rest_6_
  81.4 0.0 copy-start.6
  81.4 0.0 collective-permute-done.6.rest_7_
  81.4 0.0 copy-start.7
  81.4 6.3 %all-to-all-done.1.spec_ref = bf16[8,36,721]{2,1,0:T(8,128)(2,1)S(1)} async-done(((bf16[8,36,721]{2,1,0:T(8,128)(2,1)}), bf16[8,36,721]{2,1,0:T(8,128)(2,1)S(1)}, u32[]{:S(2)}, u32[]{:S(2)}) %all-to-all-start.1) | async-done | bytes 415328 | tf_op jit(solution)/shard_map/all_to_all | solution.py:646
  87.7 0.0 copy-start.2
  87.7 5.9 %all-to-all-start.2 = ((bf16[128,2,1152]{2,1,0:T(2,128)(2,1)}), bf16[128,2,1152]{2,1,0:T(2,128)(2,1)S(1)}, u32[]{:S(2)}, u32[]{:S(2)}) async-start(bf16[128,2,1152]{2,1,0:T(2,128)(2,1)} %bitcast.5), calls=%async_computation.2 | async-start | bytes 1179648 | tf_op jit(solution)/shard_map/all_to_all | solution.py:650
  93.6 0.0 copy-start
  93.7 0.0 copy-done.6
  93.7 0.0 copy-done.7
  93.7 0.0 copy-done.2
  93.7 13.9 %grid.1 = (bf16[16,36,2,1440]{3,2,1,0:T(2,128)(2,1)}, f32[2,36]{1,0:T(2,128)}, f32[36,8,721]{2,1,0:T(8,128)}) custom-call(f32[256]{0:T(256)} %constant.2.clone.weight_ref, bf16[72,1440]{1,0:T(8,128)(2,1)} %get-tuple-element.34.truth_ref, bf16[8,36,721]{2,1,0:T(8,128)(2,1)} %copy-done.2, bf16[2,72,1440]{2,1,0:T(8,128)(2,1)} %get-tuple-element.50.refs_0_.rest_0_, ...), custom_call_target="tpu_custom_call" | custom-call | flops 1024 | bytes 1024 | tf_op jit(solution)/shard_map/grid/pallas_call | solution.py:593
  107.6 0.0 all-to-all-done.2.in_ref
  107.6 0.0 copy-done
  107.6 3.4 %backward.1 = bf16[1152,1440]{1,0:T(8,128)(2,1)} custom-call(bf16[128,2,1152]{2,1,0:T(2,128)(2,1)S(1)} %all-to-all-done.2.in_ref, bf16[1440,256]{1,0:T(8,128)(2,1)S(1)} %copy-done), custom_call_target="tpu_custom_call" | custom-call | flops 1024 | bytes 1024 | tf_op jit(solution)/shard_map/backward/pallas_call | solution.py:352
Async XLA Ops:
  7.4 39.0 %copy-start.1 = (s32[128]{0:T(128)S(1)}, s32[128]{0:T(128)}, u32[]{:S(2)}) copy-start(s32[128]{0:T(128)} %orders_ref.1) | copy-start | bytes 1540
  7.4 39.0 %all-to-all-start = ((bf16[128,16,256]{2,1,0:T(8,128)(2,1)}), bf16[128,16,256]{2,1,0:T(8,128)(2,1)S(1)}, u32[]{:S(2)}, u32[]{:S(2)}) async-start(bf16[128,16,256]{2,1,0:T(8,128)(2,1)} %get-tuple-element.35), calls=%async_computation | async-start | bytes 2097152 | tf_op jit(solution)/shard_map/all_to_all | solution.py:636
  27.2 15.0 %collective-permute-start = (bf16[2,72,1440]{2,1,0:T(8,128)(2,1)}, bf16[2,72,1440]{2,1,0:T(8,128)(2,1)S(1)}, u32[]{:S(2)}, u32[]{:S(2)}) collective-permute-start(bf16[2,72,1440]{2,1,0:T(8,128)(2,1)} %get-tuple-element.36), channel_id=1, source_target_pairs={{0,16},{16,32},{32,48},{48,0},{64,80},{80,96},{96,112},{112,64},{1... | collective-permute-start | bytes 1244168 | tf_op jit(solution)/shard_map/ppermute | solution.py:641
  28.2 17.4 %collective-permute-start.1 = (bf16[2,72,1440]{2,1,0:T(8,128)(2,1)}, bf16[2,72,1440]{2,1,0:T(8,128)(2,1)S(1)}, u32[]{:S(2)}, u32[]{:S(2)}) collective-permute-start(bf16[2,72,1440]{2,1,0:T(8,128)(2,1)} %get-tuple-element.37), channel_id=1, source_target_pairs={{0,48},{16,0},{32,16},{48,32},{64,112},{80,64},{96,80},{112,96},{1... | collective-permute-start | bytes 1244168 | tf_op jit(solution)/shard_map/ppermute | solution.py:641
  30.5 34.2 %collective-permute-start.2 = (bf16[2,72,1440]{2,1,0:T(8,128)(2,1)}, bf16[2,72,1440]{2,1,0:T(8,128)(2,1)S(1)}, u32[]{:S(2)}, u32[]{:S(2)}) collective-permute-start(bf16[2,72,1440]{2,1,0:T(8,128)(2,1)} %get-tuple-element.44), channel_id=1, source_target_pairs={{0,112},{16,64},{32,80},{48,96},{64,48},{80,0},{96,16},{112,32},{1... | collective-permute-start | bytes 1244168 | tf_op jit(solution)/shard_map/ppermute | solution.py:641
  34.3 30.4 %collective-permute-start.3 = (bf16[2,72,1440]{2,1,0:T(8,128)(2,1)}, bf16[2,72,1440]{2,1,0:T(8,128)(2,1)}, u32[]{:S(2)}, u32[]{:S(2)}) collective-permute-start(bf16[2,72,1440]{2,1,0:T(8,128)(2,1)} %get-tuple-element.45), channel_id=1, source_target_pairs={{0,80},{16,96},{32,112},{48,64},{64,16},{80,32},{96,48},{112,0},{1... | collective-permute-start | bytes 1244168 | tf_op jit(solution)/shard_map/ppermute | solution.py:641
  35.0 38.7 %collective-permute-start.4 = (bf16[2,72,1440]{2,1,0:T(8,128)(2,1)}, bf16[2,72,1440]{2,1,0:T(8,128)(2,1)}, u32[]{:S(2)}, u32[]{:S(2)}) collective-permute-start(bf16[2,72,1440]{2,1,0:T(8,128)(2,1)} %get-tuple-element.46), channel_id=1, source_target_pairs={{0,96},{16,112},{32,64},{48,80},{64,32},{80,48},{96,0},{112,16},{1... | collective-permute-start | bytes 1244168 | tf_op jit(solution)/shard_map/ppermute | solution.py:641
  42.2 31.4 %copy-start.3 = (bf16[2,72,1440]{2,1,0:T(8,128)(2,1)}, bf16[2,72,1440]{2,1,0:T(8,128)(2,1)S(1)}, u32[]{:S(2)}) copy-start(bf16[2,72,1440]{2,1,0:T(8,128)(2,1)S(1)} %collective-permute-done.refs_1_.rest_1_) | copy-start | bytes 1244164
  42.3 39.2 %collective-permute-start.5 = (bf16[2,72,1440]{2,1,0:T(8,128)(2,1)}, bf16[2,72,1440]{2,1,0:T(8,128)(2,1)S(1)}, u32[]{:S(2)}, u32[]{:S(2)}) collective-permute-start(bf16[2,72,1440]{2,1,0:T(8,128)(2,1)} %get-tuple-element.47), channel_id=1, source_target_pairs={{0,64},{16,80},{32,96},{48,112},{64,0},{80,16},{96,32},{112,48},{1... | collective-permute-start | bytes 1244168 | tf_op jit(solution)/shard_map/ppermute | solution.py:641
  45.7 28.0 %copy-start.4 = (bf16[2,72,1440]{2,1,0:T(8,128)(2,1)}, bf16[2,72,1440]{2,1,0:T(8,128)(2,1)S(1)}, u32[]{:S(2)}) copy-start(bf16[2,72,1440]{2,1,0:T(8,128)(2,1)S(1)} %collective-permute-done.1.refs_2_.rest_2_) | copy-start | bytes 1244164
  45.7 35.8 %collective-permute-start.6 = (bf16[2,72,1440]{2,1,0:T(8,128)(2,1)}, bf16[2,72,1440]{2,1,0:T(8,128)(2,1)S(1)}, u32[]{:S(2)}, u32[]{:S(2)}) collective-permute-start(bf16[2,72,1440]{2,1,0:T(8,128)(2,1)} %get-tuple-element.48), channel_id=1, source_target_pairs={{0,32},{16,48},{32,0},{48,16},{64,96},{80,112},{96,64},{112,80},{1... | collective-permute-start | bytes 1244168 | tf_op jit(solution)/shard_map/ppermute | solution.py:641
  60.6 27.1 %all-to-all-start.1 = ((bf16[8,36,721]{2,1,0:T(8,128)(2,1)}), bf16[8,36,721]{2,1,0:T(8,128)(2,1)S(1)}, u32[]{:S(2)}, u32[]{:S(2)}) async-start(bf16[8,36,721]{2,1,0:T(8,128)(2,1)} %get-tuple-element.40), calls=%async_computation.1 | async-start | bytes 983040 | tf_op jit(solution)/shard_map/all_to_all | solution.py:646
  64.7 8.9 %copy-start.5 = (bf16[2,72,1440]{2,1,0:T(8,128)(2,1)}, bf16[2,72,1440]{2,1,0:T(8,128)(2,1)S(1)}, u32[]{:S(2)}) copy-start(bf16[2,72,1440]{2,1,0:T(8,128)(2,1)S(1)} %collective-permute-done.2.refs_3_.rest_3_) | copy-start | bytes 1244164
  81.4 12.2 %copy-start.6 = (bf16[2,72,1440]{2,1,0:T(8,128)(2,1)}, bf16[2,72,1440]{2,1,0:T(8,128)(2,1)S(1)}, u32[]{:S(2)}) copy-start(bf16[2,72,1440]{2,1,0:T(8,128)(2,1)S(1)} %collective-permute-done.5.rest_6_) | copy-start | bytes 1244164
  81.4 12.2 %copy-start.7 = (bf16[2,72,1440]{2,1,0:T(8,128)(2,1)}, bf16[2,72,1440]{2,1,0:T(8,128)(2,1)S(1)}, u32[]{:S(2)}) copy-start(bf16[2,72,1440]{2,1,0:T(8,128)(2,1)S(1)} %collective-permute-done.6.rest_7_) | copy-start | bytes 1244164
  87.7 6.0 %copy-start.2 = (bf16[8,36,721]{2,1,0:T(8,128)(2,1)}, bf16[8,36,721]{2,1,0:T(8,128)(2,1)S(1)}, u32[]{:S(2)}) copy-start(bf16[8,36,721]{2,1,0:T(8,128)(2,1)S(1)} %all-to-all-done.1.spec_ref) | copy-start | bytes 1245892
  87.7 19.9 %all-to-all-start.2 = ((bf16[128,2,1152]{2,1,0:T(2,128)(2,1)}), bf16[128,2,1152]{2,1,0:T(2,128)(2,1)S(1)}, u32[]{:S(2)}, u32[]{:S(2)}) async-start(bf16[128,2,1152]{2,1,0:T(2,128)(2,1)} %bitcast.5), calls=%async_computation.2 | async-start | bytes 1179648 | tf_op jit(solution)/shard_map/all_to_all | solution.py:650
  93.6 14.0 %copy-start = (bf16[1440,256]{1,0:T(8,128)(2,1)S(1)}, bf16[1440,256]{1,0:T(8,128)(2,1)}, u32[]{:S(2)}) copy-start(bf16[1440,256]{1,0:T(8,128)(2,1)} %get-tuple-element.63.table_ref) | copy-start | bytes 2211844

commit v7 on v6

--- a/solution.py
+++ b/solution.py
@@ -408,7 +408,7 @@
 def regroup(ens, truth, member_count):
     own_count, var_count, band_rows, lon_count = ens.shape
     sub_rows = band_rows // member_count
-    width = 3 * LANES
+    width = 6 * LANES
     rows = var_count * sub_rows
     return pl.pallas_call(
         functools.partial(regroup_kernel, var_count, sub_rows),
@@ -640,7 +640,7 @@
         if place:
             parts[place] = lax.ppermute(parts[place], "member", hop_pairs(hop, member_count))
 
-    received, *parts[1:3] = lax.optimization_barrier((received, *parts[1:3]))
+    received, parts[1] = lax.optimization_barrier((received, parts[1]))
     grads, score = spectral(received, orders, fairness, member_count, var_count, deg_count)
     signs = count_signs(parts[:EARLY_PARTS])
     spec_score = lax.all_to_all(score, "member", split_axis=0, concat_axis=0, tiled=True)

time: 112 us -> 112 us (level)
  transfers between devices with their start and end apart: 10 -> 10, of which waited for: 3 -> 3; matrix products, arithmetic and copies ran while one was open for 0% -> 0% of each run, Pallas kernels for 40% -> 39%
where the time goes in v7:
time: 112 us; the launch traced here: 111 us
  Pallas kernels  53.7 us (48%)
  starting transfers between devices  37.3 us (33%)
  waiting for transfers between devices  19.4 us (17%)
    ppermute x7, starting transfers between devices, local(): lax.ppermute(parts[place], 'member', hop_pairs(hop, member_count))  15.9 us
    pallas_call x1, Pallas kernels, spectral(): pl.pallas_call(functools.partial(spectral_kernel, fairness, member_count,...  14.2 us
    pallas_call x1, Pallas kernels, grid_scores(): pl.pallas_call(functools.partial(grid_kernel, fairness, lon_count, signs....  13.9 us
    ppermute x7, waiting for transfers between devices, local(): lax.ppermute(parts[place], 'member', hop_pairs(hop, member_count))  13.1 us
    all_to_all x1, starting transfers between devices, local(): lax.all_to_all(sent, owners, split_axis=0, concat_axis=0, tiled=True)  11.1 us
    pallas_call x1, Pallas kernels, count_signs(): pl.pallas_call(count_kernel, grid=(-(-lon_count // width),), in_specs=[pl...  7.75 us
    pallas_call x1, Pallas kernels, regroup(): pl.pallas_call(functools.partial(regroup_kernel, var_count, sub_rows), gr...  7.65 us
    pallas_call x1, Pallas kernels, forward(): pl.pallas_call(functools.partial(forward_kernel, var_count, deg_count), i...  6.76 us
  transfers between devices with their start and end apart: 10, of which 3 were waited for; matrix products, arithmetic and copies ran while one was open for 0% of the time, Pallas kernels for 39%

profile of v7, /device:TPU:0, one launch (start us, length us, event | category | flops | bytes accessed | tf_op | source)
XLA Modules:
  0.0 111.1 jit_solution(15155992385583141143)
XLA Ops:
  0.6 6.8 %forward.1 = (bf16[128,16,256]{2,1,0:T(8,128)(2,1)}, bf16[1440,256]{1,0:T(8,128)(2,1)}) custom-call(s32[1,128]{1,0:T(1,128)} %bitcast.15, bf16[1152,1440]{1,0:T(8,128)(2,1)} %bitcast.16, bf16[36,16,1440]{2,1,0:T(8,128)(2,1)} %truth_ref.1, bf16[721,16,128]{2,1,0:T(8,128)(2,1)} %bitcast.20), custom_call_target="tpu_custom_call" | custom-call | flops 1024 | bytes 1024 | tf_op jit(solution)/shard_map/forward/pallas_call | solution.py:140
  7.4 0.0 copy-start.1
  7.4 11.1 %all-to-all-start = ((bf16[128,16,256]{2,1,0:T(8,128)(2,1)}), bf16[128,16,256]{2,1,0:T(8,128)(2,1)S(1)}, u32[]{:S(2)}, u32[]{:S(2)}) async-start(bf16[128,16,256]{2,1,0:T(8,128)(2,1)} %get-tuple-element.34), calls=%async_computation | async-start | bytes 2097152 | tf_op jit(solution)/shard_map/all_to_all | solution.py:636
  18.6 7.7 %regroup.1 = (bf16[2,72,1440]{2,1,0:T(8,128)(2,1)}, bf16[2,72,1440]{2,1,0:T(8,128)(2,1)}, bf16[2,72,1440]{2,1,0:T(8,128)(2,1)}, bf16[2,72,1440]{2,1,0:T(8,128)(2...) custom-call(bf16[1152,1440]{1,0:T(8,128)(2,1)} %bitcast.17, ...), custom_call_target="tpu_custom_call" | custom-call | flops 1024 | bytes 1024 | tf_op jit(solution)/shard_map/regroup/pallas_call | solution.py:413
  26.2 1.0 collective-permute-start
  27.3 2.3 %collective-permute-start.1 = (bf16[2,72,1440]{2,1,0:T(8,128)(2,1)}, bf16[2,72,1440]{2,1,0:T(8,128)(2,1)S(1)}, u32[]{:S(2)}, u32[]{:S(2)}) collective-permute-start(bf16[2,72,1440]{2,1,0:T(8,128)(2,1)} %get-tuple-element.41), channel_id=1, source_target_pairs={{0,48},{16,0},{32,16},{48,32},{64,112},{80,64},{96,80},{112,96},{1... | collective-permute-start | bytes 1244168 | tf_op jit(solution)/shard_map/ppermute | solution.py:641
  29.5 3.8 %collective-permute-start.2 = (bf16[2,72,1440]{2,1,0:T(8,128)(2,1)}, bf16[2,72,1440]{2,1,0:T(8,128)(2,1)S(1)}, u32[]{:S(2)}, u32[]{:S(2)}) collective-permute-start(bf16[2,72,1440]{2,1,0:T(8,128)(2,1)} %get-tuple-element.42), channel_id=1, source_target_pairs={{0,112},{16,64},{32,80},{48,96},{64,48},{80,0},{96,16},{112,32},{1... | collective-permute-start | bytes 1244168 | tf_op jit(solution)/shard_map/ppermute | solution.py:641
  33.3 0.6 collective-permute-start.3
  34.0 4.1 %collective-permute-start.4 = (bf16[2,72,1440]{2,1,0:T(8,128)(2,1)}, bf16[2,72,1440]{2,1,0:T(8,128)(2,1)}, u32[]{:S(2)}, u32[]{:S(2)}) collective-permute-start(bf16[2,72,1440]{2,1,0:T(8,128)(2,1)} %get-tuple-element.44), channel_id=1, source_target_pairs={{0,96},{16,112},{32,64},{48,80},{64,32},{80,48},{96,0},{112,16},{1... | collective-permute-start | bytes 1244168 | tf_op jit(solution)/shard_map/ppermute | solution.py:641
  38.0 4.2 %collective-permute-done.refs_1_.rest_1_ = bf16[2,72,1440]{2,1,0:T(8,128)(2,1)S(1)} collective-permute-done((bf16[2,72,1440]{2,1,0:T(8,128)(2,1)}, bf16[2,72,1440]{2,1,0:T(8,128)(2,1)S(1)}, u32[]{:S(2)}, u32[]{:S(2)}) %collective-permute-start) | collective-permute-done | bytes 414752 | tf_op jit(solution)/shard_map/ppermute | solution.py:641
  42.2 0.0 copy-start.3
  42.3 3.4 %collective-permute-start.5 = (bf16[2,72,1440]{2,1,0:T(8,128)(2,1)}, bf16[2,72,1440]{2,1,0:T(8,128)(2,1)S(1)}, u32[]{:S(2)}, u32[]{:S(2)}) collective-permute-start(bf16[2,72,1440]{2,1,0:T(8,128)(2,1)} %get-tuple-element.45), channel_id=1, source_target_pairs={{0,64},{16,80},{32,96},{48,112},{64,0},{80,16},{96,32},{112,48},{1... | collective-permute-start | bytes 1244168 | tf_op jit(solution)/shard_map/ppermute | solution.py:641
  45.7 0.0 collective-permute-done.1.refs_2_.rest_2_
  45.7 0.0 copy-start.4
  45.7 0.6 collective-permute-start.6
  46.3 0.0 all-to-all-done
  46.3 0.0 copy-done.1
  46.3 14.2 %spectral.1 = (bf16[16,8,2,1152]{3,2,1,0:T(2,128)(2,1)}, bf16[8,36,721]{2,1,0:T(8,128)(2,1)}) custom-call(s32[128]{0:T(128)S(1)} %copy-done.1, bf16[16,8,16,256]{3,2,1,0:T(8,128)(2,1)S(1)} %bitcast.14), custom_call_target="tpu_custom_call" | custom-call | flops 1024 | bytes 1024 | tf_op jit(solution)/shard_map/spectral/pallas_call | solution.py:279
  60.5 4.2 %all-to-all-start.1 = ((bf16[8,36,721]{2,1,0:T(8,128)(2,1)}), bf16[8,36,721]{2,1,0:T(8,128)(2,1)S(1)}, u32[]{:S(2)}, u32[]{:S(2)}) async-start(bf16[8,36,721]{2,1,0:T(8,128)(2,1)} %get-tuple-element.38), calls=%async_computation.1 | async-start | bytes 983040 | tf_op jit(solution)/shard_map/all_to_all | solution.py:646
  64.7 0.0 collective-permute-done.2.refs_3_.rest_3_
  64.7 0.0 copy-start.5
  64.7 0.0 collective-permute-done.3.refs_4_.rest_4_
  64.7 8.9 %collective-permute-done.4.refs_5_.rest_5_ = bf16[2,72,1440]{2,1,0:T(8,128)(2,1)} collective-permute-done((bf16[2,72,1440]{2,1,0:T(8,128)(2,1)}, bf16[2,72,1440]{2,1,0:T(8,128)(2,1)}, u32[]{:S(2)}, u32[]{:S(2)}) %collective-permute-start.4) | collective-permute-done | bytes 414752 | tf_op jit(solution)/shard_map/ppermute | solution.py:641
  73.6 0.0 copy-done.3
  73.6 0.0 copy-done.4
  73.6 0.0 copy-done.5
  73.6 7.8 %count.1.rest_8_ = bf16[12,72,1440]{2,1,0:T(8,128)(2,1)} custom-call(bf16[2,72,1440]{2,1,0:T(8,128)(2,1)} %get-tuple-element.48.refs_0_.rest_0_, bf16[2,72,1440]{2,1,0:T(8,128)(2,1)} %copy-done.3, bf16[2,72,1440]{2,1,0:T(8,128)(2,1)} %copy-done.4, bf16[2,72,1440]{2,1,0:T(8,128)(2,1)} %copy-done.5, ...), custom_call_target="tpu_custom_call" | custom-call | flops 1024 | bytes 1024 | tf_op jit(solution)/shard_map/count/pallas_call | solution.py:491
  81.4 0.0 collective-permute-done.5.rest_6_
  81.4 0.0 copy-start.6
  81.4 0.0 collective-permute-done.6.rest_7_
  81.4 0.0 copy-start.7
  81.4 6.3 %all-to-all-done.1.spec_ref = bf16[8,36,721]{2,1,0:T(8,128)(2,1)S(1)} async-done(((bf16[8,36,721]{2,1,0:T(8,128)(2,1)}), bf16[8,36,721]{2,1,0:T(8,128)(2,1)S(1)}, u32[]{:S(2)}, u32[]{:S(2)}) %all-to-all-start.1) | async-done | bytes 415328 | tf_op jit(solution)/shard_map/all_to_all | solution.py:646
  87.7 0.0 copy-start.2
  87.7 6.1 %all-to-all-start.2 = ((bf16[128,2,1152]{2,1,0:T(2,128)(2,1)}), bf16[128,2,1152]{2,1,0:T(2,128)(2,1)S(1)}, u32[]{:S(2)}, u32[]{:S(2)}) async-start(bf16[128,2,1152]{2,1,0:T(2,128)(2,1)} %bitcast.5), calls=%async_computation.2 | async-start | bytes 1179648 | tf_op jit(solution)/shard_map/all_to_all | solution.py:650
  93.8 0.0 copy-start
  93.8 0.0 copy-done.6
  93.8 0.0 copy-done.7
  93.8 0.0 copy-done.2
  93.9 13.9 %grid.1 = (bf16[16,36,2,1440]{3,2,1,0:T(2,128)(2,1)}, f32[2,36]{1,0:T(2,128)}, f32[36,8,721]{2,1,0:T(8,128)}) custom-call(f32[256]{0:T(256)} %constant.2.clone.weight_ref, bf16[72,1440]{1,0:T(8,128)(2,1)} %get-tuple-element.33.truth_ref, bf16[8,36,721]{2,1,0:T(8,128)(2,1)} %copy-done.2, bf16[2,72,1440]{2,1,0:T(8,128)(2,1)} %get-tuple-element.48.refs_0_.rest_0_, ...), custom_call_target="tpu_custom_call" | custom-call | flops 1024 | bytes 1024 | tf_op jit(solution)/shard_map/grid/pallas_call | solution.py:593
  107.8 0.0 all-to-all-done.2.in_ref
  107.8 0.0 copy-done
  107.8 3.3 %backward.1 = bf16[1152,1440]{1,0:T(8,128)(2,1)} custom-call(bf16[128,2,1152]{2,1,0:T(2,128)(2,1)S(1)} %all-to-all-done.2.in_ref, bf16[1440,256]{1,0:T(8,128)(2,1)S(1)} %copy-done), custom_call_target="tpu_custom_call" | custom-call | flops 1024 | bytes 1024 | tf_op jit(solution)/shard_map/backward/pallas_call | solution.py:352
Async XLA Ops:
  7.4 38.9 %copy-start.1 = (s32[128]{0:T(128)S(1)}, s32[128]{0:T(128)}, u32[]{:S(2)}) copy-start(s32[128]{0:T(128)} %orders_ref.1) | copy-start | bytes 1540
  7.4 38.9 %all-to-all-start = ((bf16[128,16,256]{2,1,0:T(8,128)(2,1)}), bf16[128,16,256]{2,1,0:T(8,128)(2,1)S(1)}, u32[]{:S(2)}, u32[]{:S(2)}) async-start(bf16[128,16,256]{2,1,0:T(8,128)(2,1)} %get-tuple-element.34), calls=%async_computation | async-start | bytes 2097152 | tf_op jit(solution)/shard_map/all_to_all | solution.py:636
  26.2 16.0 %collective-permute-start = (bf16[2,72,1440]{2,1,0:T(8,128)(2,1)}, bf16[2,72,1440]{2,1,0:T(8,128)(2,1)S(1)}, u32[]{:S(2)}, u32[]{:S(2)}) collective-permute-start(bf16[2,72,1440]{2,1,0:T(8,128)(2,1)} %get-tuple-element.35), channel_id=1, source_target_pairs={{0,16},{16,32},{32,48},{48,0},{64,80},{80,96},{96,112},{112,64},{1... | collective-permute-start | bytes 1244168 | tf_op jit(solution)/shard_map/ppermute | solution.py:641
  27.3 18.4 %collective-permute-start.1 = (bf16[2,72,1440]{2,1,0:T(8,128)(2,1)}, bf16[2,72,1440]{2,1,0:T(8,128)(2,1)S(1)}, u32[]{:S(2)}, u32[]{:S(2)}) collective-permute-start(bf16[2,72,1440]{2,1,0:T(8,128)(2,1)} %get-tuple-element.41), channel_id=1, source_target_pairs={{0,48},{16,0},{32,16},{48,32},{64,112},{80,64},{96,80},{112,96},{1... | collective-permute-start | bytes 1244168 | tf_op jit(solution)/shard_map/ppermute | solution.py:641
  29.5 35.2 %collective-permute-start.2 = (bf16[2,72,1440]{2,1,0:T(8,128)(2,1)}, bf16[2,72,1440]{2,1,0:T(8,128)(2,1)S(1)}, u32[]{:S(2)}, u32[]{:S(2)}) collective-permute-start(bf16[2,72,1440]{2,1,0:T(8,128)(2,1)} %get-tuple-element.42), channel_id=1, source_target_pairs={{0,112},{16,64},{32,80},{48,96},{64,48},{80,0},{96,16},{112,32},{1... | collective-permute-start | bytes 1244168 | tf_op jit(solution)/shard_map/ppermute | solution.py:641
  33.3 31.4 %collective-permute-start.3 = (bf16[2,72,1440]{2,1,0:T(8,128)(2,1)}, bf16[2,72,1440]{2,1,0:T(8,128)(2,1)}, u32[]{:S(2)}, u32[]{:S(2)}) collective-permute-start(bf16[2,72,1440]{2,1,0:T(8,128)(2,1)} %get-tuple-element.43), channel_id=1, source_target_pairs={{0,80},{16,96},{32,112},{48,64},{64,16},{80,32},{96,48},{112,0},{1... | collective-permute-start | bytes 1244168 | tf_op jit(solution)/shard_map/ppermute | solution.py:641
  34.0 39.6 %collective-permute-start.4 = (bf16[2,72,1440]{2,1,0:T(8,128)(2,1)}, bf16[2,72,1440]{2,1,0:T(8,128)(2,1)}, u32[]{:S(2)}, u32[]{:S(2)}) collective-permute-start(bf16[2,72,1440]{2,1,0:T(8,128)(2,1)} %get-tuple-element.44), channel_id=1, source_target_pairs={{0,96},{16,112},{32,64},{48,80},{64,32},{80,48},{96,0},{112,16},{1... | collective-permute-start | bytes 1244168 | tf_op jit(solution)/shard_map/ppermute | solution.py:641
  42.2 31.4 %copy-start.3 = (bf16[2,72,1440]{2,1,0:T(8,128)(2,1)}, bf16[2,72,1440]{2,1,0:T(8,128)(2,1)S(1)}, u32[]{:S(2)}) copy-start(bf16[2,72,1440]{2,1,0:T(8,128)(2,1)S(1)} %collective-permute-done.refs_1_.rest_1_) | copy-start | bytes 1244164
  42.3 39.1 %collective-permute-start.5 = (bf16[2,72,1440]{2,1,0:T(8,128)(2,1)}, bf16[2,72,1440]{2,1,0:T(8,128)(2,1)S(1)}, u32[]{:S(2)}, u32[]{:S(2)}) collective-permute-start(bf16[2,72,1440]{2,1,0:T(8,128)(2,1)} %get-tuple-element.45), channel_id=1, source_target_pairs={{0,64},{16,80},{32,96},{48,112},{64,0},{80,16},{96,32},{112,48},{1... | collective-permute-start | bytes 1244168 | tf_op jit(solution)/shard_map/ppermute | solution.py:641
  45.7 27.9 %copy-start.4 = (bf16[2,72,1440]{2,1,0:T(8,128)(2,1)}, bf16[2,72,1440]{2,1,0:T(8,128)(2,1)S(1)}, u32[]{:S(2)}) copy-start(bf16[2,72,1440]{2,1,0:T(8,128)(2,1)S(1)} %collective-permute-done.1.refs_2_.rest_2_) | copy-start | bytes 1244164
  45.7 35.7 %collective-permute-start.6 = (bf16[2,72,1440]{2,1,0:T(8,128)(2,1)}, bf16[2,72,1440]{2,1,0:T(8,128)(2,1)S(1)}, u32[]{:S(2)}, u32[]{:S(2)}) collective-permute-start(bf16[2,72,1440]{2,1,0:T(8,128)(2,1)} %get-tuple-element.46), channel_id=1, source_target_pairs={{0,32},{16,48},{32,0},{48,16},{64,96},{80,112},{96,64},{112,80},{1... | collective-permute-start | bytes 1244168 | tf_op jit(solution)/shard_map/ppermute | solution.py:641
  60.5 27.1 %all-to-all-start.1 = ((bf16[8,36,721]{2,1,0:T(8,128)(2,1)}), bf16[8,36,721]{2,1,0:T(8,128)(2,1)S(1)}, u32[]{:S(2)}, u32[]{:S(2)}) async-start(bf16[8,36,721]{2,1,0:T(8,128)(2,1)} %get-tuple-element.38), calls=%async_computation.1 | async-start | bytes 983040 | tf_op jit(solution)/shard_map/all_to_all | solution.py:646
  64.7 8.9 %copy-start.5 = (bf16[2,72,1440]{2,1,0:T(8,128)(2,1)}, bf16[2,72,1440]{2,1,0:T(8,128)(2,1)S(1)}, u32[]{:S(2)}) copy-start(bf16[2,72,1440]{2,1,0:T(8,128)(2,1)S(1)} %collective-permute-done.2.refs_3_.rest_3_) | copy-start | bytes 1244164
  81.4 12.4 %copy-start.6 = (bf16[2,72,1440]{2,1,0:T(8,128)(2,1)}, bf16[2,72,1440]{2,1,0:T(8,128)(2,1)S(1)}, u32[]{:S(2)}) copy-start(bf16[2,72,1440]{2,1,0:T(8,128)(2,1)S(1)} %collective-permute-done.5.rest_6_) | copy-start | bytes 1244164
  81.4 12.4 %copy-start.7 = (bf16[2,72,1440]{2,1,0:T(8,128)(2,1)}, bf16[2,72,1440]{2,1,0:T(8,128)(2,1)S(1)}, u32[]{:S(2)}) copy-start(bf16[2,72,1440]{2,1,0:T(8,128)(2,1)S(1)} %collective-permute-done.6.rest_7_) | copy-start | bytes 1244164
  87.7 6.2 %copy-start.2 = (bf16[8,36,721]{2,1,0:T(8,128)(2,1)}, bf16[8,36,721]{2,1,0:T(8,128)(2,1)S(1)}, u32[]{:S(2)}) copy-start(bf16[8,36,721]{2,1,0:T(8,128)(2,1)S(1)} %all-to-all-done.1.spec_ref) | copy-start | bytes 1245892
  87.7 20.1 %all-to-all-start.2 = ((bf16[128,2,1152]{2,1,0:T(2,128)(2,1)}), bf16[128,2,1152]{2,1,0:T(2,128)(2,1)S(1)}, u32[]{:S(2)}, u32[]{:S(2)}) async-start(bf16[128,2,1152]{2,1,0:T(2,128)(2,1)} %bitcast.5), calls=%async_computation.2 | async-start | bytes 1179648 | tf_op jit(solution)/shard_map/all_to_all | solution.py:650
  93.8 14.0 %copy-start = (bf16[1440,256]{1,0:T(8,128)(2,1)S(1)}, bf16[1440,256]{1,0:T(8,128)(2,1)}, u32[]{:S(2)}) copy-start(bf16[1440,256]{1,0:T(8,128)(2,1)} %get-tuple-element.61.table_ref) | copy-start | bytes 2211844
